TPU v7x, 512 devices: a whole 4x4x16 slice. The times are simulated.
512 devices in a mesh: dp: 32 (over x, y, core), tensor: 16 (over z).
Axes of the slice: x: 4, y: 4, z: 16, core: 2. Of those that a mesh axis runs over, the one named last changes fastest.
Arguments:
- queries: bfloat16 [1024, 64, 128], P('dp', 'tensor'), parts along dimension 0, may hold values from -80 to 80
- new_key: bfloat16 [1024, 8, 128], P('dp'), parts along dimension 0, may hold values from -4 to 4
- new_value: bfloat16 [1024, 8, 128], P('dp'), parts along dimension 0, may hold values from -6 to 6
- key_codes: int32 [1024, 16, 2048], P('dp', 'tensor'), parts along dimension 0, may hold values from 0 to 65280
- key_scales: int32 [1024, 16, 64], P('dp', 'tensor'), parts along dimension 0, may hold values from 16 to 127
- value_codes: int32 [1024, 16, 2048], P('dp', 'tensor'), parts along dimension 0, may hold values from 0 to 65280
- value_scales: int32 [1024, 16, 64], P('dp', 'tensor'), parts along dimension 0, may hold values from 16 to 127
- lengths: int32 [1024], P('dp'), parts along dimension 0, may hold values from 1 to 128, 2048 in all
- out_codes: int32 [2048, 8192], P(None, 'tensor'), may hold values from 0 to 65280
- out_scales: int32 [64, 8192], P(None, 'tensor'), may hold values from 16 to 127
Outputs:
- projected: bfloat16 [1024, 8192], P('dp', 'tensor'), parts along dimension 0
There are 32 independent parts, one for each index of `dp`. A program takes and returns all parts, laid end to end along the dimension named above; an argument that names none is the same for every part. Nothing has to cross between parts.
Inputs may be any that keep to these rules, and one draw needn't show every extreme that they name: Each row attends to its cached tokens 0 to lengths - 1 and to its new token, which stands at position lengths; the largest length is 128 in every draw. The sum of the lengths is 2048 within each decode group's 32 rows, not over the whole array of all groups.
All inputs are finite; a program needn't handle non-finite values.
Results may differ from a plain program's by a relative error of at most 0.012.
Values may be sent and summed in bfloat16 or wider, within the bound.
No kernel may reach another device: no remote copies, remote signals or barrier semaphores. Data moves between devices by JAX's collectives and lax.ppermute only.
A program may use at most 128 MiB of HBM per device.

v0:
```python
import jax
import jax.numpy as jnp
from jax import lax
from jax.sharding import PartitionSpec as P

rope_base = 10000.0
neg_floor = -1e30
code_offset = 7.5
cache_step = 256.0
weight_step = 8192.0


def swapped(array, axis, stride):
    return lax.ppermute(array, axis, [(i, i ^ 1 << stride) for i in range(lax.axis_size(axis))])


def unpack_codes(code_words):
    shifts = 4 * jnp.arange(4, dtype=jnp.int32)
    nibbles = jnp.bitwise_and(jnp.right_shift(code_words[..., None], shifts), 15)
    return (
        nibbles.reshape(code_words.shape[:-1] + (code_words.shape[-1] * 4,)).astype(jnp.float32)
        - code_offset
    )


def unpack_rows(code_words, scale_rows):
    shifts = 4 * jnp.arange(4, dtype=jnp.int32)
    nibbles = jnp.bitwise_and(jnp.right_shift(code_words[:, None, :], shifts[None, :, None]), 15)
    row_total = code_words.shape[0] * 4
    columns = code_words.shape[1]
    levels = nibbles.reshape(row_total, columns).astype(jnp.float32) - code_offset
    group_rows = row_total // scale_rows.shape[0]
    spread = jnp.broadcast_to(
        scale_rows.astype(jnp.float32)[:, None, :], (scale_rows.shape[0], group_rows, columns)
    ).reshape(row_total, columns)
    return (levels * spread / weight_step).astype(jnp.bfloat16)


def rope_tables(positions, head_width):
    half_width = head_width // 2
    frequency = rope_base ** (-(jnp.arange(half_width, dtype=jnp.float32) * 2.0 / head_width))
    angles = positions.astype(jnp.float32)[..., None] * frequency
    return (jnp.cos(angles), jnp.sin(angles))


def rotate(vectors, cosine_table, sine_table):
    half_width = vectors.shape[-1] // 2
    first_half = vectors[..., :half_width]
    second_half = vectors[..., half_width:]
    return jnp.concatenate(
        [
            first_half * cosine_table - second_half * sine_table,
            second_half * cosine_table + first_half * sine_table,
        ],
        axis=-1,
    )


def sylvester(table_order):
    entries = jnp.arange(table_order, dtype=jnp.int32)
    intersection = jnp.bitwise_and(entries[:, None], entries[None, :])
    parity = jnp.zeros((table_order, table_order), jnp.int32)
    for bit_index in range(max(table_order.bit_length() - 1, 0)):
        parity = parity + jnp.bitwise_and(jnp.right_shift(intersection, bit_index), 1)
    return 1.0 - 2.0 * jnp.bitwise_and(parity, 1).astype(jnp.float32)


def half_partial(
    query_block,
    code_words,
    scale_block,
    value_words,
    value_scale,
    lengths,
    half_index,
    key_new,
    value_new,
    include,
):
    row_count, token_count = scale_block.shape
    head_width = query_block.shape[-1]
    key_levels = unpack_codes(code_words.reshape(row_count, token_count, head_width // 4))
    positions = half_index * token_count + jnp.arange(token_count, dtype=jnp.int32)
    cosine_table, sine_table = rope_tables(positions, head_width)
    key_block = rotate(
        key_levels * scale_block.astype(jnp.float32)[..., None] / cache_step,
        cosine_table[None],
        sine_table[None],
    ).astype(jnp.bfloat16)
    value_levels = unpack_codes(value_words.reshape(row_count, token_count, head_width // 4))
    value_block = (value_levels * value_scale.astype(jnp.float32)[..., None] / cache_step).astype(
        jnp.bfloat16
    )
    factor = head_width ** (-0.5)
    scores = (
        jnp.einsum("rqd,rkd->rqk", query_block, key_block, preferred_element_type=jnp.float32)
        * factor
    )
    new_score = (
        jnp.einsum("rqd,rd->rq", query_block, key_new, preferred_element_type=jnp.float32) * factor
    )
    live_mask = (positions[None, :] < lengths[:, None])[:, None, :]
    scores = jnp.where(live_mask, scores, neg_floor)
    row_top = jnp.maximum(jnp.max(scores, axis=-1), jnp.where(include, new_score, neg_floor))
    weights = jnp.where(live_mask, jnp.exp(scores - row_top[..., None]), 0.0).astype(jnp.bfloat16)
    new_weight = jnp.where(include, jnp.exp(new_score - row_top), 0.0).astype(jnp.bfloat16)
    weight_sum = jnp.sum(weights.astype(jnp.float32), axis=-1) + new_weight.astype(jnp.float32)
    weighted = jnp.einsum("rqk,rkd->rqd", weights, value_block, preferred_element_type=jnp.float32)
    weighted = (
        weighted
        + new_weight.astype(jnp.float32)[..., None] * value_new.astype(jnp.float32)[:, None, :]
    )
    return (row_top, weight_sum, weighted)


def combine(first, second):
    joint_top = jnp.maximum(first[0], second[0])
    first_factor = jnp.exp(first[0] - joint_top)
    second_factor = jnp.exp(second[0] - joint_top)
    numerator = first[2] * first_factor[..., None] + second[2] * second_factor[..., None]
    denominator = first[1] * first_factor + second[1] * second_factor
    return (numerator / denominator[..., None]).astype(jnp.bfloat16)


def per_device(
    queries,
    new_key,
    new_value,
    key_codes,
    key_scales,
    value_codes,
    value_scales,
    lengths,
    out_codes,
    out_scales,
):
    row_count, local_heads, head_width = queries.shape
    devices = lax.axis_size("tensor")
    tensor_rank = lax.axis_index("tensor")
    head_count = local_heads * devices
    query_cos, query_sin = rope_tables(lengths, head_width)
    query_rot = rotate(
        queries.astype(jnp.float32), query_cos[:, None, :], query_sin[:, None, :]
    ).astype(jnp.bfloat16)
    key_now = rotate(
        new_key.astype(jnp.float32), query_cos[:, None, :], query_sin[:, None, :]
    ).astype(jnp.bfloat16)
    upper_half = tensor_rank % 2
    kv_global = tensor_rank // 2
    key_new = lax.dynamic_index_in_dim(key_now, kv_global, axis=1, keepdims=False)
    value_new = lax.dynamic_index_in_dim(new_value, kv_global, axis=1, keepdims=False)
    partner = swapped(query_rot, "tensor", 0)
    is_lower = upper_half == 0
    paired = jnp.where(
        is_lower,
        jnp.concatenate([query_rot, partner], axis=1),
        jnp.concatenate([partner, query_rot], axis=1),
    )
    partial_value = half_partial(
        paired,
        key_codes[:, 0],
        key_scales[:, 0],
        value_codes[:, 0],
        value_scales[:, 0],
        lengths,
        upper_half,
        key_new,
        value_new,
        is_lower,
    )
    lower_part = (
        partial_value[0][:, :local_heads],
        partial_value[1][:, :local_heads],
        partial_value[2][:, :local_heads],
    )
    upper_part = (
        partial_value[0][:, local_heads:],
        partial_value[1][:, local_heads:],
        partial_value[2][:, local_heads:],
    )
    kept = jax.tree.map(lambda low, high: jnp.where(is_lower, low, high), lower_part, upper_part)
    sending = jax.tree.map(lambda low, high: jnp.where(is_lower, high, low), lower_part, upper_part)
    received = swapped((sending[0], sending[1], sending[2]), "tensor", 0)
    attended = combine(kept, received)
    weight = unpack_rows(out_codes, out_scales)
    norm_factor = (head_count * head_width) ** (-0.5)
    width_table = sylvester(head_width).astype(jnp.bfloat16)
    within_head = jnp.einsum(
        "rhe,de->rhd", attended, width_table, preferred_element_type=jnp.float32
    )
    own_block = jnp.einsum(
        "gh,rhd->rgd", sylvester(local_heads), within_head, precision=lax.Precision.HIGHEST
    )
    for bit_index in range(devices.bit_length() - 1):
        partner_block = swapped(own_block, "tensor", bit_index)
        high_side = jnp.bitwise_and(jnp.right_shift(tensor_rank, bit_index), 1) == 1
        own_block = jnp.where(high_side, partner_block - own_block, own_block + partner_block)
    rotated = (own_block * norm_factor).astype(jnp.bfloat16)
    piece = lax.all_gather(rotated, "tensor", axis=1, tiled=True)
    flat_piece = piece.reshape(piece.shape[0], piece.shape[1] * piece.shape[2])
    projected = jnp.dot(flat_piece, weight, preferred_element_type=jnp.float32)
    return projected.astype(jnp.bfloat16)


def solution(mesh):
    return jax.shard_map(
        per_device,
        mesh=mesh,
        in_specs=(
            P("dp", "tensor", None),
            P("dp", None, None),
            P("dp", None, None),
            P("dp", "tensor", None),
            P("dp", "tensor", None),
            P("dp", "tensor", None),
            P("dp", "tensor", None),
            P("dp"),
            P(None, "tensor"),
            P(None, "tensor"),
        ),
        out_specs=P("dp", "tensor"),
        check_vma=False,
    )
```

profile of v0, /device:TPU:24, one launch (start us, length us, event | category | flops | bytes accessed | tf_op | source)
XLA Modules:
  0.0 143.9 jit_solution(13579611109690812463)
XLA Ops:
  0.0 0.7 convert_element_type.93
  0.7 0.8 convert_element_type.92
  1.8 3.8 %collective-permute-start = (bf16[32,4,128]{2,1,0:T(4,128)(2,1)S(1)}, bf16[32,4,128]{2,1,0:T(4,128)(2,1)S(1)}, u32[]{:S(2)}, u32[]{:S(2)}) collective-permute-start(bf16[32,4,128]{2,1,0:T(4,128)(2,1)S(1)} %pad_maximum_fusion), channel_id=1, source_target_pairs={{0,1},{1,0},{2,3},{3,2},{4,5},{5,4},{6,7},{7,6},{8,9},{9,8},{10,11... | collective-permute-start | bytes 98312 | tf_op jit(solution)/shard_map/ppermute | solution.py:14
  6.0 1.6 %reduce = s32[32,2048]{1,0:T(8,128)S(1)} reduce(s32[32,1,2048]{2,1,0:T(1,128)} %param.13, s32[]{:T(128)} %constant.32.clone.1), dimensions={1}, to_apply=%param.13.reduce_sub_computation | reduce | bytes 524292 | tf_op args[3]
  7.9 0.5 copy.26
  8.7 1.3 copy.27
  10.0 0.7 convert_element_type.95
  10.7 0.7 broadcast_compare_fusion
  11.5 0.9 copy_convert_fusion
  12.4 0.9 dynamic-slice_convert_fusion
  13.6 0.5 subtract_convert_fusion
  14.2 1.6 %reduce.1 = s32[32,2048]{1,0:T(8,128)S(1)} reduce(s32[32,1,2048]{2,1,0:T(1,128)} %param.15, s32[]{:T(128)} %constant.32.clone.1), dimensions={1}, to_apply=%param.15.reduce_sub_computation | reduce | bytes 524292 | tf_op args[5]
  16.1 1.2 copy.29
  17.3 1.3 shift_right_arithmetic.134
  18.6 2.3 %copy.30 = s32[32,64,128]{2,1,0:T(8,128)} copy(s32[32,64,128]{1,0,2:T(8,128)S(1)} %bitcast.27) | data formatting | bytes 2097152 | tf_op jit(solution)/shard_map/shift_right_arithmetic | solution.py:19
  21.2 0.7 fusion.77
  22.2 2.0 %collective-permute-start.3 = (f32[32,4]{1,0:T(8,128)S(1)}, f32[32,4]{1,0:T(8,128)S(1)}, u32[]{:S(2)}, u32[]{:S(2)}) collective-permute-start(f32[32,4]{1,0:T(8,128)S(1)} %slice_select_fusion.1), channel_id=1, source_target_pairs={{0,1},{1,0},{2,3},{3,2},{4,5},{5,4},{6,7},{7,6},{8,9},{9,8},{10,11... | collective-permute-start | bytes 1544 | tf_op jit(solution)/shard_map/ppermute | solution.py:14
  24.2 3.8 %collective-permute-start.1 = (f32[32,4]{1,0:T(8,128)S(1)}, f32[32,4]{1,0:T(8,128)S(1)}, u32[]{:S(2)}, u32[]{:S(2)}) collective-permute-start(f32[32,4]{1,0:T(8,128)S(1)} %slice_select_fusion.2), channel_id=1, source_target_pairs={{0,1},{1,0},{2,3},{3,2},{4,5},{5,4},{6,7},{7,6},{8,9},{9,8},{10,11... | collective-permute-start | bytes 1544 | tf_op jit(solution)/shard_map/ppermute | solution.py:14
  28.0 1.7 %convolution_add_fusion = f32[32,8,128]{2,1,0:T(8,128)S(1)} fusion(s32[32,64,128]{2,1,0:T(8,128)} %copy.30, f32[32,64]{1,0:T(8,128)S(1)} %bitcast.33, s32[128]{0:T(128)S(1)} %shift_right_arithmetic.130, f32[32,128]{1,0:T(8,128)S(1)} %bitcast.32, f32[32,8]{1,0:T(8,128)S(1)} %get-tuple-element.9, f32[32,8,64]{2,1,0:T(8,128)S(1)} %get-tuple-element.21, ...), kind=kOutput, calls=%fused_computation.2 | convolution fusion | flops 6144000 | bytes 1274368 | tf_op jit(solution)/shard_map/rqk,rkd->rqd/dot_general | solution.py:108
  29.8 2.0 %collective-permute-start.2 = (f32[32,4,128]{2,1,0:T(4,128)S(1)}, f32[32,4,128]{2,1,0:T(4,128)S(1)}, u32[]{:S(2)}, u32[]{:S(2)}) collective-permute-start(f32[32,4,128]{2,1,0:T(4,128)S(1)} %slice_select_fusion), channel_id=1, source_target_pairs={{0,1},{1,0},{2,3},{3,2},{4,5},{5,4},{6,7},{7,6},{8,9},{9,8},{10,11... | collective-permute-start | bytes 196616 | tf_op jit(solution)/shard_map/ppermute | solution.py:14
  31.9 4.0 %collective-permute-done.2 = f32[32,4,128]{2,1,0:T(4,128)S(1)} collective-permute-done((f32[32,4,128]{2,1,0:T(4,128)S(1)}, f32[32,4,128]{2,1,0:T(4,128)S(1)}, u32[]{:S(2)}, u32[]{:S(2)}) %collective-permute-start.2) | collective-permute-done | bytes 65568 | tf_op jit(solution)/shard_map/ppermute | solution.py:14
  36.6 2.0 %collective-permute-start.4 = (f32[32,4,128]{2,0,1:T(8,128)S(1)}, f32[32,4,128]{2,0,1:T(8,128)S(1)}, u32[]{:S(2)}, u32[]{:S(2)}) collective-permute-start(f32[32,4,128]{2,0,1:T(8,128)S(1)} %bitcast.31), channel_id=1, source_target_pairs={{0,1},{1,0},{2,3},{3,2},{4,5},{5,4},{6,7},{7,6},{8,9},{9,8},{10,11... | collective-permute-start | bytes 196616 | tf_op jit(solution)/shard_map/ppermute | solution.py:14
  38.6 4.1 %collective-permute-done.4 = f32[32,4,128]{2,0,1:T(8,128)S(1)} collective-permute-done((f32[32,4,128]{2,0,1:T(8,128)S(1)}, f32[32,4,128]{2,0,1:T(8,128)S(1)}, u32[]{:S(2)}, u32[]{:S(2)}) %collective-permute-start.4) | collective-permute-done | bytes 65568 | tf_op jit(solution)/shard_map/ppermute | solution.py:14
  42.8 5.5 %collective-permute-start.5 = (f32[32,4,128]{2,0,1:T(8,128)S(1)}, f32[32,4,128]{2,0,1:T(8,128)S(1)}, u32[]{:S(2)}, u32[]{:S(2)}) collective-permute-start(f32[32,4,128]{2,0,1:T(8,128)S(1)} %add_select_fusion.2), channel_id=1, source_target_pairs={{0,2},{1,3},{2,0},{3,1},{4,6},{5,7},{6,4},{7,5},{8,10},{9,11},{10,... | collective-permute-start | bytes 196616 | tf_op jit(solution)/shard_map/ppermute | solution.py:14
  48.3 2.2 %collective-permute-done.5 = f32[32,4,128]{2,0,1:T(8,128)S(1)} collective-permute-done((f32[32,4,128]{2,0,1:T(8,128)S(1)}, f32[32,4,128]{2,0,1:T(8,128)S(1)}, u32[]{:S(2)}, u32[]{:S(2)}) %collective-permute-start.5) | collective-permute-done | bytes 65568 | tf_op jit(solution)/shard_map/ppermute | solution.py:14
  50.5 9.2 %collective-permute-start.6 = (f32[32,4,128]{2,0,1:T(8,128)S(1)}, f32[32,4,128]{2,0,1:T(8,128)S(1)}, u32[]{:S(2)}, u32[]{:S(2)}) collective-permute-start(f32[32,4,128]{2,0,1:T(8,128)S(1)} %add_select_fusion.1), channel_id=1, source_target_pairs={{0,4},{1,5},{2,6},{3,7},{4,0},{5,1},{6,2},{7,3},{8,12},{9,13},{10,... | collective-permute-start | bytes 196616 | tf_op jit(solution)/shard_map/ppermute | solution.py:14
  59.7 2.2 %collective-permute-done.6 = f32[32,4,128]{2,0,1:T(8,128)S(1)} collective-permute-done((f32[32,4,128]{2,0,1:T(8,128)S(1)}, f32[32,4,128]{2,0,1:T(8,128)S(1)}, u32[]{:S(2)}, u32[]{:S(2)}) %collective-permute-start.6) | collective-permute-done | bytes 65568 | tf_op jit(solution)/shard_map/ppermute | solution.py:14
  62.0 15.4 %collective-permute-start.7 = (f32[32,4,128]{2,0,1:T(8,128)S(1)}, f32[32,4,128]{2,0,1:T(8,128)S(1)}, u32[]{:S(2)}, u32[]{:S(2)}) collective-permute-start(f32[32,4,128]{2,0,1:T(8,128)S(1)} %add_select_fusion), channel_id=1, source_target_pairs={{0,8},{1,9},{2,10},{3,11},{4,12},{5,13},{6,14},{7,15},{8,0},{9,1},... | collective-permute-start | bytes 196616 | tf_op jit(solution)/shard_map/ppermute | solution.py:14
  77.4 9.6 %shift_right_arithmetic.152 = s32[2048,4,512]{2,1,0:T(4,128)} broadcast(s32[2048,512]{1,0:T(8,128)} %param.18), dimensions={0,2} | broadcast | bytes 20971520 | tf_op jit(solution)/shard_map/shift_right_arithmetic | solution.py:28
  87.1 19.4 %shift_right_arithmetic.153 = s32[64,128,512]{2,1,0:T(8,128)} reshape(s32[2048,4,512]{2,1,0:T(4,128)} %shift_right_arithmetic.152) | data formatting | bytes 33554432 | tf_op jit(solution)/shard_map/shift_right_arithmetic | solution.py:28
  106.5 29.0 %all_gather.3 = bf16[32,64,128]{2,0,1:T(8,128)(2,1)S(1)} all-gather(bf16[32,4,128]{2,0,1:T(8,128)(2,1)S(1)} %multiply_convert_fusion.8), channel_id=1, replica_groups=mesh['dp'=32,'tensor'=16] {'tensor'}, dimensions={1}, use_global_device_ids=true | all-gather | bytes 557056 | tf_op jit(solution)/shard_map/all_gather | solution.py:199
  135.6 8.3 %fusion.3 = bf16[32,512]{1,0:T(8,128)(2,1)} fusion(bf16[32,64,128]{2,0,1:T(8,128)(2,1)S(1)} %all_gather.3, s32[64,128,512]{2,1,0:T(8,128)} %shift_right_arithmetic.153, f32[64,512]{1,0:T(8,128)S(1)} %convert_element_type.113, s32[128]{0:T(128)S(1)} %shift_right_arithmetic.130), kind=kOutput, calls=%fused_computation.6 | convolution fusion | flops 297811968 | bytes 17465856 | tf_op jit(solution)/shard_map/dot_general | solution.py:201
  (42 shorter events, 3.6 us)
Async XLA Ops:
  0.0 20.9 %copy-start.1 = (s32[32,1,64]{2,1,0:T(1,128)S(1)}, s32[32,1,64]{2,1,0:T(1,128)}, u32[]{:S(2)}) copy-start(s32[32,1,64]{2,1,0:T(1,128)} %param.16) | copy-start | bytes 24580
  1.8 19.1 %collective-permute-start = (bf16[32,4,128]{2,1,0:T(4,128)(2,1)S(1)}, bf16[32,4,128]{2,1,0:T(4,128)(2,1)S(1)}, u32[]{:S(2)}, u32[]{:S(2)}) collective-permute-start(bf16[32,4,128]{2,1,0:T(4,128)(2,1)S(1)} %pad_maximum_fusion), channel_id=1, source_target_pairs={{0,1},{1,0},{2,3},{3,2},{4,5},{5,4},{6,7},{7,6},{8,9},{9,8},{10,11... | collective-permute-start | bytes 98312 | tf_op jit(solution)/shard_map/ppermute | solution.py:14
  22.2 9.6 %collective-permute-start.3 = (f32[32,4]{1,0:T(8,128)S(1)}, f32[32,4]{1,0:T(8,128)S(1)}, u32[]{:S(2)}, u32[]{:S(2)}) collective-permute-start(f32[32,4]{1,0:T(8,128)S(1)} %slice_select_fusion.1), channel_id=1, source_target_pairs={{0,1},{1,0},{2,3},{3,2},{4,5},{5,4},{6,7},{7,6},{8,9},{9,8},{10,11... | collective-permute-start | bytes 1544 | tf_op jit(solution)/shard_map/ppermute | solution.py:14
  24.2 7.6 %collective-permute-start.1 = (f32[32,4]{1,0:T(8,128)S(1)}, f32[32,4]{1,0:T(8,128)S(1)}, u32[]{:S(2)}, u32[]{:S(2)}) collective-permute-start(f32[32,4]{1,0:T(8,128)S(1)} %slice_select_fusion.2), channel_id=1, source_target_pairs={{0,1},{1,0},{2,3},{3,2},{4,5},{5,4},{6,7},{7,6},{8,9},{9,8},{10,11... | collective-permute-start | bytes 1544 | tf_op jit(solution)/shard_map/ppermute | solution.py:14
  29.8 6.2 %collective-permute-start.2 = (f32[32,4,128]{2,1,0:T(4,128)S(1)}, f32[32,4,128]{2,1,0:T(4,128)S(1)}, u32[]{:S(2)}, u32[]{:S(2)}) collective-permute-start(f32[32,4,128]{2,1,0:T(4,128)S(1)} %slice_select_fusion), channel_id=1, source_target_pairs={{0,1},{1,0},{2,3},{3,2},{4,5},{5,4},{6,7},{7,6},{8,9},{9,8},{10,11... | collective-permute-start | bytes 196616 | tf_op jit(solution)/shard_map/ppermute | solution.py:14
  36.6 6.2 %collective-permute-start.4 = (f32[32,4,128]{2,0,1:T(8,128)S(1)}, f32[32,4,128]{2,0,1:T(8,128)S(1)}, u32[]{:S(2)}, u32[]{:S(2)}) collective-permute-start(f32[32,4,128]{2,0,1:T(8,128)S(1)} %bitcast.31), channel_id=1, source_target_pairs={{0,1},{1,0},{2,3},{3,2},{4,5},{5,4},{6,7},{7,6},{8,9},{9,8},{10,11... | collective-permute-start | bytes 196616 | tf_op jit(solution)/shard_map/ppermute | solution.py:14
  42.8 7.7 %collective-permute-start.5 = (f32[32,4,128]{2,0,1:T(8,128)S(1)}, f32[32,4,128]{2,0,1:T(8,128)S(1)}, u32[]{:S(2)}, u32[]{:S(2)}) collective-permute-start(f32[32,4,128]{2,0,1:T(8,128)S(1)} %add_select_fusion.2), channel_id=1, source_target_pairs={{0,2},{1,3},{2,0},{3,1},{4,6},{5,7},{6,4},{7,5},{8,10},{9,11},{10,... | collective-permute-start | bytes 196616 | tf_op jit(solution)/shard_map/ppermute | solution.py:14
  50.5 11.4 %collective-permute-start.6 = (f32[32,4,128]{2,0,1:T(8,128)S(1)}, f32[32,4,128]{2,0,1:T(8,128)S(1)}, u32[]{:S(2)}, u32[]{:S(2)}) collective-permute-start(f32[32,4,128]{2,0,1:T(8,128)S(1)} %add_select_fusion.1), channel_id=1, source_target_pairs={{0,4},{1,5},{2,6},{3,7},{4,0},{5,1},{6,2},{7,3},{8,12},{9,13},{10,... | collective-permute-start | bytes 196616 | tf_op jit(solution)/shard_map/ppermute | solution.py:14
  62.0 44.5 %collective-permute-start.7 = (f32[32,4,128]{2,0,1:T(8,128)S(1)}, f32[32,4,128]{2,0,1:T(8,128)S(1)}, u32[]{:S(2)}, u32[]{:S(2)}) collective-permute-start(f32[32,4,128]{2,0,1:T(8,128)S(1)} %add_select_fusion), channel_id=1, source_target_pairs={{0,8},{1,9},{2,10},{3,11},{4,12},{5,13},{6,14},{7,15},{8,0},{9,1},... | collective-permute-start | bytes 196616 | tf_op jit(solution)/shard_map/ppermute | solution.py:14
  87.1 19.4 %copy-start = (s32[64,512]{1,0:T(8,128)S(1)}, s32[64,512]{1,0:T(8,128)}, u32[]{:S(2)}) copy-start(s32[64,512]{1,0:T(8,128)} %param.19) | copy-start | bytes 393220
where the time goes:
time: 145 us; the launch traced here: 144 us
  starting transfers between devices  43.8 us (30%)
  local copies, waits for them, and re-layouts  36.7 us (25%)
  blocking collectives  29 us (20%)
  waiting for transfers between devices  12.6 us (9%)
  matrix products  11.4 us (8%)
  other arithmetic  10 us (7%)
    ppermute x8, starting transfers between devices, swapped(): lax.ppermute(array, axis, [(i, i ^ 1 << stride) for i in range(lax.axis_s...  43.8 us
    shift_right_arithmetic x2, local copies, waits for them, and re-layouts, unpack_rows(): jnp.right_shift(code_words[:, None, :], shifts[None, :, None])  29.1 us
    all_gather x1, blocking collectives, per_device(): piece = lax.all_gather(rotated, 'tensor', axis=1, tiled=True)  29 us
    ppermute x8, waiting for transfers between devices, swapped(): lax.ppermute(array, axis, [(i, i ^ 1 << stride) for i in range(lax.axis_s...  12.6 us
    dot_general x1, matrix products, per_device(): projected = jnp.dot(flat_piece, weight, preferred_element_type=jnp.float32)  8.35 us
    shift_right_arithmetic x10, local copies, waits for them, and re-layouts, unpack_codes(): jnp.right_shift(code_words[..., None], shifts)  7.59 us
    unnamed x2, other arithmetic  3.15 us
  transfers between devices with their start and end apart: 8, of which 4 were waited for; matrix products, arithmetic and copies ran while one was open for 32% of the time, Pallas kernels for 0%

commit v1 on v0

v1 whole, which is shorter than its diff:
```python
import functools

import jax
import jax.numpy as jnp
import numpy as np
from jax import lax
from jax.experimental import pallas as pl
from jax.experimental.pallas import tpu as pltpu
from jax.sharding import PartitionSpec as P

rope_base = 10000.0
neg_floor = -1e30
code_offset = 7.5
cache_step = 256.0
weight_step = 8192.0

rows = 32
head_width = 128
local_heads = 4
half_tokens = 64
chunk = 8
nt = (((1,), (1,)), ((), ()))


def rope_angles(positions):
    frequency = rope_base ** (-(np.arange(64) * 2.0 / head_width))
    return np.asarray(positions, np.float64)[..., None] * frequency


def key_tables():
    lane = np.arange(512)
    plane, low, word = lane // 128, lane % 128 // 32, lane % 32
    entry = 4 * word + plane
    position = 4 * np.arange(16)[:, None] + low[None, :]
    out = []
    for half in range(2):
        angle = rope_angles(np.arange(128))[half * half_tokens + position, (entry % 64)[None, :]]
        sign = np.where(entry < 64, -1.0, 1.0)
        scale = head_width**-0.5 / cache_step
        out.append(np.stack([np.cos(angle) * scale, np.sin(angle) * sign * scale]))
    return np.stack(out).astype(np.float32)


def query_table():
    angle = rope_angles(np.arange(136))
    return np.concatenate([np.cos(angle), np.cos(angle), -np.sin(angle), np.sin(angle)], -1).astype(
        np.float32
    )


def selector():
    lane = np.arange(512)
    entry = 4 * (lane % 32) + lane // 128
    return (np.arange(128)[:, None] == entry[None, :]).astype(np.float32)


def swap_words():
    lane = np.arange(128)
    return (lane[:, None] == (lane ^ 16)[None, :]).astype(np.float32)


def token_spread():
    return (np.arange(64)[:, None] % 4 == np.arange(128)[None, :] // 32).astype(np.float32)


def hadamard_pair():
    column = np.arange(256)
    target = (column // 32 % 2) * 128 + 4 * (column % 32) + column // 64
    both = np.arange(256)[:, None] & target[None, :]
    parity = np.zeros_like(both)
    for bit in range(8):
        parity ^= both >> bit & 1
    return (1.0 - 2.0 * parity).astype(np.float32)


def iota(shape, dim):
    return lax.broadcasted_iota(jnp.int32, shape, dim)


def unpack_planes(codes):
    return [
        jnp.bitwise_and(jnp.right_shift(codes, 4 * j), 15).astype(jnp.float32) - code_offset
        for j in range(4)
    ]


def spread_scales(scales_ref, spread_ref):
    one_hot = (iota((512, rows), 0) // 16 == iota((512, rows), 1)).astype(jnp.bfloat16)
    by_row = jnp.dot(
        one_hot,
        scales_ref[...].astype(jnp.float32).astype(jnp.bfloat16),
        preferred_element_type=jnp.float32,
    )
    mine = iota((512, half_tokens), 1) // 4 == iota((512, half_tokens), 0) % 16
    kept = jnp.where(mine, by_row, 0.0).astype(jnp.bfloat16)
    return jnp.dot(kept, spread_ref[...], preferred_element_type=jnp.float32)


def rotate_rows(vectors, cosine, sine):
    return vectors * cosine + pltpu.roll(vectors, 64, 1) * sine


def attend(
    half,
    lengths_ref,
    q_ref,
    q_scratch,
    cosine,
    sine,
    key_now,
    value_now,
    select_ref,
    key_ref,
    value_ref,
    store,
):
    q_scratch[...] = q_ref[...].astype(jnp.float32)
    by_head = [
        rotate_rows(q_scratch[pl.ds(h, rows, stride=local_heads), :], cosine, sine)
        for h in range(local_heads)
    ]
    q_rot = jnp.concatenate(by_head, axis=0).astype(jnp.bfloat16)
    spread = jnp.dot(q_rot, select_ref[...], preferred_element_type=jnp.float32)
    new_all = lax.dot_general(
        q_rot, key_now, nt, preferred_element_type=jnp.float32
    ) * np.float32(head_width**-0.5)
    lane_low = iota((1, 512), 1) % 128 // 32
    size = local_heads * chunk
    row = iota((4 * size, 128), 0)
    lane = iota((4 * size, 128), 1)
    position = jnp.where(
        row % chunk == lane // 16,
        half * half_tokens + 4 * (lane % 16) + row // size,
        1 << 20,
    )
    for b in range(rows // chunk):
        pick = lambda a: jnp.concatenate(
            [a[h * rows + b * chunk : h * rows + (b + 1) * chunk] for h in range(local_heads)], 0
        )
        q_block = pick(spread)
        left = jnp.concatenate(
            [jnp.where(lane_low == low, q_block, 0.0) for low in range(4)], axis=0
        ).astype(jnp.bfloat16)
        cache = pl.ds(b * 128, 128)
        scores = lax.dot_general(left, key_ref[cache, :], nt, preferred_element_type=jnp.float32)
        length_row = jnp.full((1, 128), lengths_ref[b * chunk], jnp.int32)
        for i in range(1, chunk):
            length_row = jnp.where(
                iota((1, 128), 1) // 16 >= i, lengths_ref[b * chunk + i], length_row
            )
        live = position < length_row
        scores = jnp.where(live, scores, neg_floor)
        new_block = pick(new_all)
        mine = jnp.logical_and(
            iota((size, rows), 1) == b * chunk + iota((size, rows), 0) % chunk, half == 0
        )
        new_block = jnp.where(mine, new_block, neg_floor)
        parts = [scores[low * size : (low + 1) * size] for low in range(4)]
        top = jnp.maximum(
            jnp.max(
                jnp.maximum(jnp.maximum(parts[0], parts[1]), jnp.maximum(parts[2], parts[3])),
                axis=1,
                keepdims=True,
            ),
            jnp.max(new_block, axis=1, keepdims=True),
        )
        weights = jnp.where(
            live, jnp.exp(scores - jnp.concatenate([top] * 4, axis=0)), 0.0
        ).astype(jnp.bfloat16)
        new_weight = jnp.where(mine, jnp.exp(new_block - top), 0.0).astype(jnp.bfloat16)
        wide = weights.astype(jnp.float32)
        total = jnp.sum(
            wide[:size] + wide[size : 2 * size] + wide[2 * size : 3 * size] + wide[3 * size :],
            axis=1,
            keepdims=True,
        ) + jnp.sum(new_weight.astype(jnp.float32), axis=1, keepdims=True)
        crossed = jnp.dot(weights, value_ref[cache, :], preferred_element_type=jnp.float32)
        mixed = jnp.where(lane_low == 0, crossed[:size], 0.0)
        for low in range(1, 4):
            mixed = jnp.where(lane_low == low, crossed[low * size : (low + 1) * size], mixed)
        high = mixed.astype(jnp.bfloat16)
        rest = (mixed - high.astype(jnp.float32)).astype(jnp.bfloat16)
        weighted = (
            lax.dot_general(high, select_ref[...], nt, preferred_element_type=jnp.float32)
            + lax.dot_general(rest, select_ref[...], nt, preferred_element_type=jnp.float32)
            + jnp.dot(new_weight, value_now, preferred_element_type=jnp.float32)
        )
        some = total > 0.0
        floor_total = jnp.where(some, total, 1.0)
        logsum = jnp.where(some, top + jnp.log(floor_total), neg_floor)
        result = weighted / floor_total
        for h in range(local_heads):
            part = slice(h * chunk, (h + 1) * chunk)
            store(b, h, result[part], logsum[part])


def position_tables(lengths_ref, table_ref, table_scratch):
    for r in range(rows):
        table_scratch[pl.ds(r, 1), :] = table_ref[pl.ds(lengths_ref[r], 1), :]
    return table_scratch[:, :128], table_scratch[:, 128:]


def pick_head(array_ref, index):
    wide = array_ref[...].astype(jnp.float32)
    return jnp.sum(jnp.where(iota(wide.shape, 1) == index, wide, 0.0), axis=1)


def own_kernel(
    lengths_ref,
    q_ref,
    new_key_ref,
    new_value_ref,
    key_codes_ref,
    key_scales_ref,
    value_codes_ref,
    value_scales_ref,
    key_table_ref,
    query_table_ref,
    select_ref,
    swap_ref,
    spread_ref,
    key_ref,
    value_ref,
    table_ref,
    now_ref,
    own_ref,
    own_log_ref,
    q_scratch,
):
    rank = lax.axis_index("tensor")
    half = lax.rem(rank, 2)
    head = lax.div(rank, 2)
    cosine, sine = position_tables(lengths_ref, query_table_ref, table_ref)
    key_now = rotate_rows(pick_head(new_key_ref, head), cosine, sine).astype(jnp.bfloat16)
    value_now = pick_head(new_value_ref, head).astype(jnp.bfloat16)
    now_ref[0] = key_now
    now_ref[1] = value_now
    scales = spread_scales(key_scales_ref, spread_ref)
    swap = swap_ref[...]
    for j, plane in enumerate(unpack_planes(key_codes_ref[...])):
        partner = jnp.dot(plane.astype(jnp.bfloat16), swap, preferred_element_type=jnp.float32)
        lanes = slice(j * 128, (j + 1) * 128)
        shape = (rows, 16, 128)
        turned = (
            plane.reshape(shape) * key_table_ref[half, 0, :, lanes][None]
            + partner.reshape(shape) * key_table_ref[half, 1, :, lanes][None]
        ).reshape(512, 128)
        key_ref[:, lanes] = (turned * scales).astype(jnp.bfloat16)
    scales = spread_scales(value_scales_ref, spread_ref) * np.float32(1.0 / cache_step)
    for j, plane in enumerate(unpack_planes(value_codes_ref[...])):
        value_ref[:, j * 128 : (j + 1) * 128] = (plane * scales).astype(jnp.bfloat16)

    lane_head = iota((chunk, 128), 1) // 32

    def store(b, h, result, logsum):
        block = pl.ds(b * chunk, chunk)
        own_ref[block, h * 128 : (h + 1) * 128] = result
        spread_log = jnp.broadcast_to(logsum, (chunk, 128))
        own_log_ref[block, :] = (
            spread_log if h == 0 else jnp.where(lane_head == h, spread_log, own_log_ref[block, :])
        )

    attend(
        half, lengths_ref, q_ref, q_scratch, cosine, sine, key_now, value_now,
        select_ref, key_ref, value_ref, store,
    )


def partner_kernel(
    lengths_ref,
    q_ref,
    table_ref,
    now_ref,
    key_ref,
    value_ref,
    select_ref,
    out_ref,
    q_scratch,
    out_scratch,
):
    half = lax.rem(lax.axis_index("tensor"), 2)
    lane = iota((chunk, 128), 1)
    lane_head = lane // 32

    def store(b, h, result, logsum):
        block = pl.ds(b * chunk, chunk)
        out_scratch[block, h * 128 : (h + 1) * 128] = result
        whole = jnp.broadcast_to(logsum, (chunk, 128))
        first = whole.astype(jnp.bfloat16).astype(jnp.float32)
        second = (whole - first).astype(jnp.bfloat16).astype(jnp.float32)
        third = whole - first - second
        which = lane % 32
        pieces = jnp.where(
            which == 0, first, jnp.where(which == 1, second, jnp.where(which == 2, third, 0.0))
        )
        tail = slice(512, 640)
        out_scratch[block, tail] = (
            pieces if h == 0 else jnp.where(lane_head == h, pieces, out_scratch[block, tail])
        )

    attend(
        half, lengths_ref, q_ref, q_scratch, table_ref[:, :128], table_ref[:, 128:],
        now_ref[0], now_ref[1], select_ref, key_ref, value_ref, store,
    )
    out_ref[...] = out_scratch[...].astype(jnp.bfloat16)


def combine_kernel(own_ref, own_log_ref, other_ref, out_ref):
    lane_head = iota((rows, 128), 1) // 32
    other_log = other_ref[:, 512:640].astype(jnp.float32)
    for h in range(local_heads):
        lanes = slice(h * 128, (h + 1) * 128)
        theirs = jnp.sum(jnp.where(lane_head == h, other_log, 0.0), axis=1, keepdims=True)
        mine = own_log_ref[:, h * 32 : h * 32 + 1]
        joint = jnp.maximum(mine, theirs)
        mine_factor = jnp.exp(mine - joint)
        their_factor = jnp.exp(theirs - joint)
        scale = 1.0 / (mine_factor + their_factor)
        out_ref[:, lanes] = (
            own_ref[:, lanes] * (mine_factor * scale)
            + other_ref[:, lanes].astype(jnp.float32) * (their_factor * scale)
        ).astype(jnp.bfloat16)


def weight_kernel(codes_ref, scales_ref, out_ref):
    for b in range(codes_ref.shape[0] // 64):
        words = codes_ref[b * 64 : (b + 1) * 64, :]
        first = pl.program_id(0) * (codes_ref.shape[0] // 32) + 2 * b
        scale = [
            (scales_ref[pl.ds(first + n, 1), :].astype(jnp.float32) / weight_step) for n in range(2)
        ]
        for k in range(4):
            plane = (
                jnp.bitwise_and(jnp.right_shift(words, 4 * k), 15).astype(jnp.float32) - code_offset
            )
            out_ref[b * 256 + k * 64 : b * 256 + (k + 1) * 64, :] = jnp.concatenate(
                [plane[:32] * scale[0], plane[32:] * scale[1]], axis=0
            ).astype(jnp.bfloat16)


def project_kernel(gathered_ref, hadamard_ref, weight_ref, out_ref):
    hadamard = hadamard_ref[...]
    left = jnp.dot(gathered_ref[:, :256], hadamard, preferred_element_type=jnp.float32)
    right = jnp.dot(gathered_ref[:, 256:], hadamard, preferred_element_type=jnp.float32)
    factor = np.float32(8192.0**-0.5)
    total = jnp.zeros((rows, 512), jnp.float32)
    for p, mixed in enumerate((left + right, left - right)):
        blocks = [mixed[z * rows : (z + 1) * rows] for z in range(16)]
        for bit in range(4):
            step = 1 << bit
            blocks = [
                blocks[z] + blocks[z ^ step] if z & step == 0 else blocks[z ^ step] - blocks[z]
                for z in range(16)
            ]
        for z in range(16):
            start = (2 * z + p) * 256
            total = total + jnp.dot(
                (blocks[z] * factor).astype(jnp.bfloat16),
                weight_ref[start : start + 256, :],
                preferred_element_type=jnp.float32,
            )
    out_ref[...] = total.astype(jnp.bfloat16)


vmem = pl.BlockSpec(memory_space=pltpu.VMEM)
smem = pl.BlockSpec(memory_space=pltpu.SMEM)
params = pltpu.CompilerParams(vmem_limit_bytes=40 * 1024 * 1024)


def per_device(
    queries,
    new_key,
    new_value,
    key_codes,
    key_scales,
    value_codes,
    value_scales,
    lengths,
    out_codes,
    out_scales,
):
    pairs = [(i, i ^ 1) for i in range(16)]
    f32, bf16 = jnp.float32, jnp.bfloat16
    shape = jax.ShapeDtypeStruct
    other_queries = lax.ppermute(queries, "tensor", pairs)
    select = jnp.asarray(selector(), bf16)
    keys, values, table, now, own, own_log = pl.pallas_call(
        own_kernel,
        out_shape=(
            shape((512, 512), bf16),
            shape((512, 512), bf16),
            shape((rows, 256), f32),
            shape((2, rows, 128), bf16),
            shape((rows, 512), f32),
            shape((rows, 128), f32),
        ),
        in_specs=[smem] + [vmem] * 12,
        out_specs=(vmem,) * 6,
        scratch_shapes=[pltpu.VMEM((128, 128), f32)],
        compiler_params=params,
        cost_estimate=pl.CostEstimate(flops=400_000_000, bytes_accessed=2_000_000, transcendentals=65536),
        name="own_heads",
    )(
        lengths,
        queries.reshape(128, 128),
        new_key,
        new_value,
        key_codes.reshape(512, 128),
        key_scales.reshape(rows, half_tokens),
        value_codes.reshape(512, 128),
        value_scales.reshape(rows, half_tokens),
        jnp.asarray(key_tables()),
        jnp.asarray(query_table()),
        select,
        jnp.asarray(swap_words(), bf16),
        jnp.asarray(token_spread(), bf16),
    )
    sending = pl.pallas_call(
        partner_kernel,
        out_shape=shape((rows, 640), bf16),
        in_specs=[smem] + [vmem] * 6,
        out_specs=vmem,
        scratch_shapes=[pltpu.VMEM((128, 128), f32), pltpu.VMEM((rows, 640), f32)],
        compiler_params=params,
        name="other_heads",
    )(lengths, other_queries.reshape(128, 128), table, now, keys, values, select)
    received = lax.ppermute(sending, "tensor", pairs)
    out_codes, _ = lax.optimization_barrier((out_codes, sending))
    steps = 8
    weight = pl.pallas_call(
        weight_kernel,
        grid=(steps,),
        out_shape=shape((8192, 512), bf16),
        in_specs=[
            pl.BlockSpec((2048 // steps, 512), lambda i: (i, 0)),
            pl.BlockSpec((64, 512), lambda i: (0, 0)),
        ],
        out_specs=pl.BlockSpec((8192 // steps, 512), lambda i: (i, 0)),
        compiler_params=params,
        cost_estimate=pl.CostEstimate(flops=20_000_000, bytes_accessed=12_000_000, transcendentals=0),
        name="unpack_weight",
    )(out_codes, out_scales)
    attended = pl.pallas_call(
        combine_kernel,
        out_shape=shape((rows, 512), bf16),
        in_specs=[vmem] * 3,
        out_specs=vmem,
        compiler_params=params,
        name="combine_halves",
    )(own, own_log, received)
    gathered = lax.all_gather(attended, "tensor", axis=0, tiled=True)
    return pl.pallas_call(
        project_kernel,
        out_shape=shape((rows, 512), bf16),
        in_specs=[vmem] * 3,
        out_specs=vmem,
        compiler_params=params,
        name="project",
    )(gathered, jnp.asarray(hadamard_pair(), bf16), weight)


def solution(mesh):
    return jax.shard_map(
        per_device,
        mesh=mesh,
        in_specs=(
            P("dp", "tensor", None),
            P("dp", None, None),
            P("dp", None, None),
            P("dp", "tensor", None),
            P("dp", "tensor", None),
            P("dp", "tensor", None),
            P("dp", "tensor", None),
            P("dp"),
            P(None, "tensor"),
            P(None, "tensor"),
        ),
        out_specs=P("dp", "tensor"),
        check_vma=False,
    )
```

time: 145 us -> 70.5 us (0.49)
  starting transfers between devices: 43.8 us -> 5.96 us
  local copies, waits for them, and re-layouts: 36.7 us -> 13.7 us
  waiting for transfers between devices: 12.6 us -> 0.03 us
  Pallas kernels: 0 us -> 11.7 us
  matrix products: 11.4 us -> 0 us
  other arithmetic: 10 us -> 0 us
  blocking collectives: 29 us -> 38.2 us
    ppermute x8 -> x2, starting transfers between devices: 43.8 us -> 5.96 us  [the longest x1 3.94 us: per_device(): other_queries = lax.ppermute(queries, 'tensor', pairs)]
    shift_right_arithmetic x12 -> x0, local copies, waits for them, and re-layouts: 36.6 us -> none  [the longest x2 29.1 us: unpack_rows(): jnp.right_shift(code_words[:, None, :], shifts[None, :, None])]
    unnamed x4 -> x32, local copies, waits for them, and re-layouts: 0.01 us -> 13.7 us
    ppermute x8 -> x2, waiting for transfers between devices: 12.6 us -> 0.03 us  [the longest x1 0.03 us: per_device(): other_queries = lax.ppermute(queries, 'tensor', pairs)]
    pallas_call x0 -> x5, Pallas kernels: none -> 11.7 us  [the longest x1 3.29 us: per_device(): pl.pallas_call(own_kernel, out_shape=(shape((512, 512), bf16), shape((512...]
    dot_general x6 -> x0, matrix products: 11.4 us -> none  [the longest x1 8.35 us: per_device(): projected = jnp.dot(flat_piece, weight, preferred_element_type=jnp.float32)]
    all_gather x1, blocking collectives: 29 us -> 38.2 us  [per_device(): gathered = lax.all_gather(attended, 'tensor', axis=0, tiled=True)]
    convert_element_type x9 -> x0, other arithmetic: 3.23 us -> none  [the longest x1 0.85 us: per_device(): new_key.astype(jnp.float32)]
  transfers between devices with their start and end apart: 8 -> 2, of which waited for: 4 -> 0; matrix products, arithmetic and copies ran while one was open for 32% -> 0% of each run, Pallas kernels for 0% -> 9%
where the time goes in v1:
time: 70.5 us; the launch traced here: 69.7 us
  blocking collectives  38.2 us (54%)
  local copies, waits for them, and re-layouts  13.7 us (19%)
  Pallas kernels  11.7 us (17%)
  starting transfers between devices  5.96 us (8%)
    all_gather x1, blocking collectives, per_device(): gathered = lax.all_gather(attended, 'tensor', axis=0, tiled=True)  38.2 us
    unnamed x32, local copies, waits for them, and re-layouts  13.7 us
    ppermute x1, starting transfers between devices, per_device(): other_queries = lax.ppermute(queries, 'tensor', pairs)  3.94 us
    pallas_call x1, Pallas kernels, per_device(): pl.pallas_call(own_kernel, out_shape=(shape((512, 512), bf16), shape((512...  3.29 us
    pallas_call x1, Pallas kernels, per_device(): pl.pallas_call(weight_kernel, grid=(steps,), out_shape=shape((8192, 512),...  3.02 us
    pallas_call x1, Pallas kernels, per_device(): pl.pallas_call(partner_kernel, out_shape=shape((rows, 640), bf16), in_spe...  2.65 us
    pallas_call x1, Pallas kernels, per_device(): pl.pallas_call(project_kernel, out_shape=shape((rows, 512), bf16), in_spe...  2.53 us
    ppermute x1, starting transfers between devices, per_device(): received = lax.ppermute(sending, 'tensor', pairs)  2.02 us
  transfers between devices with their start and end apart: 2, of which 0 were waited for; matrix products, arithmetic and copies ran while one was open for 0% of the time, Pallas kernels for 9%

profile of v1, /device:TPU:24, one launch (start us, length us, event | category | flops | bytes accessed | tf_op | source)
XLA Modules:
  0.0 69.7 jit_solution(17821708139193217674)
XLA Ops:
  0.0 0.0 copy-start.2
  0.0 3.9 %collective-permute-start = (bf16[32,4,128]{2,1,0:T(4,128)(2,1)}, bf16[32,4,128]{2,1,0:T(4,128)(2,1)S(1)}, u32[]{:S(2)}, u32[]{:S(2)}) collective-permute-start(bf16[32,4,128]{2,1,0:T(4,128)(2,1)} %param.16), channel_id=1, source_target_pairs={{0,1},{1,0},{2,3},{3,2},{4,5},{5,4},{6,7},{7,6},{8,9},{9,8},{10,11... | collective-permute-start | bytes 98312 | tf_op jit(solution)/shard_map/ppermute | solution.py:385
  4.0 0.0 copy-start.3
  4.0 0.9 %copy-done.3 = bf16[128,512]{1,0:T(8,128)(2,1)S(1)} copy-done((bf16[128,512]{1,0:T(8,128)(2,1)S(1)}, bf16[128,512]{1,0:T(8,128)(2,1)}, u32[]{:S(2)}) %copy-start.3) | copy-done | bytes 131096
  4.9 0.0 copy-start.4
  4.9 0.7 copy-done.4
  5.5 0.0 copy-start.5
  5.5 0.9 %copy-done.5 = s32[32,1,2048]{2,1,0:T(1,128)S(1)} copy-done((s32[32,1,2048]{2,1,0:T(1,128)S(1)}, s32[32,1,2048]{2,1,0:T(1,128)}, u32[]{:S(2)}) %copy-start.5) | copy-done | bytes 262168
  6.5 0.0 copy-start.6
  6.5 0.9 %copy-done.6 = s32[32,1,2048]{2,1,0:T(1,128)S(1)} copy-done((s32[32,1,2048]{2,1,0:T(1,128)S(1)}, s32[32,1,2048]{2,1,0:T(1,128)}, u32[]{:S(2)}) %copy-start.6) | copy-done | bytes 262168
  7.4 0.8 %copy-done.7 = bf16[32,8,128]{2,1,0:T(8,128)(2,1)S(1)} copy-done((bf16[32,8,128]{2,1,0:T(8,128)(2,1)S(1)}, bf16[32,8,128]{2,1,0:T(8,128)(2,1)}, u32[]{:S(2)}) %copy-start.7) | copy-done | bytes 65560
  8.3 0.8 %copy-done.8 = bf16[32,8,128]{2,1,0:T(8,128)(2,1)S(1)} copy-done((bf16[32,8,128]{2,1,0:T(8,128)(2,1)S(1)}, bf16[32,8,128]{2,1,0:T(8,128)(2,1)}, u32[]{:S(2)}) %copy-start.8) | copy-done | bytes 65560
  9.1 0.8 %copy-done.9 = bf16[32,4,128]{2,1,0:T(4,128)(2,1)S(1)} copy-done((bf16[32,4,128]{2,1,0:T(4,128)(2,1)S(1)}, bf16[32,4,128]{2,1,0:T(4,128)(2,1)}, u32[]{:S(2)}) %copy-start.9) | copy-done | bytes 32792
  9.9 0.7 %copy-done.10 = s32[32,1,64]{2,1,0:T(1,128)S(1)} copy-done((s32[32,1,64]{2,1,0:T(1,128)S(1)}, s32[32,1,64]{2,1,0:T(1,128)}, u32[]{:S(2)}) %copy-start.10) | copy-done | bytes 8216
  10.6 0.7 %copy-done.11 = s32[32,1,64]{2,1,0:T(1,128)S(1)} copy-done((s32[32,1,64]{2,1,0:T(1,128)S(1)}, s32[32,1,64]{2,1,0:T(1,128)}, u32[]{:S(2)}) %copy-start.11) | copy-done | bytes 8216
  11.3 0.9 %copy-done.12 = f32[136,256]{1,0:T(8,128)S(1)} copy-done((f32[136,256]{1,0:T(8,128)S(1)}, f32[136,256]{1,0:T(8,128)}, u32[]{:S(2)}) %copy-start.12) | copy-done | bytes 139288
  12.2 0.9 %copy-done.13 = f32[2,2,16,512]{3,2,1,0:T(8,128)S(1)} copy-done((f32[2,2,16,512]{3,2,1,0:T(8,128)S(1)}, f32[2,2,16,512]{3,2,1,0:T(8,128)}, u32[]{:S(2)}) %copy-start.13) | copy-done | bytes 131096
  13.1 0.8 %copy-done.14 = bf16[128,128]{1,0:T(8,128)(2,1)S(1)} copy-done((bf16[128,128]{1,0:T(8,128)(2,1)S(1)}, bf16[128,128]{1,0:T(8,128)(2,1)}, u32[]{:S(2)}) %copy-start.14) | copy-done | bytes 32792
  13.9 0.7 %copy-done.15 = bf16[64,128]{1,0:T(8,128)(2,1)S(1)} copy-done((bf16[64,128]{1,0:T(8,128)(2,1)S(1)}, bf16[64,128]{1,0:T(8,128)(2,1)}, u32[]{:S(2)}) %copy-start.15) | copy-done | bytes 16408
  14.6 3.3 %own_heads.1 = (bf16[512,512]{1,0:T(8,128)(2,1)S(1)}, bf16[512,512]{1,0:T(8,128)(2,1)S(1)}, f32[32,256]{1,0:T(8,128)S(1)}, bf16[2,32,128]{2,1,0:T(8,128)(2,1)S(1...) custom-call(s32[32]{0:T(128)S(1)} %copy-done.4, bf16[128,128]{1,0:T(8,128)(2,1)S(1)} %bitcast.9, ...), custom_call_target="tpu_custom_call" | custom-call | flops 400000000 | bytes 2000000 | tf_op jit(solution)/shard_map/own_heads/pallas_call | solution.py:387
  17.9 0.0 collective-permute-done
  17.9 2.7 %other_heads.1 = bf16[32,640]{1,0:T(8,128)(2,1)S(1)} custom-call(s32[32]{0:T(128)S(1)} %copy-done.4, bf16[128,128]{1,0:T(8,128)(2,1)S(1)} %bitcast.6, f32[32,256]{1,0:T(8,128)S(1)} %get-tuple-element.14.table_ref, bf16[2,32,128]{2,1,0:T(8,128)(2,1)S(1)} %get-tuple-element.15.now_ref, bf16[512,512]{1,0:T(8,128)(2,1)S(1)} %get-tuple-element.16.key_ref, ...), custom_call_target="tpu_custom_call" | custom-call | tf_op jit(solution)/shard_map/other_heads/pallas_call | solution.py:418
  20.6 2.0 %collective-permute-start.1 = (bf16[32,640]{1,0:T(8,128)(2,1)S(1)}, bf16[32,640]{1,0:T(8,128)(2,1)S(1)}, u32[]{:S(2)}, u32[]{:S(2)}) collective-permute-start(bf16[32,640]{1,0:T(8,128)(2,1)S(1)} %other_heads.1), channel_id=1, source_target_pairs={{0,1},{1,0},{2,3},{3,2},{4,5},{5,4},{6,7},{7,6},{8,9},{9,8},{10,11... | collective-permute-start | bytes 122888 | tf_op jit(solution)/shard_map/ppermute | solution.py:427
  22.6 0.0 copy-start
  22.6 2.2 %copy-done = s32[2048,512]{1,0:T(8,128)S(1)} copy-done((s32[2048,512]{1,0:T(8,128)S(1)}, s32[2048,512]{1,0:T(8,128)}, u32[]{:S(2)}) %copy-start) | copy-done | bytes 4194328
  24.8 0.9 %copy-done.1 = s32[64,512]{1,0:T(8,128)S(1)} copy-done((s32[64,512]{1,0:T(8,128)S(1)}, s32[64,512]{1,0:T(8,128)}, u32[]{:S(2)}) %copy-start.1) | copy-done | bytes 131096
  25.7 3.0 %unpack_weight.1.weight_ref = bf16[8192,512]{1,0:T(8,128)(2,1)S(1)} custom-call(s32[2048,512]{1,0:T(8,128)S(1)} %copy-done, s32[64,512]{1,0:T(8,128)S(1)} %copy-done.1), custom_call_target="tpu_custom_call" | custom-call | flops 20000000 | bytes 12000000 | tf_op jit(solution)/shard_map/unpack_weight/pallas_call | solution.py:430
  28.7 0.0 collective-permute-done.1.other_ref
  28.7 0.2 combine_halves.1
  29.0 38.2 %all_gather.3.gathered_ref = bf16[512,512]{1,0:T(8,128)(2,1)S(1)} all-gather(bf16[32,512]{1,0:T(8,128)(2,1)S(1)} %combine_halves.1), channel_id=1, replica_groups=mesh['dp'=32,'tensor'=16] {'tensor'}, dimensions={0}, use_global_device_ids=true | all-gather | bytes 557056 | tf_op jit(solution)/shard_map/all_gather | solution.py:451
  67.2 0.0 copy-done.2
  67.2 2.5 %project.1 = bf16[32,512]{1,0:T(8,128)(2,1)} custom-call(bf16[512,512]{1,0:T(8,128)(2,1)S(1)} %all_gather.3.gathered_ref, bf16[256,256]{1,0:T(8,128)(2,1)S(1)} %copy-done.2, bf16[8192,512]{1,0:T(8,128)(2,1)S(1)} %unpack_weight.1.weight_ref), custom_call_target="tpu_custom_call" | custom-call | tf_op jit(solution)/shard_map/project/pallas_call | solution.py:452
  (10 shorter events, 0.0 us)
Async XLA Ops:
  0.0 67.2 %copy-start.2 = (bf16[256,256]{1,0:T(8,128)(2,1)S(1)}, bf16[256,256]{1,0:T(8,128)(2,1)}, u32[]{:S(2)}) copy-start(bf16[256,256]{1,0:T(8,128)(2,1)} %constant.17.clone.hadamard_ref) | copy-start | bytes 393220
  0.0 17.9 %collective-permute-start = (bf16[32,4,128]{2,1,0:T(4,128)(2,1)}, bf16[32,4,128]{2,1,0:T(4,128)(2,1)S(1)}, u32[]{:S(2)}, u32[]{:S(2)}) collective-permute-start(bf16[32,4,128]{2,1,0:T(4,128)(2,1)} %param.16), channel_id=1, source_target_pairs={{0,1},{1,0},{2,3},{3,2},{4,5},{5,4},{6,7},{7,6},{8,9},{9,8},{10,11... | collective-permute-start | bytes 98312 | tf_op jit(solution)/shard_map/ppermute | solution.py:385
  4.0 0.9 %copy-start.3 = (bf16[128,512]{1,0:T(8,128)(2,1)S(1)}, bf16[128,512]{1,0:T(8,128)(2,1)}, u32[]{:S(2)}) copy-start(bf16[128,512]{1,0:T(8,128)(2,1)} %constant.12.clone.select_ref) | copy-start | bytes 393220
  4.9 0.7 copy-start.4
  5.5 0.9 %copy-start.5 = (s32[32,1,2048]{2,1,0:T(1,128)S(1)}, s32[32,1,2048]{2,1,0:T(1,128)}, u32[]{:S(2)}) copy-start(s32[32,1,2048]{2,1,0:T(1,128)} %param.19) | copy-start | bytes 786436
  6.5 0.9 %copy-start.6 = (s32[32,1,2048]{2,1,0:T(1,128)S(1)}, s32[32,1,2048]{2,1,0:T(1,128)}, u32[]{:S(2)}) copy-start(s32[32,1,2048]{2,1,0:T(1,128)} %param.21) | copy-start | bytes 786436
  7.4 0.8 %copy-start.7 = (bf16[32,8,128]{2,1,0:T(8,128)(2,1)S(1)}, bf16[32,8,128]{2,1,0:T(8,128)(2,1)}, u32[]{:S(2)}) copy-start(bf16[32,8,128]{2,1,0:T(8,128)(2,1)} %new_key_ref.1) | copy-start | bytes 196612
  8.3 0.8 %copy-start.8 = (bf16[32,8,128]{2,1,0:T(8,128)(2,1)S(1)}, bf16[32,8,128]{2,1,0:T(8,128)(2,1)}, u32[]{:S(2)}) copy-start(bf16[32,8,128]{2,1,0:T(8,128)(2,1)} %new_value_ref.1) | copy-start | bytes 196612
  9.1 0.8 %copy-start.9 = (bf16[32,4,128]{2,1,0:T(4,128)(2,1)S(1)}, bf16[32,4,128]{2,1,0:T(4,128)(2,1)}, u32[]{:S(2)}) copy-start(bf16[32,4,128]{2,1,0:T(4,128)(2,1)} %param.16) | copy-start | bytes 98308
  9.9 0.7 %copy-start.10 = (s32[32,1,64]{2,1,0:T(1,128)S(1)}, s32[32,1,64]{2,1,0:T(1,128)}, u32[]{:S(2)}) copy-start(s32[32,1,64]{2,1,0:T(1,128)} %param.20) | copy-start | bytes 24580
  10.6 0.7 %copy-start.11 = (s32[32,1,64]{2,1,0:T(1,128)S(1)}, s32[32,1,64]{2,1,0:T(1,128)}, u32[]{:S(2)}) copy-start(s32[32,1,64]{2,1,0:T(1,128)} %param.22) | copy-start | bytes 24580
  11.3 0.9 %copy-start.12 = (f32[136,256]{1,0:T(8,128)S(1)}, f32[136,256]{1,0:T(8,128)}, u32[]{:S(2)}) copy-start(f32[136,256]{1,0:T(8,128)} %constant.14.clone.query_table_ref) | copy-start | bytes 417796
  12.2 0.9 %copy-start.13 = (f32[2,2,16,512]{3,2,1,0:T(8,128)S(1)}, f32[2,2,16,512]{3,2,1,0:T(8,128)}, u32[]{:S(2)}) copy-start(f32[2,2,16,512]{3,2,1,0:T(8,128)} %constant.13.clone.key_table_ref) | copy-start | bytes 393220
  13.1 0.8 %copy-start.14 = (bf16[128,128]{1,0:T(8,128)(2,1)S(1)}, bf16[128,128]{1,0:T(8,128)(2,1)}, u32[]{:S(2)}) copy-start(bf16[128,128]{1,0:T(8,128)(2,1)} %constant.15.clone.swap_ref) | copy-start | bytes 98308
  13.9 0.7 %copy-start.15 = (bf16[64,128]{1,0:T(8,128)(2,1)S(1)}, bf16[64,128]{1,0:T(8,128)(2,1)}, u32[]{:S(2)}) copy-start(bf16[64,128]{1,0:T(8,128)(2,1)} %constant.16.clone.spread_ref) | copy-start | bytes 49156
  20.6 8.1 %collective-permute-start.1 = (bf16[32,640]{1,0:T(8,128)(2,1)S(1)}, bf16[32,640]{1,0:T(8,128)(2,1)S(1)}, u32[]{:S(2)}, u32[]{:S(2)}) collective-permute-start(bf16[32,640]{1,0:T(8,128)(2,1)S(1)} %other_heads.1), channel_id=1, source_target_pairs={{0,1},{1,0},{2,3},{3,2},{4,5},{5,4},{6,7},{7,6},{8,9},{9,8},{10,11... | collective-permute-start | bytes 122888 | tf_op jit(solution)/shard_map/ppermute | solution.py:427
  22.6 2.2 %copy-start = (s32[2048,512]{1,0:T(8,128)S(1)}, s32[2048,512]{1,0:T(8,128)}, u32[]{:S(2)}) copy-start(s32[2048,512]{1,0:T(8,128)} %codes_ref) | copy-start | bytes 12582916
  24.8 0.9 %copy-start.1 = (s32[64,512]{1,0:T(8,128)S(1)}, s32[64,512]{1,0:T(8,128)}, u32[]{:S(2)}) copy-start(s32[64,512]{1,0:T(8,128)} %scales_ref.1) | copy-start | bytes 393220

commit v2 on v1

--- a/solution.py
+++ b/solution.py
@@ -48,33 +48,37 @@
     )
 
 
-def selector():
-    lane = np.arange(512)
-    entry = 4 * (lane % 32) + lane // 128
-    return (np.arange(128)[:, None] == entry[None, :]).astype(np.float32)
-
-
-def swap_words():
-    lane = np.arange(128)
-    return (lane[:, None] == (lane ^ 16)[None, :]).astype(np.float32)
-
-
-def token_spread():
-    return (np.arange(64)[:, None] % 4 == np.arange(128)[None, :] // 32).astype(np.float32)
-
-
-def hadamard_pair():
-    column = np.arange(256)
-    target = (column // 32 % 2) * 128 + 4 * (column % 32) + column // 64
-    both = np.arange(256)[:, None] & target[None, :]
-    parity = np.zeros_like(both)
-    for bit in range(8):
-        parity ^= both >> bit & 1
-    return (1.0 - 2.0 * parity).astype(np.float32)
-
-
 def iota(shape, dim):
     return lax.broadcasted_iota(jnp.int32, shape, dim)
+
+
+def one_hot(condition):
+    return jnp.where(condition, 1.0, 0.0).astype(jnp.bfloat16)
+
+
+def selector():
+    shape = (128, 512)
+    lane = iota(shape, 1)
+    return one_hot(iota(shape, 0) == 4 * (lane % 32) + lane // 128)
+
+
+def swap_words():
+    shape = (128, 128)
+    return one_hot(iota(shape, 0) == jnp.bitwise_xor(iota(shape, 1), 16))
+
+
+def token_spread():
+    return one_hot(iota((64, 128), 0) % 4 == iota((64, 128), 1) // 32)
+
+
+def hadamard_pair():
+    shape = (256, 256)
+    column = iota(shape, 1)
+    target = column // 32 % 2 * 128 + 4 * (column % 32) + column // 64
+    both = jnp.bitwise_and(iota(shape, 0), target)
+    for shift in (4, 2, 1):
+        both = jnp.bitwise_xor(both, jnp.right_shift(both, shift))
+    return (1.0 - 2.0 * jnp.bitwise_and(both, 1).astype(jnp.float32)).astype(jnp.bfloat16)
 
 
 def unpack_planes(codes):
@@ -84,42 +88,37 @@
     ]
 
 
-def spread_scales(scales_ref, spread_ref):
-    one_hot = (iota((512, rows), 0) // 16 == iota((512, rows), 1)).astype(jnp.bfloat16)
+def spread_scales(scales):
     by_row = jnp.dot(
-        one_hot,
-        scales_ref[...].astype(jnp.float32).astype(jnp.bfloat16),
+        one_hot(iota((512, rows), 0) // 16 == iota((512, rows), 1)),
+        scales.astype(jnp.float32).astype(jnp.bfloat16),
         preferred_element_type=jnp.float32,
     )
     mine = iota((512, half_tokens), 1) // 4 == iota((512, half_tokens), 0) % 16
     kept = jnp.where(mine, by_row, 0.0).astype(jnp.bfloat16)
-    return jnp.dot(kept, spread_ref[...], preferred_element_type=jnp.float32)
+    return jnp.dot(kept, token_spread(), preferred_element_type=jnp.float32)
 
 
 def rotate_rows(vectors, cosine, sine):
     return vectors * cosine + pltpu.roll(vectors, 64, 1) * sine
 
 
+def rotate_queries(q, scratch, table_ref):
+    scratch[...] = q.astype(jnp.float32)
+    return jnp.concatenate(
+        [
+            rotate_rows(
+                scratch[pl.ds(h, rows, stride=local_heads), :], table_ref[:, :128], table_ref[:, 128:]
+            )
+            for h in range(local_heads)
+        ],
+        axis=0,
+    ).astype(jnp.bfloat16)
+
+
 def attend(
-    half,
-    lengths_ref,
-    q_ref,
-    q_scratch,
-    cosine,
-    sine,
-    key_now,
-    value_now,
-    select_ref,
-    key_ref,
-    value_ref,
-    store,
+    half, length_ref, q_rot, key_now, value_now, select_ref, key_ref, value_ref, store
 ):
-    q_scratch[...] = q_ref[...].astype(jnp.float32)
-    by_head = [
-        rotate_rows(q_scratch[pl.ds(h, rows, stride=local_heads), :], cosine, sine)
-        for h in range(local_heads)
-    ]
-    q_rot = jnp.concatenate(by_head, axis=0).astype(jnp.bfloat16)
     spread = jnp.dot(q_rot, select_ref[...], preferred_element_type=jnp.float32)
     new_all = lax.dot_general(
         q_rot, key_now, nt, preferred_element_type=jnp.float32
@@ -143,11 +142,7 @@
         ).astype(jnp.bfloat16)
         cache = pl.ds(b * 128, 128)
         scores = lax.dot_general(left, key_ref[cache, :], nt, preferred_element_type=jnp.float32)
-        length_row = jnp.full((1, 128), lengths_ref[b * chunk], jnp.int32)
-        for i in range(1, chunk):
-            length_row = jnp.where(
-                iota((1, 128), 1) // 16 >= i, lengths_ref[b * chunk + i], length_row
-            )
+        length_row = length_ref[pl.ds(b, 1), :]
         live = position < length_row
         scores = jnp.where(live, scores, neg_floor)
         new_block = pick(new_all)
@@ -194,62 +189,141 @@
             store(b, h, result[part], logsum[part])
 
 
-def position_tables(lengths_ref, table_ref, table_scratch):
-    for r in range(rows):
-        table_scratch[pl.ds(r, 1), :] = table_ref[pl.ds(lengths_ref[r], 1), :]
-    return table_scratch[:, :128], table_scratch[:, 128:]
-
-
-def pick_head(array_ref, index):
-    wide = array_ref[...].astype(jnp.float32)
+def pick_head(array, index):
+    wide = array.astype(jnp.float32)
     return jnp.sum(jnp.where(iota(wide.shape, 1) == index, wide, 0.0), axis=1)
 
 
-def own_kernel(
-    lengths_ref,
-    q_ref,
-    new_key_ref,
-    new_value_ref,
-    key_codes_ref,
-    key_scales_ref,
-    value_codes_ref,
-    value_scales_ref,
-    key_table_ref,
-    query_table_ref,
-    select_ref,
-    swap_ref,
-    spread_ref,
+code_chunks = 8
+
+
+def prepare_kernel(
+    lengths_hbm,
+    queries_hbm,
+    new_key_hbm,
+    new_value_hbm,
+    key_codes_hbm,
+    key_scales_hbm,
+    value_codes_hbm,
+    value_scales_hbm,
+    key_table_hbm,
+    query_table_hbm,
+    out_codes_hbm,
+    out_scales_hbm,
     key_ref,
     value_ref,
     table_ref,
     now_ref,
-    own_ref,
-    own_log_ref,
+    query_ref,
+    length_ref,
+    select_ref,
+    hadamard_ref,
+    weight_ref,
+    lengths,
+    queries,
+    new_key,
+    new_value,
+    key_codes,
+    key_scales,
+    value_codes,
+    value_scales,
+    key_table,
+    query_table,
+    out_codes,
+    out_scales,
     q_scratch,
+    scale_scratch,
+    sems,
+    code_sems,
 ):
     rank = lax.axis_index("tensor")
     half = lax.rem(rank, 2)
     head = lax.div(rank, 2)
-    cosine, sine = position_tables(lengths_ref, query_table_ref, table_ref)
-    key_now = rotate_rows(pick_head(new_key_ref, head), cosine, sine).astype(jnp.bfloat16)
-    value_now = pick_head(new_value_ref, head).astype(jnp.bfloat16)
-    now_ref[0] = key_now
-    now_ref[1] = value_now
-    scales = spread_scales(key_scales_ref, spread_ref)
-    swap = swap_ref[...]
-    for j, plane in enumerate(unpack_planes(key_codes_ref[...])):
+    pairs = [
+        (key_codes_hbm, key_codes),
+        (key_scales_hbm, key_scales),
+        (key_table_hbm.at[half], key_table),
+        (value_codes_hbm, value_codes),
+        (value_scales_hbm, value_scales),
+        (lengths_hbm, lengths),
+        (query_table_hbm, query_table),
+        (new_key_hbm, new_key),
+        (new_value_hbm, new_value),
+        (queries_hbm, queries),
+        (out_scales_hbm, out_scales),
+    ]
+    copies = [
+        pltpu.make_async_copy(source, target, sems.at[i]) for i, (source, target) in enumerate(pairs)
+    ]
+    for copy in copies:
+        copy.start()
+    size = out_codes_hbm.shape[0] // code_chunks
+
+    def code_copy(i):
+        part = pl.ds(i * size, size)
+        return pltpu.make_async_copy(out_codes_hbm.at[part, :], out_codes.at[part, :], code_sems.at[i])
+
+    for i in range(code_chunks):
+        code_copy(i).start()
+    select_ref[...] = selector()
+    hadamard_ref[...] = hadamard_pair()
+    swap = swap_words()
+    for copy in copies[:3]:
+        copy.wait()
+    scales = spread_scales(key_scales[...])
+    for j, plane in enumerate(unpack_planes(key_codes[...])):
         partner = jnp.dot(plane.astype(jnp.bfloat16), swap, preferred_element_type=jnp.float32)
         lanes = slice(j * 128, (j + 1) * 128)
         shape = (rows, 16, 128)
         turned = (
-            plane.reshape(shape) * key_table_ref[half, 0, :, lanes][None]
-            + partner.reshape(shape) * key_table_ref[half, 1, :, lanes][None]
+            plane.reshape(shape) * key_table[0, :, lanes][None]
+            + partner.reshape(shape) * key_table[1, :, lanes][None]
         ).reshape(512, 128)
         key_ref[:, lanes] = (turned * scales).astype(jnp.bfloat16)
-    scales = spread_scales(value_scales_ref, spread_ref) * np.float32(1.0 / cache_step)
-    for j, plane in enumerate(unpack_planes(value_codes_ref[...])):
+    for copy in copies[3:5]:
+        copy.wait()
+    scales = spread_scales(value_scales[...]) * np.float32(1.0 / cache_step)
+    for j, plane in enumerate(unpack_planes(value_codes[...])):
         value_ref[:, j * 128 : (j + 1) * 128] = (plane * scales).astype(jnp.bfloat16)
-
+    for copy in copies[5:]:
+        copy.wait()
+    for r in range(rows):
+        table_ref[pl.ds(r, 1), :] = query_table[pl.ds(lengths[r], 1), :]
+    cosine, sine = table_ref[:, :128], table_ref[:, 128:]
+    now_ref[0] = rotate_rows(pick_head(new_key[...], head), cosine, sine).astype(jnp.bfloat16)
+    now_ref[1] = pick_head(new_value[...], head).astype(jnp.bfloat16)
+    query_ref[...] = rotate_queries(queries[...], q_scratch, table_ref)
+    lane_row = iota((1, 128), 1) // 16
+    for b in range(rows // chunk):
+        line = jnp.full((1, 128), lengths[b * chunk], jnp.int32)
+        for i in range(1, chunk):
+            line = jnp.where(lane_row >= i, lengths[b * chunk + i], line)
+        length_ref[pl.ds(b, 1), :] = line
+    scale_scratch[...] = out_scales[...].astype(jnp.float32) * np.float32(1.0 / weight_step)
+
+    @pl.loop(0, code_chunks)
+    def _(i):
+        code_copy(i).wait()
+        for b in range(size // 32):
+            words = out_codes[pl.ds(i * size + b * 32, 32), :]
+            group = i * (size // 32) + b
+            scale = jnp.broadcast_to(scale_scratch[pl.ds(group, 1), :], (16, 512)).astype(jnp.bfloat16)
+            for k in range(4):
+                power = 16.0**k
+                plane = (
+                    jnp.bitwise_and(words, 15 << 4 * k).astype(jnp.float32).astype(jnp.bfloat16)
+                    - jnp.bfloat16(code_offset * power)
+                )
+                scaled = scale * jnp.bfloat16(1.0 / power)
+                for part in range(2):
+                    start = i * size * 4 + (b // 2) * 256 + k * 64 + (b % 2) * 32 + part * 16
+                    weight_ref[pl.ds(start, 16), :] = plane[part * 16 : (part + 1) * 16] * scaled
+
+
+def own_kernel(
+    q_ref, now_ref, length_ref, select_ref, key_ref, value_ref, own_ref, own_log_ref
+):
+    half = lax.rem(lax.axis_index("tensor"), 2)
     lane_head = iota((chunk, 128), 1) // 32
 
     def store(b, h, result, logsum):
@@ -261,22 +335,12 @@
         )
 
     attend(
-        half, lengths_ref, q_ref, q_scratch, cosine, sine, key_now, value_now,
-        select_ref, key_ref, value_ref, store,
+        half, length_ref, q_ref[...], now_ref[0], now_ref[1], select_ref, key_ref, value_ref, store
     )
 
 
 def partner_kernel(
-    lengths_ref,
-    q_ref,
-    table_ref,
-    now_ref,
-    key_ref,
-    value_ref,
-    select_ref,
-    out_ref,
-    q_scratch,
-    out_scratch,
+    q_ref, table_ref, now_ref, length_ref, select_ref, key_ref, value_ref, out_ref, q_scratch, out_scratch
 ):
     half = lax.rem(lax.axis_index("tensor"), 2)
     lane = iota((chunk, 128), 1)
@@ -299,8 +363,15 @@
         )
 
     attend(
-        half, lengths_ref, q_ref, q_scratch, table_ref[:, :128], table_ref[:, 128:],
-        now_ref[0], now_ref[1], select_ref, key_ref, value_ref, store,
+        half,
+        length_ref,
+        rotate_queries(q_ref[...], q_scratch, table_ref),
+        now_ref[0],
+        now_ref[1],
+        select_ref,
+        key_ref,
+        value_ref,
+        store,
     )
     out_ref[...] = out_scratch[...].astype(jnp.bfloat16)
 
@@ -320,22 +391,6 @@
             own_ref[:, lanes] * (mine_factor * scale)
             + other_ref[:, lanes].astype(jnp.float32) * (their_factor * scale)
         ).astype(jnp.bfloat16)
-
-
-def weight_kernel(codes_ref, scales_ref, out_ref):
-    for b in range(codes_ref.shape[0] // 64):
-        words = codes_ref[b * 64 : (b + 1) * 64, :]
-        first = pl.program_id(0) * (codes_ref.shape[0] // 32) + 2 * b
-        scale = [
-            (scales_ref[pl.ds(first + n, 1), :].astype(jnp.float32) / weight_step) for n in range(2)
-        ]
-        for k in range(4):
-            plane = (
-                jnp.bitwise_and(jnp.right_shift(words, 4 * k), 15).astype(jnp.float32) - code_offset
-            )
-            out_ref[b * 256 + k * 64 : b * 256 + (k + 1) * 64, :] = jnp.concatenate(
-                [plane[:32] * scale[0], plane[32:] * scale[1]], axis=0
-            ).astype(jnp.bfloat16)
 
 
 def project_kernel(gathered_ref, hadamard_ref, weight_ref, out_ref):
@@ -363,8 +418,8 @@
 
 
 vmem = pl.BlockSpec(memory_space=pltpu.VMEM)
-smem = pl.BlockSpec(memory_space=pltpu.SMEM)
-params = pltpu.CompilerParams(vmem_limit_bytes=40 * 1024 * 1024)
+hbm = pl.BlockSpec(memory_space=pltpu.HBM)
+params = pltpu.CompilerParams(vmem_limit_bytes=20 * 1024 * 1024)
 
 
 def per_device(
@@ -380,66 +435,84 @@
     out_scales,
 ):
     pairs = [(i, i ^ 1) for i in range(16)]
-    f32, bf16 = jnp.float32, jnp.bfloat16
+    f32, bf16, i32 = jnp.float32, jnp.bfloat16, jnp.int32
     shape = jax.ShapeDtypeStruct
     other_queries = lax.ppermute(queries, "tensor", pairs)
-    select = jnp.asarray(selector(), bf16)
-    keys, values, table, now, own, own_log = pl.pallas_call(
-        own_kernel,
+    keys, values, table, now, query, length, select, hadamard, weight = pl.pallas_call(
+        prepare_kernel,
         out_shape=(
             shape((512, 512), bf16),
             shape((512, 512), bf16),
             shape((rows, 256), f32),
             shape((2, rows, 128), bf16),
-            shape((rows, 512), f32),
-            shape((rows, 128), f32),
+            shape((128, 128), bf16),
+            shape((8, 128), i32),
+            shape((128, 512), bf16),
+            shape((256, 256), bf16),
+            shape((8192, 512), bf16),
         ),
-        in_specs=[smem] + [vmem] * 12,
-        out_specs=(vmem,) * 6,
-        scratch_shapes=[pltpu.VMEM((128, 128), f32)],
+        in_specs=[hbm] * 12,
+        out_specs=(vmem,) * 9,
+        scratch_shapes=[
+            pltpu.SMEM((rows,), i32),
+            pltpu.VMEM((128, 128), bf16),
+            pltpu.VMEM((rows, 8, 128), bf16),
+            pltpu.VMEM((rows, 8, 128), bf16),
+            pltpu.VMEM((512, 128), i32),
+            pltpu.VMEM((rows, half_tokens), i32),
+            pltpu.VMEM((512, 128), i32),
+            pltpu.VMEM((rows, half_tokens), i32),
+            pltpu.VMEM((2, 16, 512), f32),
+            pltpu.VMEM((136, 256), f32),
+            pltpu.VMEM((2048, 512), i32),
+            pltpu.VMEM((64, 512), i32),
+            pltpu.VMEM((128, 128), f32),
+            pltpu.VMEM((64, 512), f32),
+            pltpu.SemaphoreType.DMA((11,)),
+            pltpu.SemaphoreType.DMA((code_chunks,)),
+        ],
         compiler_params=params,
-        cost_estimate=pl.CostEstimate(flops=400_000_000, bytes_accessed=2_000_000, transcendentals=65536),
-        name="own_heads",
+        cost_estimate=pl.CostEstimate(flops=100_000_000, bytes_accessed=14_000_000, transcendentals=0),
+        name="prepare",
     )(
-        lengths,
-        queries.reshape(128, 128),
-        new_key,
-        new_value,
-        key_codes.reshape(512, 128),
-        key_scales.reshape(rows, half_tokens),
-        value_codes.reshape(512, 128),
-        value_scales.reshape(rows, half_tokens),
-        jnp.asarray(key_tables()),
-        jnp.asarray(query_table()),
-        select,
-        jnp.asarray(swap_words(), bf16),
-        jnp.asarray(token_spread(), bf16),
+        *[
+            pltpu.with_memory_space_constraint(array, pltpu.HBM)
+            for array in (
+                lengths,
+                queries.reshape(128, 128),
+                new_key,
+                new_value,
+                key_codes.reshape(512, 128),
+                key_scales.reshape(rows, half_tokens),
+                value_codes.reshape(512, 128),
+                value_scales.reshape(rows, half_tokens),
+                jnp.asarray(key_tables()),
+                jnp.asarray(query_table()),
+                out_codes,
+                out_scales,
+            )
+        ]
     )
     sending = pl.pallas_call(
         partner_kernel,
         out_shape=shape((rows, 640), bf16),
-        in_specs=[smem] + [vmem] * 6,
+        in_specs=[vmem] * 7,
         out_specs=vmem,
         scratch_shapes=[pltpu.VMEM((128, 128), f32), pltpu.VMEM((rows, 640), f32)],
         compiler_params=params,
         name="other_heads",
-    )(lengths, other_queries.reshape(128, 128), table, now, keys, values, select)
+    )(other_queries.reshape(128, 128), table, now, length, select, keys, values)
     received = lax.ppermute(sending, "tensor", pairs)
-    out_codes, _ = lax.optimization_barrier((out_codes, sending))
-    steps = 8
-    weight = pl.pallas_call(
-        weight_kernel,
-        grid=(steps,),
-        out_shape=shape((8192, 512), bf16),
-        in_specs=[
-            pl.BlockSpec((2048 // steps, 512), lambda i: (i, 0)),
-            pl.BlockSpec((64, 512), lambda i: (0, 0)),
-        ],
-        out_specs=pl.BlockSpec((8192 // steps, 512), lambda i: (i, 0)),
+    query, _ = lax.optimization_barrier((query, sending))
+    own, own_log = pl.pallas_call(
+        own_kernel,
+        out_shape=(shape((rows, 512), f32), shape((rows, 128), f32)),
+        in_specs=[vmem] * 6,
+        out_specs=(vmem,) * 2,
         compiler_params=params,
-        cost_estimate=pl.CostEstimate(flops=20_000_000, bytes_accessed=12_000_000, transcendentals=0),
-        name="unpack_weight",
-    )(out_codes, out_scales)
+        cost_estimate=pl.CostEstimate(flops=300_000_000, bytes_accessed=2_000_000, transcendentals=65536),
+        name="own_heads",
+    )(query, now, length, select, keys, values)
     attended = pl.pallas_call(
         combine_kernel,
         out_shape=shape((rows, 512), bf16),
@@ -456,7 +529,7 @@
         out_specs=vmem,
         compiler_params=params,
         name="project",
-    )(gathered, jnp.asarray(hadamard_pair(), bf16), weight)
+    )(gathered, hadamard, weight)
 
 
 def solution(mesh):

time: 70.5 us -> 57.3 us (0.81)
  local copies, waits for them, and re-layouts: 13.7 us -> 0 us
  waiting for transfers between devices: 0.03 us -> 1.85 us
  blocking collectives: 38.2 us -> 37.3 us
    unnamed x32 -> x0, local copies, waits for them, and re-layouts: 13.7 us -> none
    ppermute x1, waiting for transfers between devices: 0.01 us -> 1.85 us  [per_device(): received = lax.ppermute(sending, 'tensor', pairs)]
    pallas_call x2, Pallas kernels: 6.31 us -> 7.26 us  [the longest x1 5.23 us: per_device(): pl.pallas_call(prepare_kernel, out_shape=(shape((512, 512), bf16), shape(...]
    all_gather x1, blocking collectives: 38.2 us -> 37.3 us  [per_device(): gathered = lax.all_gather(attended, 'tensor', axis=0, tiled=True)]
  transfers between devices with their start and end apart: 2 -> 2, of which waited for: 0 -> 1; matrix products, arithmetic and copies ran while one was open for 0% -> 0% of each run, Pallas kernels for 9% -> 13%
where the time goes in v2:
time: 57.3 us; the launch traced here: 57.2 us
  blocking collectives  37.3 us (65%)
  Pallas kernels  12.1 us (21%)
  starting transfers between devices  5.83 us (10%)
  waiting for transfers between devices  1.85 us (3%)
    all_gather x1, blocking collectives, per_device(): gathered = lax.all_gather(attended, 'tensor', axis=0, tiled=True)  37.3 us
    pallas_call x1, Pallas kernels, per_device(): pl.pallas_call(prepare_kernel, out_shape=(shape((512, 512), bf16), shape(...  5.23 us
    ppermute x1, starting transfers between devices, per_device(): other_queries = lax.ppermute(queries, 'tensor', pairs)  3.81 us
    pallas_call x1, Pallas kernels, per_device(): pl.pallas_call(project_kernel, out_shape=shape((rows, 512), bf16), in_spe...  2.54 us
    pallas_call x1, Pallas kernels, per_device(): pl.pallas_call(partner_kernel, out_shape=shape((rows, 640), bf16), in_spe...  2.11 us
    pallas_call x1, Pallas kernels, per_device(): pl.pallas_call(own_kernel, out_shape=(shape((rows, 512), f32), shape((row...  2.02 us
    ppermute x1, starting transfers between devices, per_device(): received = lax.ppermute(sending, 'tensor', pairs)  2.02 us
    ppermute x1, waiting for transfers between devices, per_device(): received = lax.ppermute(sending, 'tensor', pairs)  1.85 us
  transfers between devices with their start and end apart: 2, of which 1 were waited for; matrix products, arithmetic and copies ran while one was open for 0% of the time, Pallas kernels for 13%

profile of v2, /device:TPU:24, one launch (start us, length us, event | category | flops | bytes accessed | tf_op | source)
XLA Modules:
  0.0 57.2 jit_solution(2904319016626114510)
XLA Ops:
  0.0 3.8 %collective-permute-start = (bf16[32,4,128]{2,1,0:T(4,128)(2,1)}, bf16[32,4,128]{2,1,0:T(4,128)(2,1)S(1)}, u32[]{:S(2)}, u32[]{:S(2)}) collective-permute-start(bf16[32,4,128]{2,1,0:T(4,128)(2,1)} %param.12), channel_id=1, source_target_pairs={{0,1},{1,0},{2,3},{3,2},{4,5},{5,4},{6,7},{7,6},{8,9},{9,8},{10,11... | collective-permute-start | bytes 98312 | tf_op jit(solution)/shard_map/ppermute | solution.py:440
  3.8 5.2 %prepare.1 = (bf16[512,512]{1,0:T(8,128)(2,1)S(1)}, bf16[512,512]{1,0:T(8,128)(2,1)S(1)}, f32[32,256]{1,0:T(8,128)S(1)}, bf16[2,32,128]{2,1,0:T(8,128)(2,1)S(1)}...) custom-call(s32[32]{0:T(128)} %lengths_hbm.1, ...), custom_call_target="tpu_custom_call" | custom-call | flops 100000000 | bytes 14000000 | tf_op jit(solution)/shard_map/prepare/pallas_call | solution.py:441
  9.1 0.0 collective-permute-done
  9.1 2.1 %other_heads.1 = bf16[32,640]{1,0:T(8,128)(2,1)S(1)} custom-call(bf16[128,128]{1,0:T(8,128)(2,1)S(1)} %bitcast.6, f32[32,256]{1,0:T(8,128)S(1)} %get-tuple-element.18.table_ref, bf16[2,32,128]{2,1,0:T(8,128)(2,1)S(1)} %get-tuple-element.19.now_ref, s32[8,128]{1,0:T(8,128)S(1)} %get-tuple-element.20.length_ref, ...), custom_call_target="tpu_custom_call" | custom-call | tf_op jit(solution)/shard_map/other_heads/pallas_call | solution.py:496
  11.2 2.0 %collective-permute-start.1 = (bf16[32,640]{1,0:T(8,128)(2,1)S(1)}, bf16[32,640]{1,0:T(8,128)(2,1)S(1)}, u32[]{:S(2)}, u32[]{:S(2)}) collective-permute-start(bf16[32,640]{1,0:T(8,128)(2,1)S(1)} %other_heads.1), channel_id=1, source_target_pairs={{0,1},{1,0},{2,3},{3,2},{4,5},{5,4},{6,7},{7,6},{8,9},{9,8},{10,11... | collective-permute-start | bytes 122888 | tf_op jit(solution)/shard_map/ppermute | solution.py:505
  13.2 2.0 %own_heads.1 = (f32[32,512]{1,0:T(8,128)S(1)}, f32[32,128]{1,0:T(8,128)S(1)}) custom-call(bf16[128,128]{1,0:T(8,128)(2,1)S(1)} %get-tuple-element.24.q_ref, bf16[2,32,128]{2,1,0:T(8,128)(2,1)S(1)} %get-tuple-element.19.now_ref, s32[8,128]{1,0:T(8,128)S(1)} %get-tuple-element.20.length_ref, bf16[128,512]{1,0:T(8,128)(2,1)S(1)} %get-tuple-element.21.select_ref, ...), custom_call_target="tpu_custom_call" | custom-call | flops 300000000 | bytes 2000000 | tf_op jit(solution)/shard_map/own_heads/pallas_call | solution.py:507
  15.2 1.8 %collective-permute-done.1.other_ref = bf16[32,640]{1,0:T(8,128)(2,1)S(1)} collective-permute-done((bf16[32,640]{1,0:T(8,128)(2,1)S(1)}, bf16[32,640]{1,0:T(8,128)(2,1)S(1)}, u32[]{:S(2)}, u32[]{:S(2)}) %collective-permute-start.1) | collective-permute-done | bytes 40992 | tf_op jit(solution)/shard_map/ppermute | solution.py:505
  17.1 0.2 combine_halves.1
  17.3 37.3 %all_gather.3.gathered_ref = bf16[512,512]{1,0:T(8,128)(2,1)S(1)} all-gather(bf16[32,512]{1,0:T(8,128)(2,1)S(1)} %combine_halves.1), channel_id=1, replica_groups=mesh['dp'=32,'tensor'=16] {'tensor'}, dimensions={0}, use_global_device_ids=true | all-gather | bytes 557056 | tf_op jit(solution)/shard_map/all_gather | solution.py:524
  54.6 2.5 %project.1 = bf16[32,512]{1,0:T(8,128)(2,1)} custom-call(bf16[512,512]{1,0:T(8,128)(2,1)S(1)} %all_gather.3.gathered_ref, bf16[256,256]{1,0:T(8,128)(2,1)S(1)} %get-tuple-element.27.hadamard_ref, bf16[8192,512]{1,0:T(8,128)(2,1)S(1)} %get-tuple-element.28.weight_ref), custom_call_target="tpu_custom_call" | custom-call | tf_op jit(solution)/shard_map/project/pallas_call | solution.py:525
Async XLA Ops:
  0.0 9.1 %collective-permute-start = (bf16[32,4,128]{2,1,0:T(4,128)(2,1)}, bf16[32,4,128]{2,1,0:T(4,128)(2,1)S(1)}, u32[]{:S(2)}, u32[]{:S(2)}) collective-permute-start(bf16[32,4,128]{2,1,0:T(4,128)(2,1)} %param.12), channel_id=1, source_target_pairs={{0,1},{1,0},{2,3},{3,2},{4,5},{5,4},{6,7},{7,6},{8,9},{9,8},{10,11... | collective-permute-start | bytes 98312 | tf_op jit(solution)/shard_map/ppermute | solution.py:440
  11.2 5.9 %collective-permute-start.1 = (bf16[32,640]{1,0:T(8,128)(2,1)S(1)}, bf16[32,640]{1,0:T(8,128)(2,1)S(1)}, u32[]{:S(2)}, u32[]{:S(2)}) collective-permute-start(bf16[32,640]{1,0:T(8,128)(2,1)S(1)} %other_heads.1), channel_id=1, source_target_pairs={{0,1},{1,0},{2,3},{3,2},{4,5},{5,4},{6,7},{7,6},{8,9},{9,8},{10,11... | collective-permute-start | bytes 122888 | tf_op jit(solution)/shard_map/ppermute | solution.py:505

commit v3 on v2

--- a/solution.py
+++ b/solution.py
@@ -197,7 +197,33 @@
 code_chunks = 8
 
 
-def prepare_kernel(
+def stats_of(logsum):
+    which = iota((chunk, 128), 1) % 32
+    whole = jnp.broadcast_to(logsum, (chunk, 128))
+    first = whole.astype(jnp.bfloat16).astype(jnp.float32)
+    second = (whole - first).astype(jnp.bfloat16).astype(jnp.float32)
+    third = whole - first - second
+    return jnp.where(
+        which == 0, first, jnp.where(which == 1, second, jnp.where(which == 2, third, 0.0))
+    )
+
+
+def storing(target):
+    lane_head = iota((chunk, 128), 1) // 32
+    tail = slice(512, 640)
+
+    def store(b, h, result, logsum):
+        block = pl.ds(b * chunk, chunk)
+        target[block, h * 128 : (h + 1) * 128] = result
+        pieces = stats_of(logsum)
+        target[block, tail] = (
+            pieces if h == 0 else jnp.where(lane_head == h, pieces, target[block, tail])
+        )
+
+    return store
+
+
+def own_kernel(
     lengths_hbm,
     queries_hbm,
     new_key_hbm,
@@ -208,17 +234,14 @@
     value_scales_hbm,
     key_table_hbm,
     query_table_hbm,
-    out_codes_hbm,
-    out_scales_hbm,
     key_ref,
     value_ref,
     table_ref,
     now_ref,
-    query_ref,
     length_ref,
     select_ref,
     hadamard_ref,
-    weight_ref,
+    own_ref,
     lengths,
     queries,
     new_key,
@@ -229,12 +252,8 @@
     value_scales,
     key_table,
     query_table,
-    out_codes,
-    out_scales,
     q_scratch,
-    scale_scratch,
     sems,
-    code_sems,
 ):
     rank = lax.axis_index("tensor")
     half = lax.rem(rank, 2)
@@ -250,21 +269,12 @@
         (new_key_hbm, new_key),
         (new_value_hbm, new_value),
         (queries_hbm, queries),
-        (out_scales_hbm, out_scales),
     ]
     copies = [
         pltpu.make_async_copy(source, target, sems.at[i]) for i, (source, target) in enumerate(pairs)
     ]
     for copy in copies:
         copy.start()
-    size = out_codes_hbm.shape[0] // code_chunks
-
-    def code_copy(i):
-        part = pl.ds(i * size, size)
-        return pltpu.make_async_copy(out_codes_hbm.at[part, :], out_codes.at[part, :], code_sems.at[i])
-
-    for i in range(code_chunks):
-        code_copy(i).start()
     select_ref[...] = selector()
     hadamard_ref[...] = hadamard_pair()
     swap = swap_words()
@@ -290,22 +300,103 @@
     for r in range(rows):
         table_ref[pl.ds(r, 1), :] = query_table[pl.ds(lengths[r], 1), :]
     cosine, sine = table_ref[:, :128], table_ref[:, 128:]
-    now_ref[0] = rotate_rows(pick_head(new_key[...], head), cosine, sine).astype(jnp.bfloat16)
-    now_ref[1] = pick_head(new_value[...], head).astype(jnp.bfloat16)
-    query_ref[...] = rotate_queries(queries[...], q_scratch, table_ref)
+    key_now = rotate_rows(pick_head(new_key[...], head), cosine, sine).astype(jnp.bfloat16)
+    value_now = pick_head(new_value[...], head).astype(jnp.bfloat16)
+    now_ref[0] = key_now
+    now_ref[1] = value_now
     lane_row = iota((1, 128), 1) // 16
     for b in range(rows // chunk):
         line = jnp.full((1, 128), lengths[b * chunk], jnp.int32)
         for i in range(1, chunk):
             line = jnp.where(lane_row >= i, lengths[b * chunk + i], line)
         length_ref[pl.ds(b, 1), :] = line
-    scale_scratch[...] = out_scales[...].astype(jnp.float32) * np.float32(1.0 / weight_step)
+    attend(
+        half,
+        length_ref,
+        rotate_queries(queries[...], q_scratch, table_ref),
+        key_now,
+        value_now,
+        select_ref,
+        key_ref,
+        value_ref,
+        storing(own_ref),
+    )
+
+
+def partner_kernel(
+    q_ref,
+    table_ref,
+    now_ref,
+    length_ref,
+    select_ref,
+    key_ref,
+    value_ref,
+    own_ref,
+    out_ref,
+    q_scratch,
+    out_scratch,
+):
+    attend(
+        lax.rem(lax.axis_index("tensor"), 2),
+        length_ref,
+        rotate_queries(q_ref[...], q_scratch, table_ref),
+        now_ref[0],
+        now_ref[1],
+        select_ref,
+        key_ref,
+        value_ref,
+        storing(out_scratch),
+    )
+    out_ref[:, :640] = own_ref[...].astype(jnp.bfloat16)
+    out_ref[:, 640:] = out_scratch[...].astype(jnp.bfloat16)
+
+
+def combine_kernel(mine_ref, theirs_ref, out_ref, scratch):
+    half = lax.rem(lax.axis_index("tensor"), 2)
+    lane_head = iota((rows, 128), 1) // 32
+    for own in range(2):
+        at, other = own * 640, 640 - own * 640
+        logs = [mine_ref[:, at + 512 : at + 640], theirs_ref[:, other + 512 : other + 640]]
+        logs = [log.astype(jnp.float32) for log in logs]
+        for h in range(local_heads):
+            mine, theirs = [
+                jnp.sum(jnp.where(lane_head == h, log, 0.0), axis=1, keepdims=True) for log in logs
+            ]
+            joint = jnp.maximum(mine, theirs)
+            mine_factor = jnp.exp(mine - joint)
+            their_factor = jnp.exp(theirs - joint)
+            scale = 1.0 / (mine_factor + their_factor)
+            block = mine_ref[:, at + h * 128 : at + (h + 1) * 128].astype(jnp.float32)
+            other_block = theirs_ref[:, other + h * 128 : other + (h + 1) * 128].astype(jnp.float32)
+            scratch[own, :, h * 128 : (h + 1) * 128] = block * (
+                mine_factor * scale
+            ) + other_block * (their_factor * scale)
+    first = scratch[half].astype(jnp.bfloat16)
+    second = scratch[1 - half].astype(jnp.bfloat16)
+    for k in range(out_ref.shape[0]):
+        out_ref[k, :, :512] = first
+        out_ref[k, :, 512:] = second
+
+
+def weight_kernel(codes_hbm, scales_hbm, weight_ref, codes, scales, scale_scratch, sem, code_sems):
+    size = codes_hbm.shape[0] // code_chunks
+
+    def code_copy(i):
+        part = pl.ds(i * size, size)
+        return pltpu.make_async_copy(codes_hbm.at[part, :], codes.at[part, :], code_sems.at[i])
+
+    scale_copy = pltpu.make_async_copy(scales_hbm, scales, sem)
+    scale_copy.start()
+    for i in range(code_chunks):
+        code_copy(i).start()
+    scale_copy.wait()
+    scale_scratch[...] = scales[...].astype(jnp.float32) * np.float32(1.0 / weight_step)
 
     @pl.loop(0, code_chunks)
     def _(i):
         code_copy(i).wait()
         for b in range(size // 32):
-            words = out_codes[pl.ds(i * size + b * 32, 32), :]
+            words = codes[pl.ds(i * size + b * 32, 32), :]
             group = i * (size // 32) + b
             scale = jnp.broadcast_to(scale_scratch[pl.ds(group, 1), :], (16, 512)).astype(jnp.bfloat16)
             for k in range(4):
@@ -320,106 +411,40 @@
                     weight_ref[pl.ds(start, 16), :] = plane[part * 16 : (part + 1) * 16] * scaled
 
 
-def own_kernel(
-    q_ref, now_ref, length_ref, select_ref, key_ref, value_ref, own_ref, own_log_ref
-):
-    half = lax.rem(lax.axis_index("tensor"), 2)
-    lane_head = iota((chunk, 128), 1) // 32
-
-    def store(b, h, result, logsum):
-        block = pl.ds(b * chunk, chunk)
-        own_ref[block, h * 128 : (h + 1) * 128] = result
-        spread_log = jnp.broadcast_to(logsum, (chunk, 128))
-        own_log_ref[block, :] = (
-            spread_log if h == 0 else jnp.where(lane_head == h, spread_log, own_log_ref[block, :])
-        )
-
-    attend(
-        half, length_ref, q_ref[...], now_ref[0], now_ref[1], select_ref, key_ref, value_ref, store
-    )
-
-
-def partner_kernel(
-    q_ref, table_ref, now_ref, length_ref, select_ref, key_ref, value_ref, out_ref, q_scratch, out_scratch
-):
-    half = lax.rem(lax.axis_index("tensor"), 2)
-    lane = iota((chunk, 128), 1)
-    lane_head = lane // 32
-
-    def store(b, h, result, logsum):
-        block = pl.ds(b * chunk, chunk)
-        out_scratch[block, h * 128 : (h + 1) * 128] = result
-        whole = jnp.broadcast_to(logsum, (chunk, 128))
-        first = whole.astype(jnp.bfloat16).astype(jnp.float32)
-        second = (whole - first).astype(jnp.bfloat16).astype(jnp.float32)
-        third = whole - first - second
-        which = lane % 32
-        pieces = jnp.where(
-            which == 0, first, jnp.where(which == 1, second, jnp.where(which == 2, third, 0.0))
-        )
-        tail = slice(512, 640)
-        out_scratch[block, tail] = (
-            pieces if h == 0 else jnp.where(lane_head == h, pieces, out_scratch[block, tail])
-        )
-
-    attend(
-        half,
-        length_ref,
-        rotate_queries(q_ref[...], q_scratch, table_ref),
-        now_ref[0],
-        now_ref[1],
-        select_ref,
-        key_ref,
-        value_ref,
-        store,
-    )
-    out_ref[...] = out_scratch[...].astype(jnp.bfloat16)
-
-
-def combine_kernel(own_ref, own_log_ref, other_ref, out_ref):
-    lane_head = iota((rows, 128), 1) // 32
-    other_log = other_ref[:, 512:640].astype(jnp.float32)
-    for h in range(local_heads):
-        lanes = slice(h * 128, (h + 1) * 128)
-        theirs = jnp.sum(jnp.where(lane_head == h, other_log, 0.0), axis=1, keepdims=True)
-        mine = own_log_ref[:, h * 32 : h * 32 + 1]
-        joint = jnp.maximum(mine, theirs)
-        mine_factor = jnp.exp(mine - joint)
-        their_factor = jnp.exp(theirs - joint)
-        scale = 1.0 / (mine_factor + their_factor)
-        out_ref[:, lanes] = (
-            own_ref[:, lanes] * (mine_factor * scale)
-            + other_ref[:, lanes].astype(jnp.float32) * (their_factor * scale)
-        ).astype(jnp.bfloat16)
-
-
 def project_kernel(gathered_ref, hadamard_ref, weight_ref, out_ref):
     hadamard = hadamard_ref[...]
-    left = jnp.dot(gathered_ref[:, :256], hadamard, preferred_element_type=jnp.float32)
-    right = jnp.dot(gathered_ref[:, 256:], hadamard, preferred_element_type=jnp.float32)
     factor = np.float32(8192.0**-0.5)
+    turned = [
+        jnp.dot(
+            gathered_ref[:, q * 256 : (q + 1) * 256], hadamard, preferred_element_type=jnp.float32
+        )
+        for q in range(4)
+    ]
+    start = [((i // 4) % 2 * 4 + i // 8) * rows for i in range(32)]
+    blocks = [turned[i % 4][start[i] : start[i] + rows] for i in range(32)]
+    for bit in range(5):
+        step = 1 << bit
+        blocks = [
+            blocks[i] + blocks[i ^ step] if i & step == 0 else blocks[i ^ step] - blocks[i]
+            for i in range(32)
+        ]
     total = jnp.zeros((rows, 512), jnp.float32)
-    for p, mixed in enumerate((left + right, left - right)):
-        blocks = [mixed[z * rows : (z + 1) * rows] for z in range(16)]
-        for bit in range(4):
-            step = 1 << bit
-            blocks = [
-                blocks[z] + blocks[z ^ step] if z & step == 0 else blocks[z ^ step] - blocks[z]
-                for z in range(16)
-            ]
-        for z in range(16):
-            start = (2 * z + p) * 256
-            total = total + jnp.dot(
-                (blocks[z] * factor).astype(jnp.bfloat16),
-                weight_ref[start : start + 256, :],
-                preferred_element_type=jnp.float32,
-            )
+    for i in range(32):
+        total = total + jnp.dot(
+            (blocks[i] * factor).astype(jnp.bfloat16),
+            weight_ref[i * 256 : (i + 1) * 256, :],
+            preferred_element_type=jnp.float32,
+        )
     out_ref[...] = total.astype(jnp.bfloat16)
 
 
 vmem = pl.BlockSpec(memory_space=pltpu.VMEM)
 hbm = pl.BlockSpec(memory_space=pltpu.HBM)
 params = pltpu.CompilerParams(vmem_limit_bytes=20 * 1024 * 1024)
+
+
+def in_hbm(*arrays):
+    return [pltpu.with_memory_space_constraint(array, pltpu.HBM) for array in arrays]
 
 
 def per_device(
@@ -438,21 +463,20 @@
     f32, bf16, i32 = jnp.float32, jnp.bfloat16, jnp.int32
     shape = jax.ShapeDtypeStruct
     other_queries = lax.ppermute(queries, "tensor", pairs)
-    keys, values, table, now, query, length, select, hadamard, weight = pl.pallas_call(
-        prepare_kernel,
+    keys, values, table, now, length, select, hadamard, own = pl.pallas_call(
+        own_kernel,
         out_shape=(
             shape((512, 512), bf16),
             shape((512, 512), bf16),
             shape((rows, 256), f32),
             shape((2, rows, 128), bf16),
-            shape((128, 128), bf16),
             shape((8, 128), i32),
             shape((128, 512), bf16),
             shape((256, 256), bf16),
-            shape((8192, 512), bf16),
+            shape((rows, 640), f32),
         ),
-        in_specs=[hbm] * 12,
-        out_specs=(vmem,) * 9,
+        in_specs=[hbm] * 10,
+        out_specs=(vmem,) * 8,
         scratch_shapes=[
             pltpu.SMEM((rows,), i32),
             pltpu.VMEM((128, 128), bf16),
@@ -464,64 +488,69 @@
             pltpu.VMEM((rows, half_tokens), i32),
             pltpu.VMEM((2, 16, 512), f32),
             pltpu.VMEM((136, 256), f32),
-            pltpu.VMEM((2048, 512), i32),
-            pltpu.VMEM((64, 512), i32),
             pltpu.VMEM((128, 128), f32),
-            pltpu.VMEM((64, 512), f32),
-            pltpu.SemaphoreType.DMA((11,)),
-            pltpu.SemaphoreType.DMA((code_chunks,)),
+            pltpu.SemaphoreType.DMA((10,)),
         ],
         compiler_params=params,
-        cost_estimate=pl.CostEstimate(flops=100_000_000, bytes_accessed=14_000_000, transcendentals=0),
-        name="prepare",
+        cost_estimate=pl.CostEstimate(flops=400_000_000, bytes_accessed=14_000_000, transcendentals=0),
+        name="own_heads",
     )(
-        *[
-            pltpu.with_memory_space_constraint(array, pltpu.HBM)
-            for array in (
-                lengths,
-                queries.reshape(128, 128),
-                new_key,
-                new_value,
-                key_codes.reshape(512, 128),
-                key_scales.reshape(rows, half_tokens),
-                value_codes.reshape(512, 128),
-                value_scales.reshape(rows, half_tokens),
-                jnp.asarray(key_tables()),
-                jnp.asarray(query_table()),
-                out_codes,
-                out_scales,
-            )
-        ]
+        *in_hbm(
+            lengths,
+            queries.reshape(128, 128),
+            new_key,
+            new_value,
+            key_codes.reshape(512, 128),
+            key_scales.reshape(rows, half_tokens),
+            value_codes.reshape(512, 128),
+            value_scales.reshape(rows, half_tokens),
+            jnp.asarray(key_tables()),
+            jnp.asarray(query_table()),
+        )
     )
     sending = pl.pallas_call(
         partner_kernel,
-        out_shape=shape((rows, 640), bf16),
-        in_specs=[vmem] * 7,
+        out_shape=shape((rows, 1280), bf16),
+        in_specs=[vmem] * 8,
         out_specs=vmem,
         scratch_shapes=[pltpu.VMEM((128, 128), f32), pltpu.VMEM((rows, 640), f32)],
         compiler_params=params,
         name="other_heads",
-    )(other_queries.reshape(128, 128), table, now, length, select, keys, values)
+    )(other_queries.reshape(128, 128), table, now, length, select, keys, values, own)
     received = lax.ppermute(sending, "tensor", pairs)
-    query, _ = lax.optimization_barrier((query, sending))
-    own, own_log = pl.pallas_call(
-        own_kernel,
-        out_shape=(shape((rows, 512), f32), shape((rows, 128), f32)),
-        in_specs=[vmem] * 6,
-        out_specs=(vmem,) * 2,
+    out_scales, _ = lax.optimization_barrier((out_scales, sending))
+    weight = pl.pallas_call(
+        weight_kernel,
+        out_shape=shape((8192, 512), bf16),
+        in_specs=[hbm] * 2,
+        out_specs=vmem,
+        scratch_shapes=[
+            pltpu.VMEM((2048, 512), i32),
+            pltpu.VMEM((64, 512), i32),
+            pltpu.VMEM((64, 512), f32),
+            pltpu.SemaphoreType.DMA,
+            pltpu.SemaphoreType.DMA((code_chunks,)),
+        ],
         compiler_params=params,
-        cost_estimate=pl.CostEstimate(flops=300_000_000, bytes_accessed=2_000_000, transcendentals=65536),
-        name="own_heads",
-    )(query, now, length, select, keys, values)
+        cost_estimate=pl.CostEstimate(flops=20_000_000, bytes_accessed=12_000_000, transcendentals=0),
+        name="unpack_weight",
+    )(*in_hbm(out_codes, out_scales))
+    received, weight = lax.optimization_barrier((received, weight))
     attended = pl.pallas_call(
         combine_kernel,
-        out_shape=shape((rows, 512), bf16),
-        in_specs=[vmem] * 3,
+        out_shape=shape((1, rows, 1024), bf16),
+        in_specs=[vmem] * 2,
         out_specs=vmem,
+        scratch_shapes=[pltpu.VMEM((2, rows, 512), f32)],
         compiler_params=params,
         name="combine_halves",
-    )(own, own_log, received)
-    gathered = lax.all_gather(attended, "tensor", axis=0, tiled=True)
+    )(sending, received)
+    groups = [list(range(parity, 16, 2)) for parity in range(2)]
+    strided = [[4 * k + i for k in range(4)] for i in range(4)]
+    edges = [[2 * a + 1, (2 * a + 2) % 16] for a in range(8)]
+    edges = [edge if a % 2 == 0 else edge[::-1] for a, edge in enumerate(edges)]
+    gathered = lax.all_gather(attended[0], "tensor", axis=0, tiled=True, axis_index_groups=strided)
+    gathered = lax.all_gather(gathered, "tensor", axis=0, tiled=True, axis_index_groups=edges)
     return pl.pallas_call(
         project_kernel,
         out_shape=shape((rows, 512), bf16),
@@ -529,7 +558,7 @@
         out_specs=vmem,
         compiler_params=params,
         name="project",
-    )(gathered, hadamard, weight)
+    )(gathered.reshape(256, 1024), hadamard, weight)
 
 
 def solution(mesh):

time: 57.3 us -> 54.2 us (0.946)
  blocking collectives: 37.3 us -> 34.5 us
  waiting for transfers between devices: 1.85 us -> 0.01 us
  Pallas kernels: 12.1 us -> 13.7 us
    all_gather x1 -> x2, blocking collectives: 37.3 us -> 34.5 us  [the longest x1 26.2 us: per_device(): lax.all_gather(attended[0], 'tensor', axis=0, tiled=True, axis_index_grou...]
    ppermute x1, waiting for transfers between devices: 1.85 us -> 0.01 us  [per_device(): received = lax.ppermute(sending, 'tensor', pairs)]
    pallas_call x4, Pallas kernels: 9.59 us -> 11.1 us  [the longest x1 4.63 us: per_device(): pl.pallas_call(weight_kernel, out_shape=shape((8192, 512), bf16), in_spec...]
  transfers between devices with their start and end apart: 2 -> 2, of which waited for: 1 -> 0; matrix products, arithmetic and copies ran while one was open for 0% -> 0% of each run, Pallas kernels for 13% -> 16%
where the time goes in v3:
time: 54.2 us; the launch traced here: 54 us
  blocking collectives  34.5 us (64%)
  Pallas kernels  13.7 us (25%)
  starting transfers between devices  5.83 us (11%)
    all_gather x1, blocking collectives, per_device(): lax.all_gather(attended[0], 'tensor', axis=0, tiled=True, axis_index_grou...  26.2 us
    all_gather x1, blocking collectives, per_device(): lax.all_gather(gathered, 'tensor', axis=0, tiled=True, axis_index_groups=...  8.25 us
    pallas_call x1, Pallas kernels, per_device(): pl.pallas_call(weight_kernel, out_shape=shape((8192, 512), bf16), in_spec...  4.63 us
    pallas_call x1, Pallas kernels, per_device(): pl.pallas_call(own_kernel, out_shape=(shape((512, 512), bf16), shape((512...  4.21 us
    ppermute x1, starting transfers between devices, per_device(): other_queries = lax.ppermute(queries, 'tensor', pairs)  3.81 us
    pallas_call x1, Pallas kernels, per_device(): pl.pallas_call(project_kernel, out_shape=shape((rows, 512), bf16), in_spe...  2.53 us
    pallas_call x1, Pallas kernels, per_device(): pl.pallas_call(partner_kernel, out_shape=shape((rows, 1280), bf16), in_sp...  2.11 us
    ppermute x1, starting transfers between devices, per_device(): received = lax.ppermute(sending, 'tensor', pairs)  2.02 us
  transfers between devices with their start and end apart: 2, of which 0 were waited for; matrix products, arithmetic and copies ran while one was open for 0% of the time, Pallas kernels for 16%

profile of v3, /device:TPU:24, one launch (start us, length us, event | category | flops | bytes accessed | tf_op | source)
XLA Modules:
  0.0 54.0 jit_solution(14330835896190961964)
XLA Ops:
  0.0 3.8 %collective-permute-start = (bf16[32,4,128]{2,1,0:T(4,128)(2,1)}, bf16[32,4,128]{2,1,0:T(4,128)(2,1)S(1)}, u32[]{:S(2)}, u32[]{:S(2)}) collective-permute-start(bf16[32,4,128]{2,1,0:T(4,128)(2,1)} %param.12), channel_id=1, source_target_pairs={{0,1},{1,0},{2,3},{3,2},{4,5},{5,4},{6,7},{7,6},{8,9},{9,8},{10,11... | collective-permute-start | bytes 98312 | tf_op jit(solution)/shard_map/ppermute | solution.py:465
  3.8 4.2 %own_heads.1 = (bf16[512,512]{1,0:T(8,128)(2,1)S(1)}, bf16[512,512]{1,0:T(8,128)(2,1)S(1)}, f32[32,256]{1,0:T(8,128)S(1)}, bf16[2,32,128]{2,1,0:T(8,128)(2,1)S(1...) custom-call(s32[32]{0:T(128)} %lengths_hbm.1, ...), custom_call_target="tpu_custom_call" | custom-call | flops 400000000 | bytes 14000000 | tf_op jit(solution)/shard_map/own_heads/pallas_call | solution.py:466
  8.0 0.0 collective-permute-done
  8.1 2.1 %other_heads.1.mine_ref = bf16[32,1280]{1,0:T(8,128)(2,1)S(1)} custom-call(bf16[128,128]{1,0:T(8,128)(2,1)S(1)} %bitcast.8, f32[32,256]{1,0:T(8,128)S(1)} %get-tuple-element.16.table_ref, bf16[2,32,128]{2,1,0:T(8,128)(2,1)S(1)} %get-tuple-element.17.now_ref, s32[8,128]{1,0:T(8,128)S(1)} %get-tuple-element.18.length_ref, ...), custom_call_target="tpu_custom_call" | custom-call | tf_op jit(solution)/shard_map/other_heads/pallas_call | solution.py:511
  10.2 2.0 %collective-permute-start.1 = (bf16[32,1280]{1,0:T(8,128)(2,1)S(1)}, bf16[32,1280]{1,0:T(8,128)(2,1)S(1)}, u32[]{:S(2)}, u32[]{:S(2)}) collective-permute-start(bf16[32,1280]{1,0:T(8,128)(2,1)S(1)} %other_heads.1.mine_ref), channel_id=1, source_target_pairs={{0,1},{1,0},{2,3},{3,2},{4,5},{5,4},{6,7},{7,6},{8,9},{9,8},{10,11... | collective-permute-start | bytes 245768 | tf_op jit(solution)/shard_map/ppermute | solution.py:520
  12.2 4.6 %unpack_weight.1.weight_ref = bf16[8192,512]{1,0:T(8,128)(2,1)S(1)} custom-call(s32[2048,512]{1,0:T(8,128)} %codes_hbm.1, s32[64,512]{1,0:T(8,128)} %scales_hbm), custom_call_target="tpu_custom_call" | custom-call | flops 20000000 | bytes 12000000 | tf_op jit(solution)/shard_map/unpack_weight/pallas_call | solution.py:522
  16.8 0.0 collective-permute-done.1.theirs_ref
  16.8 0.2 combine_halves.1
  17.0 26.2 %all-gather = bf16[1,128,1024]{2,1,0:T(8,128)(2,1)S(1)} all-gather(bf16[1,32,1024]{2,1,0:T(8,128)(2,1)S(1)} %combine_halves.1), channel_id=2, replica_groups={{0,4,8,12},{1,5,9,13},{2,6,10,14},{3,7,11,15},{16,20,24,28},{17,21,25,2..., dimensions={1}, use_global_device_ids=true | all-gather | bytes 327680 | tf_op jit(solution)/shard_map/all_gather | solution.py:552
  43.3 8.2 %all-gather.1 = bf16[1,256,1024]{2,1,0:T(8,128)(2,1)S(1)} all-gather(bf16[1,128,1024]{2,1,0:T(8,128)(2,1)S(1)} %all-gather), channel_id=3, replica_groups={{1,2},{4,3},{5,6},{8,7},{9,10},{12,11},{13,14},{0,15},{17,18},{20,19},{..., dimensions={1}, use_global_device_ids=true | all-gather | bytes 786432 | tf_op jit(solution)/shard_map/all_gather | solution.py:553
  51.5 2.5 %project.1 = bf16[32,512]{1,0:T(8,128)(2,1)} custom-call(bf16[256,1024]{1,0:T(8,128)(2,1)S(1)} %bitcast.7, bf16[256,256]{1,0:T(8,128)(2,1)S(1)} %get-tuple-element.25.hadamard_ref, bf16[8192,512]{1,0:T(8,128)(2,1)S(1)} %unpack_weight.1.weight_ref), custom_call_target="tpu_custom_call" | custom-call | tf_op jit(solution)/shard_map/project/pallas_call | solution.py:554
Async XLA Ops:
  0.0 8.0 %collective-permute-start = (bf16[32,4,128]{2,1,0:T(4,128)(2,1)}, bf16[32,4,128]{2,1,0:T(4,128)(2,1)S(1)}, u32[]{:S(2)}, u32[]{:S(2)}) collective-permute-start(bf16[32,4,128]{2,1,0:T(4,128)(2,1)} %param.12), channel_id=1, source_target_pairs={{0,1},{1,0},{2,3},{3,2},{4,5},{5,4},{6,7},{7,6},{8,9},{9,8},{10,11... | collective-permute-start | bytes 98312 | tf_op jit(solution)/shard_map/ppermute | solution.py:465
  10.2 6.7 %collective-permute-start.1 = (bf16[32,1280]{1,0:T(8,128)(2,1)S(1)}, bf16[32,1280]{1,0:T(8,128)(2,1)S(1)}, u32[]{:S(2)}, u32[]{:S(2)}) collective-permute-start(bf16[32,1280]{1,0:T(8,128)(2,1)S(1)} %other_heads.1.mine_ref), channel_id=1, source_target_pairs={{0,1},{1,0},{2,3},{3,2},{4,5},{5,4},{6,7},{7,6},{8,9},{9,8},{10,11... | collective-permute-start | bytes 245768 | tf_op jit(solution)/shard_map/ppermute | solution.py:520

commit v4 on v3

--- a/solution.py
+++ b/solution.py
@@ -105,11 +105,16 @@
 
 def rotate_queries(q, scratch, table_ref):
     scratch[...] = q.astype(jnp.float32)
+    heads = [
+        rotate_rows(
+            scratch[pl.ds(h, rows, stride=local_heads), :], table_ref[:, :128], table_ref[:, 128:]
+        )
+        for h in range(local_heads)
+    ]
     return jnp.concatenate(
         [
-            rotate_rows(
-                scratch[pl.ds(h, rows, stride=local_heads), :], table_ref[:, :128], table_ref[:, 128:]
-            )
+            heads[h][b * chunk : (b + 1) * chunk]
+            for b in range(rows // chunk)
             for h in range(local_heads)
         ],
         axis=0,
@@ -117,14 +122,19 @@
 
 
 def attend(
-    half, length_ref, q_rot, key_now, value_now, select_ref, key_ref, value_ref, store
+    half, length_ref, q_rot, key_now, value_now, select_ref, key_ref, value_ref, target
 ):
-    spread = jnp.dot(q_rot, select_ref[...], preferred_element_type=jnp.float32)
-    new_all = lax.dot_general(
+    size = local_heads * chunk
+    blocks = range(rows // chunk)
+    select = select_ref[...]
+    spread = jnp.dot(q_rot, select, preferred_element_type=jnp.float32)
+    new_scores = lax.dot_general(
         q_rot, key_now, nt, preferred_element_type=jnp.float32
     ) * np.float32(head_width**-0.5)
+    row = iota((128, rows), 0)
+    mine = jnp.logical_and(iota((128, rows), 1) == row // size * chunk + row % chunk, half == 0)
+    new_scores = jnp.where(mine, new_scores, neg_floor)
     lane_low = iota((1, 512), 1) % 128 // 32
-    size = local_heads * chunk
     row = iota((4 * size, 128), 0)
     lane = iota((4 * size, 128), 1)
     position = jnp.where(
@@ -132,74 +142,81 @@
         half * half_tokens + 4 * (lane % 16) + row // size,
         1 << 20,
     )
-    for b in range(rows // chunk):
-        pick = lambda a: jnp.concatenate(
-            [a[h * rows + b * chunk : h * rows + (b + 1) * chunk] for h in range(local_heads)], 0
+    scores, live = [], []
+    for b in blocks:
+        part = spread[b * size : (b + 1) * size]
+        left = jnp.concatenate(
+            [jnp.where(lane_low == low, part, 0.0) for low in range(4)], axis=0
+        ).astype(jnp.bfloat16)
+        scores.append(
+            lax.dot_general(
+                left, key_ref[pl.ds(b * 128, 128), :], nt, preferred_element_type=jnp.float32
+            )
         )
-        q_block = pick(spread)
-        left = jnp.concatenate(
-            [jnp.where(lane_low == low, q_block, 0.0) for low in range(4)], axis=0
-        ).astype(jnp.bfloat16)
-        cache = pl.ds(b * 128, 128)
-        scores = lax.dot_general(left, key_ref[cache, :], nt, preferred_element_type=jnp.float32)
-        length_row = length_ref[pl.ds(b, 1), :]
-        live = position < length_row
-        scores = jnp.where(live, scores, neg_floor)
-        new_block = pick(new_all)
-        mine = jnp.logical_and(
-            iota((size, rows), 1) == b * chunk + iota((size, rows), 0) % chunk, half == 0
+    for b in blocks:
+        live.append(position < length_ref[pl.ds(b, 1), :])
+        scores[b] = jnp.where(live[b], scores[b], neg_floor)
+    quarter = lambda a, low: a[low * size : (low + 1) * size]
+    widest = [
+        jnp.maximum(
+            jnp.maximum(quarter(a, 0), quarter(a, 1)), jnp.maximum(quarter(a, 2), quarter(a, 3))
         )
-        new_block = jnp.where(mine, new_block, neg_floor)
-        parts = [scores[low * size : (low + 1) * size] for low in range(4)]
-        top = jnp.maximum(
-            jnp.max(
-                jnp.maximum(jnp.maximum(parts[0], parts[1]), jnp.maximum(parts[2], parts[3])),
-                axis=1,
-                keepdims=True,
-            ),
-            jnp.max(new_block, axis=1, keepdims=True),
+        for a in scores
+    ]
+    top = jnp.maximum(
+        jnp.max(jnp.concatenate(widest, axis=0), axis=1, keepdims=True),
+        jnp.max(new_scores, axis=1, keepdims=True),
+    )
+    weights = []
+    for b in blocks:
+        shift = jnp.broadcast_to(top[b * size : (b + 1) * size], (size, 128))
+        shift = jnp.concatenate([shift] * 4, axis=0)
+        weights.append(jnp.where(live[b], jnp.exp(scores[b] - shift), 0.0).astype(jnp.bfloat16))
+    new_weight = jnp.where(mine, jnp.exp(new_scores - top), 0.0).astype(jnp.bfloat16)
+    mixed = []
+    for b in blocks:
+        crossed = jnp.dot(
+            weights[b], value_ref[pl.ds(b * 128, 128), :], preferred_element_type=jnp.float32
         )
-        weights = jnp.where(
-            live, jnp.exp(scores - jnp.concatenate([top] * 4, axis=0)), 0.0
-        ).astype(jnp.bfloat16)
-        new_weight = jnp.where(mine, jnp.exp(new_block - top), 0.0).astype(jnp.bfloat16)
-        wide = weights.astype(jnp.float32)
-        total = jnp.sum(
-            wide[:size] + wide[size : 2 * size] + wide[2 * size : 3 * size] + wide[3 * size :],
-            axis=1,
-            keepdims=True,
-        ) + jnp.sum(new_weight.astype(jnp.float32), axis=1, keepdims=True)
-        crossed = jnp.dot(weights, value_ref[cache, :], preferred_element_type=jnp.float32)
-        mixed = jnp.where(lane_low == 0, crossed[:size], 0.0)
+        kept = quarter(crossed, 0)
         for low in range(1, 4):
-            mixed = jnp.where(lane_low == low, crossed[low * size : (low + 1) * size], mixed)
-        high = mixed.astype(jnp.bfloat16)
-        rest = (mixed - high.astype(jnp.float32)).astype(jnp.bfloat16)
-        weighted = (
-            lax.dot_general(high, select_ref[...], nt, preferred_element_type=jnp.float32)
-            + lax.dot_general(rest, select_ref[...], nt, preferred_element_type=jnp.float32)
-            + jnp.dot(new_weight, value_now, preferred_element_type=jnp.float32)
-        )
-        some = total > 0.0
-        floor_total = jnp.where(some, total, 1.0)
-        logsum = jnp.where(some, top + jnp.log(floor_total), neg_floor)
-        result = weighted / floor_total
+            kept = jnp.where(lane_low == low, quarter(crossed, low), kept)
+        mixed.append(kept)
+    sums = []
+    for b in blocks:
+        wide = weights[b].astype(jnp.float32)
+        sums.append((quarter(wide, 0) + quarter(wide, 1)) + (quarter(wide, 2) + quarter(wide, 3)))
+    total = jnp.sum(jnp.concatenate(sums, axis=0), axis=1, keepdims=True) + jnp.sum(
+        new_weight.astype(jnp.float32), axis=1, keepdims=True
+    )
+    mixed = jnp.concatenate(mixed, axis=0)
+    high = mixed.astype(jnp.bfloat16)
+    rest = (mixed - high.astype(jnp.float32)).astype(jnp.bfloat16)
+    weighted = (
+        lax.dot_general(high, select, nt, preferred_element_type=jnp.float32)
+        + lax.dot_general(rest, select, nt, preferred_element_type=jnp.float32)
+        + jnp.dot(new_weight, value_now, preferred_element_type=jnp.float32)
+    )
+    some = total > 0.0
+    floor_total = jnp.where(some, total, 1.0)
+    logsum = jnp.where(some, top + jnp.log(floor_total), neg_floor)
+    result = weighted / floor_total
+    pieces = stats_of(logsum)
+    lane_head = iota((chunk, 128), 1) // 32
+    for b in blocks:
+        at = pl.ds(b * chunk, chunk)
+        tail = None
         for h in range(local_heads):
-            part = slice(h * chunk, (h + 1) * chunk)
-            store(b, h, result[part], logsum[part])
-
-
-def pick_head(array, index):
-    wide = array.astype(jnp.float32)
-    return jnp.sum(jnp.where(iota(wide.shape, 1) == index, wide, 0.0), axis=1)
-
-
-code_chunks = 8
+            start = b * size + h * chunk
+            target[at, h * 128 : (h + 1) * 128] = result[start : start + chunk]
+            stat = pieces[start : start + chunk]
+            tail = stat if tail is None else jnp.where(lane_head == h, stat, tail)
+        target[at, 512:640] = tail
 
 
 def stats_of(logsum):
-    which = iota((chunk, 128), 1) % 32
-    whole = jnp.broadcast_to(logsum, (chunk, 128))
+    which = iota((128, 128), 1) % 32
+    whole = jnp.broadcast_to(logsum, (128, 128))
     first = whole.astype(jnp.bfloat16).astype(jnp.float32)
     second = (whole - first).astype(jnp.bfloat16).astype(jnp.float32)
     third = whole - first - second
@@ -208,19 +225,9 @@
     )
 
 
-def storing(target):
-    lane_head = iota((chunk, 128), 1) // 32
-    tail = slice(512, 640)
-
-    def store(b, h, result, logsum):
-        block = pl.ds(b * chunk, chunk)
-        target[block, h * 128 : (h + 1) * 128] = result
-        pieces = stats_of(logsum)
-        target[block, tail] = (
-            pieces if h == 0 else jnp.where(lane_head == h, pieces, target[block, tail])
-        )
-
-    return store
+def pick_head(array, index):
+    wide = array.astype(jnp.float32)
+    return jnp.sum(jnp.where(iota(wide.shape, 1) == index, wide, 0.0), axis=1)
 
 
 def own_kernel(
@@ -234,6 +241,8 @@
     value_scales_hbm,
     key_table_hbm,
     query_table_hbm,
+    out_codes_hbm,
+    out_scales_hbm,
     key_ref,
     value_ref,
     table_ref,
@@ -242,6 +251,8 @@
     select_ref,
     hadamard_ref,
     own_ref,
+    out_codes_ref,
+    out_scales_ref,
     lengths,
     queries,
     new_key,
@@ -269,6 +280,8 @@
         (new_key_hbm, new_key),
         (new_value_hbm, new_value),
         (queries_hbm, queries),
+        (out_codes_hbm, out_codes_ref),
+        (out_scales_hbm, out_scales_ref),
     ]
     copies = [
         pltpu.make_async_copy(source, target, sems.at[i]) for i, (source, target) in enumerate(pairs)
@@ -295,7 +308,7 @@
     scales = spread_scales(value_scales[...]) * np.float32(1.0 / cache_step)
     for j, plane in enumerate(unpack_planes(value_codes[...])):
         value_ref[:, j * 128 : (j + 1) * 128] = (plane * scales).astype(jnp.bfloat16)
-    for copy in copies[5:]:
+    for copy in copies[5:10]:
         copy.wait()
     for r in range(rows):
         table_ref[pl.ds(r, 1), :] = query_table[pl.ds(lengths[r], 1), :]
@@ -319,8 +332,10 @@
         select_ref,
         key_ref,
         value_ref,
-        storing(own_ref),
-    )
+        own_ref,
+    )
+    for copy in copies[10:]:
+        copy.wait()
 
 
 def partner_kernel(
@@ -345,7 +360,7 @@
         select_ref,
         key_ref,
         value_ref,
-        storing(out_scratch),
+        out_scratch,
     )
     out_ref[:, :640] = own_ref[...].astype(jnp.bfloat16)
     out_ref[:, 640:] = out_scratch[...].astype(jnp.bfloat16)
@@ -373,45 +388,41 @@
             ) + other_block * (their_factor * scale)
     first = scratch[half].astype(jnp.bfloat16)
     second = scratch[1 - half].astype(jnp.bfloat16)
-    for k in range(out_ref.shape[0]):
-        out_ref[k, :, :512] = first
-        out_ref[k, :, 512:] = second
-
-
-def weight_kernel(codes_hbm, scales_hbm, weight_ref, codes, scales, scale_scratch, sem, code_sems):
-    size = codes_hbm.shape[0] // code_chunks
-
-    def code_copy(i):
-        part = pl.ds(i * size, size)
-        return pltpu.make_async_copy(codes_hbm.at[part, :], codes.at[part, :], code_sems.at[i])
-
-    scale_copy = pltpu.make_async_copy(scales_hbm, scales, sem)
-    scale_copy.start()
-    for i in range(code_chunks):
-        code_copy(i).start()
-    scale_copy.wait()
-    scale_scratch[...] = scales[...].astype(jnp.float32) * np.float32(1.0 / weight_step)
-
-    @pl.loop(0, code_chunks)
-    def _(i):
-        code_copy(i).wait()
-        for b in range(size // 32):
-            words = codes[pl.ds(i * size + b * 32, 32), :]
-            group = i * (size // 32) + b
-            scale = jnp.broadcast_to(scale_scratch[pl.ds(group, 1), :], (16, 512)).astype(jnp.bfloat16)
+    out_ref[:, :512] = first
+    out_ref[:, 512:] = second
+
+
+def weight_kernel(codes_ref, scales_ref, weight_ref, scale_scratch):
+    scale_scratch[...] = scales_ref[...].astype(jnp.float32) * np.float32(1.0 / weight_step)
+
+    @pl.loop(0, 4)
+    def _(q):
+        for b in range(8):
+            words, scales = [], []
+            for c in range(2):
+                group = q * 16 + c * 8 + b
+                words.append(codes_ref[pl.ds(group * 32, 32), :])
+                scales.append(
+                    jnp.broadcast_to(scale_scratch[pl.ds(group, 1), :], (32, 512)).astype(
+                        jnp.bfloat16
+                    )
+                )
             for k in range(4):
                 power = 16.0**k
-                plane = (
-                    jnp.bitwise_and(words, 15 << 4 * k).astype(jnp.float32).astype(jnp.bfloat16)
-                    - jnp.bfloat16(code_offset * power)
-                )
-                scaled = scale * jnp.bfloat16(1.0 / power)
-                for part in range(2):
-                    start = i * size * 4 + (b // 2) * 256 + k * 64 + (b % 2) * 32 + part * 16
-                    weight_ref[pl.ds(start, 16), :] = plane[part * 16 : (part + 1) * 16] * scaled
-
-
-def project_kernel(gathered_ref, hadamard_ref, weight_ref, out_ref):
+                first, second = [
+                    (
+                        jnp.bitwise_and(word, 15 << 4 * k).astype(jnp.float32).astype(jnp.bfloat16)
+                        - jnp.bfloat16(code_offset * power)
+                    )
+                    * (scale * jnp.bfloat16(1.0 / power))
+                    for word, scale in zip(words, scales)
+                ]
+                start = q * 1024 + (b // 2) * 256 + k * 64 + (b % 2) * 32
+                weight_ref[0, pl.ds(start, 32), :] = first + second
+                weight_ref[1, pl.ds(start, 32), :] = first - second
+
+
+def project_half(gathered_ref, hadamard_ref, weight_ref, pair_class):
     hadamard = hadamard_ref[...]
     factor = np.float32(8192.0**-0.5)
     turned = [
@@ -420,22 +431,35 @@
         )
         for q in range(4)
     ]
-    start = [((i // 4) % 2 * 4 + i // 8) * rows for i in range(32)]
-    blocks = [turned[i % 4][start[i] : start[i] + rows] for i in range(32)]
-    for bit in range(5):
+    blocks = [turned[i % 4][i // 4 * rows : (i // 4 + 1) * rows] for i in range(16)]
+    for bit in range(4):
         step = 1 << bit
         blocks = [
             blocks[i] + blocks[i ^ step] if i & step == 0 else blocks[i ^ step] - blocks[i]
-            for i in range(32)
+            for i in range(16)
         ]
-    total = jnp.zeros((rows, 512), jnp.float32)
-    for i in range(32):
-        total = total + jnp.dot(
+    total = None
+    for i in range(16):
+        term = jnp.dot(
             (blocks[i] * factor).astype(jnp.bfloat16),
-            weight_ref[i * 256 : (i + 1) * 256, :],
+            weight_ref[pair_class, i * 256 : (i + 1) * 256, :],
             preferred_element_type=jnp.float32,
         )
-    out_ref[...] = total.astype(jnp.bfloat16)
+        total = term if total is None else total + term
+    return total
+
+
+def pair_class_here():
+    return lax.rem(lax.div(lax.axis_index("tensor"), 2), 2)
+
+
+def first_half_kernel(gathered_ref, hadamard_ref, weight_ref, out_ref):
+    out_ref[...] = project_half(gathered_ref, hadamard_ref, weight_ref, pair_class_here())
+
+
+def second_half_kernel(gathered_ref, hadamard_ref, weight_ref, first_ref, out_ref):
+    second = project_half(gathered_ref, hadamard_ref, weight_ref, 1 - pair_class_here())
+    out_ref[...] = (first_ref[...] + second).astype(jnp.bfloat16)
 
 
 vmem = pl.BlockSpec(memory_space=pltpu.VMEM)
@@ -463,7 +487,7 @@
     f32, bf16, i32 = jnp.float32, jnp.bfloat16, jnp.int32
     shape = jax.ShapeDtypeStruct
     other_queries = lax.ppermute(queries, "tensor", pairs)
-    keys, values, table, now, length, select, hadamard, own = pl.pallas_call(
+    outputs = pl.pallas_call(
         own_kernel,
         out_shape=(
             shape((512, 512), bf16),
@@ -474,9 +498,11 @@
             shape((128, 512), bf16),
             shape((256, 256), bf16),
             shape((rows, 640), f32),
+            shape((2048, 512), i32),
+            shape((64, 512), i32),
         ),
-        in_specs=[hbm] * 10,
-        out_specs=(vmem,) * 8,
+        in_specs=[hbm] * 12,
+        out_specs=(vmem,) * 10,
         scratch_shapes=[
             pltpu.SMEM((rows,), i32),
             pltpu.VMEM((128, 128), bf16),
@@ -489,7 +515,7 @@
             pltpu.VMEM((2, 16, 512), f32),
             pltpu.VMEM((136, 256), f32),
             pltpu.VMEM((128, 128), f32),
-            pltpu.SemaphoreType.DMA((10,)),
+            pltpu.SemaphoreType.DMA((12,)),
         ],
         compiler_params=params,
         cost_estimate=pl.CostEstimate(flops=400_000_000, bytes_accessed=14_000_000, transcendentals=0),
@@ -506,8 +532,11 @@
             value_scales.reshape(rows, half_tokens),
             jnp.asarray(key_tables()),
             jnp.asarray(query_table()),
+            out_codes,
+            out_scales,
         )
     )
+    keys, values, table, now, length, select, hadamard, own, codes, scales = outputs
     sending = pl.pallas_call(
         partner_kernel,
         out_shape=shape((rows, 1280), bf16),
@@ -518,47 +547,48 @@
         name="other_heads",
     )(other_queries.reshape(128, 128), table, now, length, select, keys, values, own)
     received = lax.ppermute(sending, "tensor", pairs)
-    out_scales, _ = lax.optimization_barrier((out_scales, sending))
+    scales, _ = lax.optimization_barrier((scales, sending))
     weight = pl.pallas_call(
         weight_kernel,
-        out_shape=shape((8192, 512), bf16),
-        in_specs=[hbm] * 2,
+        out_shape=shape((2, 4096, 512), bf16),
+        in_specs=[vmem] * 2,
         out_specs=vmem,
-        scratch_shapes=[
-            pltpu.VMEM((2048, 512), i32),
-            pltpu.VMEM((64, 512), i32),
-            pltpu.VMEM((64, 512), f32),
-            pltpu.SemaphoreType.DMA,
-            pltpu.SemaphoreType.DMA((code_chunks,)),
-        ],
+        scratch_shapes=[pltpu.VMEM((64, 512), f32)],
         compiler_params=params,
         cost_estimate=pl.CostEstimate(flops=20_000_000, bytes_accessed=12_000_000, transcendentals=0),
         name="unpack_weight",
-    )(*in_hbm(out_codes, out_scales))
+    )(codes, scales)
     received, weight = lax.optimization_barrier((received, weight))
     attended = pl.pallas_call(
         combine_kernel,
-        out_shape=shape((1, rows, 1024), bf16),
+        out_shape=shape((rows, 1024), bf16),
         in_specs=[vmem] * 2,
         out_specs=vmem,
         scratch_shapes=[pltpu.VMEM((2, rows, 512), f32)],
         compiler_params=params,
         name="combine_halves",
     )(sending, received)
-    groups = [list(range(parity, 16, 2)) for parity in range(2)]
     strided = [[4 * k + i for k in range(4)] for i in range(4)]
-    edges = [[2 * a + 1, (2 * a + 2) % 16] for a in range(8)]
-    edges = [edge if a % 2 == 0 else edge[::-1] for a, edge in enumerate(edges)]
-    gathered = lax.all_gather(attended[0], "tensor", axis=0, tiled=True, axis_index_groups=strided)
-    gathered = lax.all_gather(gathered, "tensor", axis=0, tiled=True, axis_index_groups=edges)
-    return pl.pallas_call(
-        project_kernel,
-        out_shape=shape((rows, 512), bf16),
+    gathered = lax.all_gather(attended, "tensor", axis=0, tiled=True, axis_index_groups=strided)
+    edges = [(2 * a + 1, (2 * a + 2) % 16) for a in range(8)]
+    other_class = lax.ppermute(gathered, "tensor", edges + [edge[::-1] for edge in edges])
+    first = pl.pallas_call(
+        first_half_kernel,
+        out_shape=shape((rows, 512), f32),
         in_specs=[vmem] * 3,
         out_specs=vmem,
         compiler_params=params,
-        name="project",
-    )(gathered.reshape(256, 1024), hadamard, weight)
+        cost_estimate=pl.CostEstimate(flops=300_000_000, bytes_accessed=5_000_000, transcendentals=0),
+        name="project_first",
+    )(gathered, hadamard, weight)
+    return pl.pallas_call(
+        second_half_kernel,
+        out_shape=shape((rows, 512), bf16),
+        in_specs=[vmem] * 4,
+        out_specs=vmem,
+        compiler_params=params,
+        name="project_second",
+    )(other_class, hadamard, weight, first)
 
 
 def solution(mesh):

time: 54.2 us -> 51.3 us (0.946)
  blocking collectives: 34.5 us -> 25.3 us
  waiting for transfers between devices: 0.01 us -> 5.11 us
  starting transfers between devices: 5.83 us -> 10.5 us
  Pallas kernels: 13.7 us -> 9.89 us
    all_gather x2 -> x1, blocking collectives: 34.5 us -> 25.3 us  [per_device(): lax.all_gather(attended, 'tensor', axis=0, tiled=True, axis_index_groups=...]
    ppermute x0 -> x1, waiting for transfers between devices: none -> 4.71 us  [per_device(): lax.ppermute(gathered, 'tensor', edges + [edge[::-1] for edge in edges])]
    ppermute x0 -> x1, starting transfers between devices: none -> 3.68 us  [per_device(): lax.ppermute(gathered, 'tensor', edges + [edge[::-1] for edge in edges])]
    pallas_call x3 -> x4, Pallas kernels: 7.35 us -> 5.86 us  [the longest x1 2.93 us: per_device(): pl.pallas_call(weight_kernel, out_shape=shape((2, 4096, 512), bf16), in_s...]
    pallas_call x1, Pallas kernels: 4.21 us -> 3.01 us  [per_device(): pl.pallas_call(own_kernel, out_shape=(shape((512, 512), bf16), shape((512...]
    pallas_call x1, Pallas kernels: 2.11 us -> 1.02 us  [per_device(): pl.pallas_call(partner_kernel, out_shape=shape((rows, 1280), bf16), in_sp...]
    ppermute x1, starting transfers between devices: 2.02 us -> 3 us  [per_device(): received = lax.ppermute(sending, 'tensor', pairs)]
  transfers between devices with their start and end apart: 2 -> 3, of which waited for: 0 -> 2; matrix products, arithmetic and copies ran while one was open for 0% -> 0% of each run, Pallas kernels for 16% -> 14%
where the time goes in v4:
time: 51.3 us; the launch traced here: 50.9 us
  blocking collectives  25.3 us (49%)
  starting transfers between devices  10.5 us (20%)
  Pallas kernels  9.89 us (19%)
  waiting for transfers between devices  5.11 us (10%)
    all_gather x1, blocking collectives, per_device(): lax.all_gather(attended, 'tensor', axis=0, tiled=True, axis_index_groups=...  25.3 us
    ppermute x1, waiting for transfers between devices, per_device(): lax.ppermute(gathered, 'tensor', edges + [edge[::-1] for edge in edges])  4.71 us
    ppermute x1, starting transfers between devices, per_device(): other_queries = lax.ppermute(queries, 'tensor', pairs)  3.81 us
    ppermute x1, starting transfers between devices, per_device(): lax.ppermute(gathered, 'tensor', edges + [edge[::-1] for edge in edges])  3.68 us
    pallas_call x1, Pallas kernels, per_device(): pl.pallas_call(own_kernel, out_shape=(shape((512, 512), bf16), shape((512...  3.01 us
    ppermute x1, starting transfers between devices, per_device(): received = lax.ppermute(sending, 'tensor', pairs)  3 us
    pallas_call x1, Pallas kernels, per_device(): pl.pallas_call(weight_kernel, out_shape=shape((2, 4096, 512), bf16), in_s...  2.93 us
    pallas_call x1, Pallas kernels, per_device(): pl.pallas_call(second_half_kernel, out_shape=shape((rows, 512), bf16), in...  1.69 us
  transfers between devices with their start and end apart: 3, of which 2 were waited for; matrix products, arithmetic and copies ran while one was open for 0% of the time, Pallas kernels for 14%

profile of v4, /device:TPU:24, one launch (start us, length us, event | category | flops | bytes accessed | tf_op | source)
XLA Modules:
  0.0 50.9 jit_solution(1459825606772600844)
XLA Ops:
  0.0 3.8 %collective-permute-start = (bf16[32,4,128]{2,1,0:T(4,128)(2,1)}, bf16[32,4,128]{2,1,0:T(4,128)(2,1)S(1)}, u32[]{:S(2)}, u32[]{:S(2)}) collective-permute-start(bf16[32,4,128]{2,1,0:T(4,128)(2,1)} %param.12), channel_id=1, source_target_pairs={{0,1},{1,0},{2,3},{3,2},{4,5},{5,4},{6,7},{7,6},{8,9},{9,8},{10,11... | collective-permute-start | bytes 98312 | tf_op jit(solution)/shard_map/ppermute | solution.py:489
  3.8 3.0 %own_heads.1 = (bf16[512,512]{1,0:T(8,128)(2,1)S(1)}, bf16[512,512]{1,0:T(8,128)(2,1)S(1)}, f32[32,256]{1,0:T(8,128)S(1)}, bf16[2,32,128]{2,1,0:T(8,128)(2,1)S(1...) custom-call(s32[32]{0:T(128)} %lengths_hbm.1, ...), custom_call_target="tpu_custom_call" | custom-call | flops 400000000 | bytes 14000000 | tf_op jit(solution)/shard_map/own_heads/pallas_call | solution.py:490
  6.8 0.0 collective-permute-done
  6.8 1.0 %other_heads.1.mine_ref = bf16[32,1280]{1,0:T(8,128)(2,1)S(1)} custom-call(bf16[128,128]{1,0:T(8,128)(2,1)S(1)} %bitcast.6, f32[32,256]{1,0:T(8,128)S(1)} %get-tuple-element.18.table_ref, bf16[2,32,128]{2,1,0:T(8,128)(2,1)S(1)} %get-tuple-element.19.now_ref, s32[8,128]{1,0:T(8,128)S(1)} %get-tuple-element.20.length_ref, ...), custom_call_target="tpu_custom_call" | custom-call | tf_op jit(solution)/shard_map/other_heads/pallas_call | solution.py:540
  7.9 3.0 %collective-permute-start.1 = (bf16[32,1280]{1,0:T(8,128)(2,1)S(1)}, bf16[32,1280]{1,0:T(8,128)(2,1)S(1)}, u32[]{:S(2)}, u32[]{:S(2)}) collective-permute-start(bf16[32,1280]{1,0:T(8,128)(2,1)S(1)} %other_heads.1.mine_ref), channel_id=1, source_target_pairs={{0,1},{1,0},{2,3},{3,2},{4,5},{5,4},{6,7},{7,6},{8,9},{9,8},{10,11... | collective-permute-start | bytes 245768 | tf_op jit(solution)/shard_map/ppermute | solution.py:549
  10.9 2.9 %unpack_weight.1.weight_ref = bf16[2,4096,512]{2,1,0:T(8,128)(2,1)S(1)} custom-call(s32[2048,512]{1,0:T(8,128)S(1)} %get-tuple-element.25.codes_ref, s32[64,512]{1,0:T(8,128)S(1)} %get-tuple-element.27.scales_ref), custom_call_target="tpu_custom_call" | custom-call | flops 20000000 | bytes 12000000 | tf_op jit(solution)/shard_map/unpack_weight/pallas_call | solution.py:551
  13.8 0.4 collective-permute-done.1.theirs_ref
  14.2 0.2 combine_halves.1
  14.4 25.3 %all_gather.3.gathered_ref = bf16[128,1024]{1,0:T(8,128)(2,1)S(1)} all-gather(bf16[32,1024]{1,0:T(8,128)(2,1)S(1)} %combine_halves.1), channel_id=1, replica_groups={{0,4,8,12},{1,5,9,13},{2,6,10,14},{3,7,11,15},{16,20,24,28},{17,21,25,2..., dimensions={0}, use_global_device_ids=true | all-gather | bytes 327680 | tf_op jit(solution)/shard_map/all_gather | solution.py:572
  39.7 3.7 %collective-permute-start.2 = (bf16[128,1024]{1,0:T(8,128)(2,1)S(1)}, bf16[128,1024]{1,0:T(8,128)(2,1)S(1)}, u32[]{:S(2)}, u32[]{:S(2)}) collective-permute-start(bf16[128,1024]{1,0:T(8,128)(2,1)S(1)} %all_gather.3.gathered_ref), channel_id=1, source_target_pairs={{1,2},{3,4},{5,6},{7,8},{9,10},{11,12},{13,14},{15,0},{2,1},{4,3},... | collective-permute-start | bytes 786440 | tf_op jit(solution)/shard_map/ppermute | solution.py:574
  43.4 1.1 %project_first.1.first_ref = f32[32,512]{1,0:T(8,128)S(1)} custom-call(bf16[128,1024]{1,0:T(8,128)(2,1)S(1)} %all_gather.3.gathered_ref, bf16[256,256]{1,0:T(8,128)(2,1)S(1)} %get-tuple-element.29.hadamard_ref, bf16[2,4096,512]{2,1,0:T(8,128)(2,1)S(1)} %unpack_weight.1.weight_ref), custom_call_target="tpu_custom_call" | custom-call | flops 300000000 | bytes 5000000 | tf_op jit(solution)/shard_map/project_first/pallas_call | solution.py:575
  44.5 4.7 %collective-permute-done.2.gathered_ref = bf16[128,1024]{1,0:T(8,128)(2,1)S(1)} collective-permute-done((bf16[128,1024]{1,0:T(8,128)(2,1)S(1)}, bf16[128,1024]{1,0:T(8,128)(2,1)S(1)}, u32[]{:S(2)}, u32[]{:S(2)}) %collective-permute-start.2) | collective-permute-done | bytes 262176 | tf_op jit(solution)/shard_map/ppermute | solution.py:574
  49.2 1.7 %project_second.1 = bf16[32,512]{1,0:T(8,128)(2,1)} custom-call(bf16[128,1024]{1,0:T(8,128)(2,1)S(1)} %collective-permute-done.2.gathered_ref, bf16[256,256]{1,0:T(8,128)(2,1)S(1)} %get-tuple-element.29.hadamard_ref, bf16[2,4096,512]{2,1,0:T(8,128)(2,1)S(1)} %unpack_weight.1.weight_ref, f32[32,512]{1,0:T(8,128)S(1)} %project_first.1.first_ref), custom_call_target="tpu_custom_call" | custom-call | tf_op jit(solution)/shard_map/project_second/pallas_call | solution.py:584
Async XLA Ops:
  0.0 6.8 %collective-permute-start = (bf16[32,4,128]{2,1,0:T(4,128)(2,1)}, bf16[32,4,128]{2,1,0:T(4,128)(2,1)S(1)}, u32[]{:S(2)}, u32[]{:S(2)}) collective-permute-start(bf16[32,4,128]{2,1,0:T(4,128)(2,1)} %param.12), channel_id=1, source_target_pairs={{0,1},{1,0},{2,3},{3,2},{4,5},{5,4},{6,7},{7,6},{8,9},{9,8},{10,11... | collective-permute-start | bytes 98312 | tf_op jit(solution)/shard_map/ppermute | solution.py:489
  7.9 6.3 %collective-permute-start.1 = (bf16[32,1280]{1,0:T(8,128)(2,1)S(1)}, bf16[32,1280]{1,0:T(8,128)(2,1)S(1)}, u32[]{:S(2)}, u32[]{:S(2)}) collective-permute-start(bf16[32,1280]{1,0:T(8,128)(2,1)S(1)} %other_heads.1.mine_ref), channel_id=1, source_target_pairs={{0,1},{1,0},{2,3},{3,2},{4,5},{5,4},{6,7},{7,6},{8,9},{9,8},{10,11... | collective-permute-start | bytes 245768 | tf_op jit(solution)/shard_map/ppermute | solution.py:549
  39.7 9.5 %collective-permute-start.2 = (bf16[128,1024]{1,0:T(8,128)(2,1)S(1)}, bf16[128,1024]{1,0:T(8,128)(2,1)S(1)}, u32[]{:S(2)}, u32[]{:S(2)}) collective-permute-start(bf16[128,1024]{1,0:T(8,128)(2,1)S(1)} %all_gather.3.gathered_ref), channel_id=1, source_target_pairs={{1,2},{3,4},{5,6},{7,8},{9,10},{11,12},{13,14},{15,0},{2,1},{4,3},... | collective-permute-start | bytes 786440 | tf_op jit(solution)/shard_map/ppermute | solution.py:574

commit v5 on v4

--- a/solution.py
+++ b/solution.py
@@ -366,9 +366,10 @@
     out_ref[:, 640:] = out_scratch[...].astype(jnp.bfloat16)
 
 
-def combine_kernel(mine_ref, theirs_ref, out_ref, scratch):
+def combine_kernel(both_ref, out_ref, scratch):
     half = lax.rem(lax.axis_index("tensor"), 2)
     lane_head = iota((rows, 128), 1) // 32
+    mine_ref, theirs_ref = both_ref.at[half], both_ref.at[1 - half]
     for own in range(2):
         at, other = own * 640, 640 - own * 640
         logs = [mine_ref[:, at + 512 : at + 640], theirs_ref[:, other + 512 : other + 640]]
@@ -392,74 +393,76 @@
     out_ref[:, 512:] = second
 
 
-def weight_kernel(codes_ref, scales_ref, weight_ref, scale_scratch):
+def unpacks_early():
+    return lax.axis_index("tensor") < 4
+
+
+def unpack_weight(codes_ref, scales_ref, weight_ref, scale_scratch):
     scale_scratch[...] = scales_ref[...].astype(jnp.float32) * np.float32(1.0 / weight_step)
 
-    @pl.loop(0, 4)
-    def _(q):
+    @pl.loop(0, 8)
+    def _(pair):
         for b in range(8):
-            words, scales = [], []
-            for c in range(2):
-                group = q * 16 + c * 8 + b
-                words.append(codes_ref[pl.ds(group * 32, 32), :])
-                scales.append(
-                    jnp.broadcast_to(scale_scratch[pl.ds(group, 1), :], (32, 512)).astype(
-                        jnp.bfloat16
-                    )
-                )
+            group = pair * 8 + b
+            words = codes_ref[pl.ds(group * 32, 32), :]
+            scale = jnp.broadcast_to(scale_scratch[pl.ds(group, 1), :], (32, 512)).astype(
+                jnp.bfloat16
+            )
             for k in range(4):
                 power = 16.0**k
-                first, second = [
-                    (
-                        jnp.bitwise_and(word, 15 << 4 * k).astype(jnp.float32).astype(jnp.bfloat16)
-                        - jnp.bfloat16(code_offset * power)
-                    )
-                    * (scale * jnp.bfloat16(1.0 / power))
-                    for word, scale in zip(words, scales)
-                ]
-                start = q * 1024 + (b // 2) * 256 + k * 64 + (b % 2) * 32
-                weight_ref[0, pl.ds(start, 32), :] = first + second
-                weight_ref[1, pl.ds(start, 32), :] = first - second
-
-
-def project_half(gathered_ref, hadamard_ref, weight_ref, pair_class):
+                plane = jnp.bitwise_and(words, 15 << 4 * k).astype(jnp.float32).astype(
+                    jnp.bfloat16
+                ) - jnp.bfloat16(code_offset * power)
+                start = pair * 1024 + (b // 2) * 256 + k * 64 + (b % 2) * 32
+                weight_ref[pl.ds(start, 32), :] = plane * (scale * jnp.bfloat16(1.0 / power))
+
+
+def weight_kernel(codes_ref, scales_ref, weight_ref, scale_scratch):
+    @pl.when(unpacks_early())
+    def _():
+        unpack_weight(codes_ref, scales_ref, weight_ref, scale_scratch)
+
+
+def project(gathered_ref, hadamard_ref, weight_ref, out_ref):
     hadamard = hadamard_ref[...]
-    factor = np.float32(8192.0**-0.5)
     turned = [
         jnp.dot(
             gathered_ref[:, q * 256 : (q + 1) * 256], hadamard, preferred_element_type=jnp.float32
         )
         for q in range(4)
     ]
-    blocks = [turned[i % 4][i // 4 * rows : (i // 4 + 1) * rows] for i in range(16)]
-    for bit in range(4):
+    start = [(i // 4 % 2 * 4 + i // 8) * rows for i in range(32)]
+    blocks = [turned[i % 4][start[i] : start[i] + rows] for i in range(32)]
+    for bit in range(5):
         step = 1 << bit
         blocks = [
             blocks[i] + blocks[i ^ step] if i & step == 0 else blocks[i ^ step] - blocks[i]
-            for i in range(16)
+            for i in range(32)
         ]
     total = None
-    for i in range(16):
+    for i in range(32):
         term = jnp.dot(
-            (blocks[i] * factor).astype(jnp.bfloat16),
-            weight_ref[pair_class, i * 256 : (i + 1) * 256, :],
+            blocks[i].astype(jnp.bfloat16),
+            weight_ref[i * 256 : (i + 1) * 256, :],
             preferred_element_type=jnp.float32,
         )
         total = term if total is None else total + term
-    return total
-
-
-def pair_class_here():
-    return lax.rem(lax.div(lax.axis_index("tensor"), 2), 2)
-
-
-def first_half_kernel(gathered_ref, hadamard_ref, weight_ref, out_ref):
-    out_ref[...] = project_half(gathered_ref, hadamard_ref, weight_ref, pair_class_here())
-
-
-def second_half_kernel(gathered_ref, hadamard_ref, weight_ref, first_ref, out_ref):
-    second = project_half(gathered_ref, hadamard_ref, weight_ref, 1 - pair_class_here())
-    out_ref[...] = (first_ref[...] + second).astype(jnp.bfloat16)
+    out_ref[...] = (total * np.float32(8192.0**-0.5)).astype(jnp.bfloat16)
+
+
+def project_kernel(
+    gathered_ref, hadamard_ref, weight_ref, codes_ref, scales_ref, out_ref, late_weight, scale_scratch
+):
+    early = unpacks_early()
+
+    @pl.when(early)
+    def _():
+        project(gathered_ref, hadamard_ref, weight_ref, out_ref)
+
+    @pl.when(jnp.logical_not(early))
+    def _():
+        unpack_weight(codes_ref, scales_ref, late_weight, scale_scratch)
+        project(gathered_ref, hadamard_ref, late_weight, out_ref)
 
 
 vmem = pl.BlockSpec(memory_space=pltpu.VMEM)
@@ -546,11 +549,13 @@
         compiler_params=params,
         name="other_heads",
     )(other_queries.reshape(128, 128), table, now, length, select, keys, values, own)
-    received = lax.ppermute(sending, "tensor", pairs)
-    scales, _ = lax.optimization_barrier((scales, sending))
+    both = lax.all_gather(
+        sending, "tensor", axis=0, axis_index_groups=[[2 * a, 2 * a + 1] for a in range(8)]
+    )
+    scales, _ = lax.optimization_barrier((scales, both))
     weight = pl.pallas_call(
         weight_kernel,
-        out_shape=shape((2, 4096, 512), bf16),
+        out_shape=shape((8192, 512), bf16),
         in_specs=[vmem] * 2,
         out_specs=vmem,
         scratch_shapes=[pltpu.VMEM((64, 512), f32)],
@@ -558,37 +563,30 @@
         cost_estimate=pl.CostEstimate(flops=20_000_000, bytes_accessed=12_000_000, transcendentals=0),
         name="unpack_weight",
     )(codes, scales)
-    received, weight = lax.optimization_barrier((received, weight))
+    both, weight = lax.optimization_barrier((both, weight))
     attended = pl.pallas_call(
         combine_kernel,
         out_shape=shape((rows, 1024), bf16),
-        in_specs=[vmem] * 2,
+        in_specs=[vmem],
         out_specs=vmem,
         scratch_shapes=[pltpu.VMEM((2, rows, 512), f32)],
         compiler_params=params,
         name="combine_halves",
-    )(sending, received)
+    )(both)
     strided = [[4 * k + i for k in range(4)] for i in range(4)]
     gathered = lax.all_gather(attended, "tensor", axis=0, tiled=True, axis_index_groups=strided)
-    edges = [(2 * a + 1, (2 * a + 2) % 16) for a in range(8)]
-    other_class = lax.ppermute(gathered, "tensor", edges + [edge[::-1] for edge in edges])
-    first = pl.pallas_call(
-        first_half_kernel,
-        out_shape=shape((rows, 512), f32),
-        in_specs=[vmem] * 3,
+    edges = [[2 * a + 1, (2 * a + 2) % 16] for a in range(8)]
+    edges = [edge if a % 2 == 0 else edge[::-1] for a, edge in enumerate(edges)]
+    gathered = lax.all_gather(gathered, "tensor", axis=0, tiled=True, axis_index_groups=edges)
+    return pl.pallas_call(
+        project_kernel,
+        out_shape=shape((rows, 512), bf16),
+        in_specs=[vmem] * 5,
         out_specs=vmem,
+        scratch_shapes=[pltpu.VMEM((8192, 512), bf16), pltpu.VMEM((64, 512), f32)],
         compiler_params=params,
-        cost_estimate=pl.CostEstimate(flops=300_000_000, bytes_accessed=5_000_000, transcendentals=0),
-        name="project_first",
-    )(gathered, hadamard, weight)
-    return pl.pallas_call(
-        second_half_kernel,
-        out_shape=shape((rows, 512), bf16),
-        in_specs=[vmem] * 4,
-        out_specs=vmem,
-        compiler_params=params,
-        name="project_second",
-    )(other_class, hadamard, weight, first)
+        name="project",
+    )(gathered, hadamard, weight, codes, scales)
 
 
 def solution(mesh):

time: 51.3 us -> 51.1 us (level)
  blocking collectives: 25.3 us -> 37.5 us
  starting transfers between devices: 10.5 us -> 3.81 us
  waiting for transfers between devices: 5.11 us -> 0.01 us
  Pallas kernels: 9.89 us -> 9.33 us
    all_gather x0 -> x2, blocking collectives: none -> 13.4 us  [the longest x1 8.25 us: per_device(): lax.all_gather(gathered, 'tensor', axis=0, tiled=True, axis_index_groups=...]
    ppermute x2 -> x0, starting transfers between devices: 6.68 us -> none  [the longest x1 3.68 us: per_device(): lax.ppermute(gathered, 'tensor', edges + [edge[::-1] for edge in edges])]
    ppermute x2 -> x0, waiting for transfers between devices: 5.11 us -> none  [the longest x1 4.71 us: per_device(): lax.ppermute(gathered, 'tensor', edges + [edge[::-1] for edge in edges])]
    all_gather x1, blocking collectives: 25.3 us -> 24.2 us  [per_device(): lax.all_gather(attended, 'tensor', axis=0, tiled=True, axis_index_groups=...]
    pallas_call x3 -> x2, Pallas kernels: 5.68 us -> 5.11 us  [the longest x1 2.56 us: per_device(): pl.pallas_call(weight_kernel, out_shape=shape((8192, 512), bf16), in_spec...]
  transfers between devices with their start and end apart: 3 -> 1, of which waited for: 2 -> 0; matrix products, arithmetic and copies ran while one was open for 0% -> 0% of each run, Pallas kernels for 14% -> 6%
where the time goes in v5:
time: 51.1 us; the launch traced here: 50.7 us
  blocking collectives  37.5 us (73%)
  Pallas kernels  9.33 us (18%)
  starting transfers between devices  3.81 us (7%)
    all_gather x1, blocking collectives, per_device(): lax.all_gather(attended, 'tensor', axis=0, tiled=True, axis_index_groups=...  24.2 us
    all_gather x1, blocking collectives, per_device(): lax.all_gather(gathered, 'tensor', axis=0, tiled=True, axis_index_groups=...  8.25 us
    all_gather x1, blocking collectives, per_device(): lax.all_gather(sending, 'tensor', axis=0, axis_index_groups=[[2 * a, 2 *...  5.12 us
    ppermute x1, starting transfers between devices, per_device(): other_queries = lax.ppermute(queries, 'tensor', pairs)  3.81 us
    pallas_call x1, Pallas kernels, per_device(): pl.pallas_call(own_kernel, out_shape=(shape((512, 512), bf16), shape((512...  3.01 us
    pallas_call x1, Pallas kernels, per_device(): pl.pallas_call(weight_kernel, out_shape=shape((8192, 512), bf16), in_spec...  2.56 us
    pallas_call x1, Pallas kernels, per_device(): pl.pallas_call(project_kernel, out_shape=shape((rows, 512), bf16), in_spe...  2.55 us
    pallas_call x1, Pallas kernels, per_device(): pl.pallas_call(partner_kernel, out_shape=shape((rows, 1280), bf16), in_sp...  1.03 us
  transfers between devices with their start and end apart: 1, of which 0 were waited for; matrix products, arithmetic and copies ran while one was open for 0% of the time, Pallas kernels for 6%

profile of v5, /device:TPU:24, one launch (start us, length us, event | category | flops | bytes accessed | tf_op | source)
XLA Modules:
  0.0 50.7 jit_solution(2318986268197711712)
XLA Ops:
  0.0 3.8 %collective-permute-start = (bf16[32,4,128]{2,1,0:T(4,128)(2,1)}, bf16[32,4,128]{2,1,0:T(4,128)(2,1)S(1)}, u32[]{:S(2)}, u32[]{:S(2)}) collective-permute-start(bf16[32,4,128]{2,1,0:T(4,128)(2,1)} %param.12), channel_id=1, source_target_pairs={{0,1},{1,0},{2,3},{3,2},{4,5},{5,4},{6,7},{7,6},{8,9},{9,8},{10,11... | collective-permute-start | bytes 98312 | tf_op jit(solution)/shard_map/ppermute | solution.py:492
  3.8 3.0 %own_heads.1 = (bf16[512,512]{1,0:T(8,128)(2,1)S(1)}, bf16[512,512]{1,0:T(8,128)(2,1)S(1)}, f32[32,256]{1,0:T(8,128)S(1)}, bf16[2,32,128]{2,1,0:T(8,128)(2,1)S(1...) custom-call(s32[32]{0:T(128)} %lengths_hbm.1, ...), custom_call_target="tpu_custom_call" | custom-call | flops 400000000 | bytes 14000000 | tf_op jit(solution)/shard_map/own_heads/pallas_call | solution.py:493
  6.8 0.0 collective-permute-done
  6.8 1.0 %other_heads.1 = bf16[32,1280]{1,0:T(8,128)(2,1)S(1)} custom-call(bf16[128,128]{1,0:T(8,128)(2,1)S(1)} %bitcast.8, f32[32,256]{1,0:T(8,128)S(1)} %get-tuple-element.18.table_ref, bf16[2,32,128]{2,1,0:T(8,128)(2,1)S(1)} %get-tuple-element.19.now_ref, s32[8,128]{1,0:T(8,128)S(1)} %get-tuple-element.20.length_ref, ...), custom_call_target="tpu_custom_call" | custom-call | tf_op jit(solution)/shard_map/other_heads/pallas_call | solution.py:543
  7.9 5.1 %all-gather = bf16[64,1280]{1,0:T(8,128)(2,1)S(1)} all-gather(bf16[32,1280]{1,0:T(8,128)(2,1)S(1)} %other_heads.1), channel_id=2, replica_groups={{0,1},{2,3},{4,5},{6,7},{8,9},{10,11},{12,13},{14,15},{16,17},{18,19},{..., dimensions={0}, use_global_device_ids=true | all-gather | bytes 245760 | tf_op jit(solution)/shard_map/all_gather | solution.py:552
  13.0 2.6 %unpack_weight.1.weight_ref = bf16[8192,512]{1,0:T(8,128)(2,1)S(1)} custom-call(s32[2048,512]{1,0:T(8,128)S(1)} %get-tuple-element.25.codes_ref, s32[64,512]{1,0:T(8,128)S(1)} %get-tuple-element.27.scales_ref), custom_call_target="tpu_custom_call" | custom-call | flops 20000000 | bytes 12000000 | tf_op jit(solution)/shard_map/unpack_weight/pallas_call | solution.py:556
  15.6 0.2 combine_halves.1
  15.8 24.2 %all_gather.14 = bf16[128,1024]{1,0:T(8,128)(2,1)S(1)} all-gather(bf16[32,1024]{1,0:T(8,128)(2,1)S(1)} %combine_halves.1), channel_id=1, replica_groups={{0,4,8,12},{1,5,9,13},{2,6,10,14},{3,7,11,15},{16,20,24,28},{17,21,25,2..., dimensions={0}, use_global_device_ids=true | all-gather | bytes 327680 | tf_op jit(solution)/shard_map/all_gather | solution.py:577
  39.9 8.2 %all_gather.15.gathered_ref = bf16[256,1024]{1,0:T(8,128)(2,1)S(1)} all-gather(bf16[128,1024]{1,0:T(8,128)(2,1)S(1)} %all_gather.14), channel_id=1, replica_groups={{1,2},{4,3},{5,6},{8,7},{9,10},{12,11},{13,14},{0,15},{17,18},{20,19},{..., dimensions={0}, use_global_device_ids=true | all-gather | bytes 786432 | tf_op jit(solution)/shard_map/all_gather | solution.py:580
  48.2 2.5 %project.1 = bf16[32,512]{1,0:T(8,128)(2,1)} custom-call(bf16[256,1024]{1,0:T(8,128)(2,1)S(1)} %all_gather.15.gathered_ref, bf16[256,256]{1,0:T(8,128)(2,1)S(1)} %get-tuple-element.29.hadamard_ref, bf16[8192,512]{1,0:T(8,128)(2,1)S(1)} %unpack_weight.1.weight_ref, s32[2048,512]{1,0:T(8,128)S(1)} %get-tuple-element.25.codes_ref, ...), custom_call_target="tpu_custom_call" | custom-call | tf_op jit(solution)/shard_map/project/pallas_call | solution.py:581
Async XLA Ops:
  0.0 6.8 %collective-permute-start = (bf16[32,4,128]{2,1,0:T(4,128)(2,1)}, bf16[32,4,128]{2,1,0:T(4,128)(2,1)S(1)}, u32[]{:S(2)}, u32[]{:S(2)}) collective-permute-start(bf16[32,4,128]{2,1,0:T(4,128)(2,1)} %param.12), channel_id=1, source_target_pairs={{0,1},{1,0},{2,3},{3,2},{4,5},{5,4},{6,7},{7,6},{8,9},{9,8},{10,11... | collective-permute-start | bytes 98312 | tf_op jit(solution)/shard_map/ppermute | solution.py:492

commit v6 on v4

--- a/solution.py
+++ b/solution.py
@@ -424,7 +424,6 @@
 
 def project_half(gathered_ref, hadamard_ref, weight_ref, pair_class):
     hadamard = hadamard_ref[...]
-    factor = np.float32(8192.0**-0.5)
     turned = [
         jnp.dot(
             gathered_ref[:, q * 256 : (q + 1) * 256], hadamard, preferred_element_type=jnp.float32
@@ -441,7 +440,7 @@
     total = None
     for i in range(16):
         term = jnp.dot(
-            (blocks[i] * factor).astype(jnp.bfloat16),
+            blocks[i].astype(jnp.bfloat16),
             weight_ref[pair_class, i * 256 : (i + 1) * 256, :],
             preferred_element_type=jnp.float32,
         )
@@ -449,17 +448,12 @@
     return total
 
 
-def pair_class_here():
-    return lax.rem(lax.div(lax.axis_index("tensor"), 2), 2)
-
-
-def first_half_kernel(gathered_ref, hadamard_ref, weight_ref, out_ref):
-    out_ref[...] = project_half(gathered_ref, hadamard_ref, weight_ref, pair_class_here())
-
-
-def second_half_kernel(gathered_ref, hadamard_ref, weight_ref, first_ref, out_ref):
-    second = project_half(gathered_ref, hadamard_ref, weight_ref, 1 - pair_class_here())
-    out_ref[...] = (first_ref[...] + second).astype(jnp.bfloat16)
+def project_kernel(gathered_ref, hadamard_ref, weight_ref, out_ref):
+    parts = [
+        project_half(gathered_ref.at[c * 128 : (c + 1) * 128], hadamard_ref, weight_ref, c)
+        for c in range(2)
+    ]
+    out_ref[...] = ((parts[0] + parts[1]) * np.float32(8192.0**-0.5)).astype(jnp.bfloat16)
 
 
 vmem = pl.BlockSpec(memory_space=pltpu.VMEM)
@@ -570,25 +564,17 @@
     )(sending, received)
     strided = [[4 * k + i for k in range(4)] for i in range(4)]
     gathered = lax.all_gather(attended, "tensor", axis=0, tiled=True, axis_index_groups=strided)
-    edges = [(2 * a + 1, (2 * a + 2) % 16) for a in range(8)]
-    other_class = lax.ppermute(gathered, "tensor", edges + [edge[::-1] for edge in edges])
-    first = pl.pallas_call(
-        first_half_kernel,
-        out_shape=shape((rows, 512), f32),
+    edges = [[2 * a + 1, (2 * a + 2) % 16] for a in range(8)]
+    edges = [edge if a % 2 == 0 else edge[::-1] for a, edge in enumerate(edges)]
+    gathered = lax.all_gather(gathered, "tensor", axis=0, tiled=True, axis_index_groups=edges)
+    return pl.pallas_call(
+        project_kernel,
+        out_shape=shape((rows, 512), bf16),
         in_specs=[vmem] * 3,
         out_specs=vmem,
         compiler_params=params,
-        cost_estimate=pl.CostEstimate(flops=300_000_000, bytes_accessed=5_000_000, transcendentals=0),
-        name="project_first",
+        name="project",
     )(gathered, hadamard, weight)
-    return pl.pallas_call(
-        second_half_kernel,
-        out_shape=shape((rows, 512), bf16),
-        in_specs=[vmem] * 4,
-        out_specs=vmem,
-        compiler_params=params,
-        name="project_second",
-    )(other_class, hadamard, weight, first)
 
 
 def solution(mesh):

time: 51.3 us -> 51 us (level)
  blocking collectives: 25.3 us -> 33.6 us
  waiting for transfers between devices: 5.11 us -> 0.4 us
  starting transfers between devices: 10.5 us -> 6.81 us
    all_gather x0 -> x1, blocking collectives: none -> 8.25 us  [per_device(): lax.all_gather(gathered, 'tensor', axis=0, tiled=True, axis_index_groups=...]
    ppermute x1 -> x0, waiting for transfers between devices: 4.71 us -> none  [per_device(): lax.ppermute(gathered, 'tensor', edges + [edge[::-1] for edge in edges])]
    ppermute x1 -> x0, starting transfers between devices: 3.68 us -> none  [per_device(): lax.ppermute(gathered, 'tensor', edges + [edge[::-1] for edge in edges])]
    pallas_call x2 -> x1, Pallas kernels: 2.75 us -> 2.63 us  [per_device(): pl.pallas_call(project_kernel, out_shape=shape((rows, 512), bf16), in_spe...]
  transfers between devices with their start and end apart: 3 -> 2, of which waited for: 2 -> 1; matrix products, arithmetic and copies ran while one was open for 0% -> 0% of each run, Pallas kernels for 14% -> 12%
where the time goes in v6:
time: 51 us; the launch traced here: 50.6 us
  blocking collectives  33.6 us (66%)
  Pallas kernels  9.77 us (19%)
  starting transfers between devices  6.81 us (13%)
    all_gather x1, blocking collectives, per_device(): lax.all_gather(attended, 'tensor', axis=0, tiled=True, axis_index_groups=...  25.3 us
    all_gather x1, blocking collectives, per_device(): lax.all_gather(gathered, 'tensor', axis=0, tiled=True, axis_index_groups=...  8.25 us
    ppermute x1, starting transfers between devices, per_device(): other_queries = lax.ppermute(queries, 'tensor', pairs)  3.81 us
    pallas_call x1, Pallas kernels, per_device(): pl.pallas_call(own_kernel, out_shape=(shape((512, 512), bf16), shape((512...  3.01 us
    ppermute x1, starting transfers between devices, per_device(): received = lax.ppermute(sending, 'tensor', pairs)  3 us
    pallas_call x1, Pallas kernels, per_device(): pl.pallas_call(weight_kernel, out_shape=shape((2, 4096, 512), bf16), in_s...  2.93 us
    pallas_call x1, Pallas kernels, per_device(): pl.pallas_call(project_kernel, out_shape=shape((rows, 512), bf16), in_spe...  2.63 us
  transfers between devices with their start and end apart: 2, of which 1 were waited for; matrix products, arithmetic and copies ran while one was open for 0% of the time, Pallas kernels for 12%

profile of v6, /device:TPU:24, one launch (start us, length us, event | category | flops | bytes accessed | tf_op | source)
XLA Modules:
  0.0 50.6 jit_solution(12189132014830710019)
XLA Ops:
  0.0 3.8 %collective-permute-start = (bf16[32,4,128]{2,1,0:T(4,128)(2,1)}, bf16[32,4,128]{2,1,0:T(4,128)(2,1)S(1)}, u32[]{:S(2)}, u32[]{:S(2)}) collective-permute-start(bf16[32,4,128]{2,1,0:T(4,128)(2,1)} %param.12), channel_id=1, source_target_pairs={{0,1},{1,0},{2,3},{3,2},{4,5},{5,4},{6,7},{7,6},{8,9},{9,8},{10,11... | collective-permute-start | bytes 98312 | tf_op jit(solution)/shard_map/ppermute | solution.py:483
  3.8 3.0 %own_heads.1 = (bf16[512,512]{1,0:T(8,128)(2,1)S(1)}, bf16[512,512]{1,0:T(8,128)(2,1)S(1)}, f32[32,256]{1,0:T(8,128)S(1)}, bf16[2,32,128]{2,1,0:T(8,128)(2,1)S(1...) custom-call(s32[32]{0:T(128)} %lengths_hbm.1, ...), custom_call_target="tpu_custom_call" | custom-call | flops 400000000 | bytes 14000000 | tf_op jit(solution)/shard_map/own_heads/pallas_call | solution.py:484
  6.8 0.0 collective-permute-done
  6.8 1.0 %other_heads.1.mine_ref = bf16[32,1280]{1,0:T(8,128)(2,1)S(1)} custom-call(bf16[128,128]{1,0:T(8,128)(2,1)S(1)} %bitcast.6, f32[32,256]{1,0:T(8,128)S(1)} %get-tuple-element.18.table_ref, bf16[2,32,128]{2,1,0:T(8,128)(2,1)S(1)} %get-tuple-element.19.now_ref, s32[8,128]{1,0:T(8,128)S(1)} %get-tuple-element.20.length_ref, ...), custom_call_target="tpu_custom_call" | custom-call | tf_op jit(solution)/shard_map/other_heads/pallas_call | solution.py:534
  7.9 3.0 %collective-permute-start.1 = (bf16[32,1280]{1,0:T(8,128)(2,1)S(1)}, bf16[32,1280]{1,0:T(8,128)(2,1)S(1)}, u32[]{:S(2)}, u32[]{:S(2)}) collective-permute-start(bf16[32,1280]{1,0:T(8,128)(2,1)S(1)} %other_heads.1.mine_ref), channel_id=1, source_target_pairs={{0,1},{1,0},{2,3},{3,2},{4,5},{5,4},{6,7},{7,6},{8,9},{9,8},{10,11... | collective-permute-start | bytes 245768 | tf_op jit(solution)/shard_map/ppermute | solution.py:543
  10.9 2.9 %unpack_weight.1.weight_ref = bf16[2,4096,512]{2,1,0:T(8,128)(2,1)S(1)} custom-call(s32[2048,512]{1,0:T(8,128)S(1)} %get-tuple-element.25.codes_ref, s32[64,512]{1,0:T(8,128)S(1)} %get-tuple-element.27.scales_ref), custom_call_target="tpu_custom_call" | custom-call | flops 20000000 | bytes 12000000 | tf_op jit(solution)/shard_map/unpack_weight/pallas_call | solution.py:545
  13.8 0.4 collective-permute-done.1.theirs_ref
  14.2 0.2 combine_halves.1
  14.4 25.3 %all_gather.6 = bf16[128,1024]{1,0:T(8,128)(2,1)S(1)} all-gather(bf16[32,1024]{1,0:T(8,128)(2,1)S(1)} %combine_halves.1), channel_id=1, replica_groups={{0,4,8,12},{1,5,9,13},{2,6,10,14},{3,7,11,15},{16,20,24,28},{17,21,25,2..., dimensions={0}, use_global_device_ids=true | all-gather | bytes 327680 | tf_op jit(solution)/shard_map/all_gather | solution.py:566
  39.7 8.2 %all_gather.7.gathered_ref = bf16[256,1024]{1,0:T(8,128)(2,1)S(1)} all-gather(bf16[128,1024]{1,0:T(8,128)(2,1)S(1)} %all_gather.6), channel_id=1, replica_groups={{1,2},{4,3},{5,6},{8,7},{9,10},{12,11},{13,14},{0,15},{17,18},{20,19},{..., dimensions={0}, use_global_device_ids=true | all-gather | bytes 786432 | tf_op jit(solution)/shard_map/all_gather | solution.py:569
  48.0 2.6 %project.1 = bf16[32,512]{1,0:T(8,128)(2,1)} custom-call(bf16[256,1024]{1,0:T(8,128)(2,1)S(1)} %all_gather.7.gathered_ref, bf16[256,256]{1,0:T(8,128)(2,1)S(1)} %get-tuple-element.29.hadamard_ref, bf16[2,4096,512]{2,1,0:T(8,128)(2,1)S(1)} %unpack_weight.1.weight_ref), custom_call_target="tpu_custom_call" | custom-call | tf_op jit(solution)/shard_map/project/pallas_call | solution.py:570
Async XLA Ops:
  0.0 6.8 %collective-permute-start = (bf16[32,4,128]{2,1,0:T(4,128)(2,1)}, bf16[32,4,128]{2,1,0:T(4,128)(2,1)S(1)}, u32[]{:S(2)}, u32[]{:S(2)}) collective-permute-start(bf16[32,4,128]{2,1,0:T(4,128)(2,1)} %param.12), channel_id=1, source_target_pairs={{0,1},{1,0},{2,3},{3,2},{4,5},{5,4},{6,7},{7,6},{8,9},{9,8},{10,11... | collective-permute-start | bytes 98312 | tf_op jit(solution)/shard_map/ppermute | solution.py:483
  7.9 6.3 %collective-permute-start.1 = (bf16[32,1280]{1,0:T(8,128)(2,1)S(1)}, bf16[32,1280]{1,0:T(8,128)(2,1)S(1)}, u32[]{:S(2)}, u32[]{:S(2)}) collective-permute-start(bf16[32,1280]{1,0:T(8,128)(2,1)S(1)} %other_heads.1.mine_ref), channel_id=1, source_target_pairs={{0,1},{1,0},{2,3},{3,2},{4,5},{5,4},{6,7},{7,6},{8,9},{9,8},{10,11... | collective-permute-start | bytes 245768 | tf_op jit(solution)/shard_map/ppermute | solution.py:543

commit v7 on v5

--- a/solution.py
+++ b/solution.py
@@ -393,14 +393,17 @@
     out_ref[:, 512:] = second
 
 
-def unpacks_early():
-    return lax.axis_index("tensor") < 4
-
-
-def unpack_weight(codes_ref, scales_ref, weight_ref, scale_scratch):
+def early_share():
+    z = lax.axis_index("tensor")
+    ring = lax.rem(z, 4)
+    middle = jnp.logical_or(ring == 1, ring == 2)
+    return jnp.where(z < 4, 8, jnp.where(middle, 2, 0))
+
+
+def unpack_weight(first, last, codes_ref, scales_ref, weight_ref, scale_scratch):
     scale_scratch[...] = scales_ref[...].astype(jnp.float32) * np.float32(1.0 / weight_step)
 
-    @pl.loop(0, 8)
+    @pl.loop(first, last)
     def _(pair):
         for b in range(8):
             group = pair * 8 + b
@@ -418,9 +421,7 @@
 
 
 def weight_kernel(codes_ref, scales_ref, weight_ref, scale_scratch):
-    @pl.when(unpacks_early())
-    def _():
-        unpack_weight(codes_ref, scales_ref, weight_ref, scale_scratch)
+    unpack_weight(0, early_share(), codes_ref, scales_ref, weight_ref, scale_scratch)
 
 
 def project(gathered_ref, hadamard_ref, weight_ref, out_ref):
@@ -451,18 +452,10 @@
 
 
 def project_kernel(
-    gathered_ref, hadamard_ref, weight_ref, codes_ref, scales_ref, out_ref, late_weight, scale_scratch
+    gathered_ref, hadamard_ref, _, codes_ref, scales_ref, out_ref, weight_ref, scale_scratch
 ):
-    early = unpacks_early()
-
-    @pl.when(early)
-    def _():
-        project(gathered_ref, hadamard_ref, weight_ref, out_ref)
-
-    @pl.when(jnp.logical_not(early))
-    def _():
-        unpack_weight(codes_ref, scales_ref, late_weight, scale_scratch)
-        project(gathered_ref, hadamard_ref, late_weight, out_ref)
+    unpack_weight(early_share(), 8, codes_ref, scales_ref, weight_ref, scale_scratch)
+    project(gathered_ref, hadamard_ref, weight_ref, out_ref)
 
 
 vmem = pl.BlockSpec(memory_space=pltpu.VMEM)
@@ -580,13 +573,14 @@
     gathered = lax.all_gather(gathered, "tensor", axis=0, tiled=True, axis_index_groups=edges)
     return pl.pallas_call(
         project_kernel,
-        out_shape=shape((rows, 512), bf16),
+        out_shape=(shape((rows, 512), bf16), shape((8192, 512), bf16)),
         in_specs=[vmem] * 5,
-        out_specs=vmem,
-        scratch_shapes=[pltpu.VMEM((8192, 512), bf16), pltpu.VMEM((64, 512), f32)],
+        out_specs=(vmem,) * 2,
+        input_output_aliases={2: 1},
+        scratch_shapes=[pltpu.VMEM((64, 512), f32)],
         compiler_params=params,
         name="project",
-    )(gathered, hadamard, weight, codes, scales)
+    )(gathered, hadamard, weight, codes, scales)[0]
 
 
 def solution(mesh):

time: 51.1 us -> 50.6 us (level)
  blocking collectives: 37.5 us -> 36.8 us
    all_gather x1, blocking collectives: 24.2 us -> 23.4 us  [per_device(): lax.all_gather(attended, 'tensor', axis=0, tiled=True, axis_index_groups=...]
where the time goes in v7:
time: 50.6 us; the launch traced here: 50 us
  blocking collectives  36.8 us (73%)
  Pallas kernels  9.35 us (18%)
  starting transfers between devices  3.81 us (8%)
    all_gather x1, blocking collectives, per_device(): lax.all_gather(attended, 'tensor', axis=0, tiled=True, axis_index_groups=...  23.4 us
    all_gather x1, blocking collectives, per_device(): lax.all_gather(gathered, 'tensor', axis=0, tiled=True, axis_index_groups=...  8.25 us
    all_gather x1, blocking collectives, per_device(): lax.all_gather(sending, 'tensor', axis=0, axis_index_groups=[[2 * a, 2 *...  5.12 us
    ppermute x1, starting transfers between devices, per_device(): other_queries = lax.ppermute(queries, 'tensor', pairs)  3.81 us
    pallas_call x1, Pallas kernels, per_device(): pl.pallas_call(own_kernel, out_shape=(shape((512, 512), bf16), shape((512...  3.01 us
    pallas_call x1, Pallas kernels, per_device(): pl.pallas_call(weight_kernel, out_shape=shape((8192, 512), bf16), in_spec...  2.58 us
    pallas_call x1, Pallas kernels, per_device(): pl.pallas_call(project_kernel, out_shape=(shape((rows, 512), bf16), shape...  2.56 us
    pallas_call x1, Pallas kernels, per_device(): pl.pallas_call(partner_kernel, out_shape=shape((rows, 1280), bf16), in_sp...  1.02 us
  transfers between devices with their start and end apart: 1, of which 0 were waited for; matrix products, arithmetic and copies ran while one was open for 0% of the time, Pallas kernels for 6%

profile of v7, /device:TPU:24, one launch (start us, length us, event | category | flops | bytes accessed | tf_op | source)
XLA Modules:
  0.0 50.0 jit_solution(12221475854410699403)
XLA Ops:
  0.0 3.8 %collective-permute-start = (bf16[32,4,128]{2,1,0:T(4,128)(2,1)}, bf16[32,4,128]{2,1,0:T(4,128)(2,1)S(1)}, u32[]{:S(2)}, u32[]{:S(2)}) collective-permute-start(bf16[32,4,128]{2,1,0:T(4,128)(2,1)} %param.12), channel_id=1, source_target_pairs={{0,1},{1,0},{2,3},{3,2},{4,5},{5,4},{6,7},{7,6},{8,9},{9,8},{10,11... | collective-permute-start | bytes 98312 | tf_op jit(solution)/shard_map/ppermute | solution.py:485
  3.8 3.0 %own_heads.1 = (bf16[512,512]{1,0:T(8,128)(2,1)S(1)}, bf16[512,512]{1,0:T(8,128)(2,1)S(1)}, f32[32,256]{1,0:T(8,128)S(1)}, bf16[2,32,128]{2,1,0:T(8,128)(2,1)S(1...) custom-call(s32[32]{0:T(128)} %lengths_hbm.1, ...), custom_call_target="tpu_custom_call" | custom-call | flops 400000000 | bytes 14000000 | tf_op jit(solution)/shard_map/own_heads/pallas_call | solution.py:486
  6.8 0.0 collective-permute-done
  6.8 1.0 %other_heads.1 = bf16[32,1280]{1,0:T(8,128)(2,1)S(1)} custom-call(bf16[128,128]{1,0:T(8,128)(2,1)S(1)} %bitcast.8, f32[32,256]{1,0:T(8,128)S(1)} %get-tuple-element.19.table_ref, bf16[2,32,128]{2,1,0:T(8,128)(2,1)S(1)} %get-tuple-element.20.now_ref, s32[8,128]{1,0:T(8,128)S(1)} %get-tuple-element.21.length_ref, ...), custom_call_target="tpu_custom_call" | custom-call | tf_op jit(solution)/shard_map/other_heads/pallas_call | solution.py:536
  7.9 5.1 %all-gather = bf16[64,1280]{1,0:T(8,128)(2,1)S(1)} all-gather(bf16[32,1280]{1,0:T(8,128)(2,1)S(1)} %other_heads.1), channel_id=2, replica_groups={{0,1},{2,3},{4,5},{6,7},{8,9},{10,11},{12,13},{14,15},{16,17},{18,19},{..., dimensions={0}, use_global_device_ids=true | all-gather | bytes 245760 | tf_op jit(solution)/shard_map/all_gather | solution.py:545
  13.0 2.6 %unpack_weight.1._ = bf16[8192,512]{1,0:T(8,128)(2,1)S(1)} custom-call(s32[2048,512]{1,0:T(8,128)S(1)} %get-tuple-element.26.codes_ref, s32[64,512]{1,0:T(8,128)S(1)} %get-tuple-element.28.scales_ref), custom_call_target="tpu_custom_call" | custom-call | flops 20000000 | bytes 12000000 | tf_op jit(solution)/shard_map/unpack_weight/pallas_call | solution.py:549
  15.6 0.2 combine_halves.1
  15.8 23.4 %all_gather.14 = bf16[128,1024]{1,0:T(8,128)(2,1)S(1)} all-gather(bf16[32,1024]{1,0:T(8,128)(2,1)S(1)} %combine_halves.1), channel_id=1, replica_groups={{0,4,8,12},{1,5,9,13},{2,6,10,14},{3,7,11,15},{16,20,24,28},{17,21,25,2..., dimensions={0}, use_global_device_ids=true | all-gather | bytes 327680 | tf_op jit(solution)/shard_map/all_gather | solution.py:570
  39.2 8.2 %all_gather.15.gathered_ref = bf16[256,1024]{1,0:T(8,128)(2,1)S(1)} all-gather(bf16[128,1024]{1,0:T(8,128)(2,1)S(1)} %all_gather.14), channel_id=1, replica_groups={{1,2},{4,3},{5,6},{8,7},{9,10},{12,11},{13,14},{0,15},{17,18},{20,19},{..., dimensions={0}, use_global_device_ids=true | all-gather | bytes 786432 | tf_op jit(solution)/shard_map/all_gather | solution.py:573
  47.5 2.6 %project.1 = (bf16[32,512]{1,0:T(8,128)(2,1)}, bf16[8192,512]{1,0:T(8,128)(2,1)S(1)}) custom-call(bf16[256,1024]{1,0:T(8,128)(2,1)S(1)} %all_gather.15.gathered_ref, bf16[256,256]{1,0:T(8,128)(2,1)S(1)} %get-tuple-element.30.hadamard_ref, bf16[8192,512]{1,0:T(8,128)(2,1)S(1)} %unpack_weight.1._, ...), custom_call_target="tpu_custom_call", output_to_operand_aliasing={{1}: (2, {})} | custom-call | tf_op jit(solution)/shard_map/project/pallas_call | solution.py:574
Async XLA Ops:
  0.0 6.8 %collective-permute-start = (bf16[32,4,128]{2,1,0:T(4,128)(2,1)}, bf16[32,4,128]{2,1,0:T(4,128)(2,1)S(1)}, u32[]{:S(2)}, u32[]{:S(2)}) collective-permute-start(bf16[32,4,128]{2,1,0:T(4,128)(2,1)} %param.12), channel_id=1, source_target_pairs={{0,1},{1,0},{2,3},{3,2},{4,5},{5,4},{6,7},{7,6},{8,9},{9,8},{10,11... | collective-permute-start | bytes 98312 | tf_op jit(solution)/shard_map/ppermute | solution.py:485

commit v8 on v7

--- a/solution.py
+++ b/solution.py
@@ -452,10 +452,23 @@
 
 
 def project_kernel(
-    gathered_ref, hadamard_ref, _, codes_ref, scales_ref, out_ref, weight_ref, scale_scratch
+    gathered_ref, hadamard_ref, weight_ref, codes_ref, scales_ref, out_ref, late_weight, scale_scratch
 ):
-    unpack_weight(early_share(), 8, codes_ref, scales_ref, weight_ref, scale_scratch)
-    project(gathered_ref, hadamard_ref, weight_ref, out_ref)
+    share = early_share()
+
+    @pl.when(share == 8)
+    def _():
+        project(gathered_ref, hadamard_ref, weight_ref, out_ref)
+
+    @pl.when(share < 8)
+    def _():
+        @pl.loop(0, share)
+        def _(pair):
+            part = pl.ds(pair * 1024, 1024)
+            late_weight[part, :] = weight_ref[part, :]
+
+        unpack_weight(share, 8, codes_ref, scales_ref, late_weight, scale_scratch)
+        project(gathered_ref, hadamard_ref, late_weight, out_ref)
 
 
 vmem = pl.BlockSpec(memory_space=pltpu.VMEM)
@@ -573,14 +586,13 @@
     gathered = lax.all_gather(gathered, "tensor", axis=0, tiled=True, axis_index_groups=edges)
     return pl.pallas_call(
         project_kernel,
-        out_shape=(shape((rows, 512), bf16), shape((8192, 512), bf16)),
+        out_shape=shape((rows, 512), bf16),
         in_specs=[vmem] * 5,
-        out_specs=(vmem,) * 2,
-        input_output_aliases={2: 1},
-        scratch_shapes=[pltpu.VMEM((64, 512), f32)],
+        out_specs=vmem,
+        scratch_shapes=[pltpu.VMEM((8192, 512), bf16), pltpu.VMEM((64, 512), f32)],
         compiler_params=params,
         name="project",
-    )(gathered, hadamard, weight, codes, scales)[0]
+    )(gathered, hadamard, weight, codes, scales)
 
 
 def solution(mesh):

time: 50.6 us -> 50.6 us (level)
  no operation moved by 1% of the time
where the time goes in v8:
time: 50.6 us; the launch traced here: 50 us
  blocking collectives  36.8 us (73%)
  Pallas kernels  9.34 us (18%)
  starting transfers between devices  3.81 us (8%)
    all_gather x1, blocking collectives, per_device(): lax.all_gather(attended, 'tensor', axis=0, tiled=True, axis_index_groups=...  23.4 us
    all_gather x1, blocking collectives, per_device(): lax.all_gather(gathered, 'tensor', axis=0, tiled=True, axis_index_groups=...  8.25 us
    all_gather x1, blocking collectives, per_device(): lax.all_gather(sending, 'tensor', axis=0, axis_index_groups=[[2 * a, 2 *...  5.12 us
    ppermute x1, starting transfers between devices, per_device(): other_queries = lax.ppermute(queries, 'tensor', pairs)  3.81 us
    pallas_call x1, Pallas kernels, per_device(): pl.pallas_call(own_kernel, out_shape=(shape((512, 512), bf16), shape((512...  3.01 us
    pallas_call x1, Pallas kernels, per_device(): pl.pallas_call(weight_kernel, out_shape=shape((8192, 512), bf16), in_spec...  2.58 us
    pallas_call x1, Pallas kernels, per_device(): pl.pallas_call(project_kernel, out_shape=shape((rows, 512), bf16), in_spe...  2.55 us
    pallas_call x1, Pallas kernels, per_device(): pl.pallas_call(partner_kernel, out_shape=shape((rows, 1280), bf16), in_sp...  1.02 us
  transfers between devices with their start and end apart: 1, of which 0 were waited for; matrix products, arithmetic and copies ran while one was open for 0% of the time, Pallas kernels for 6%

profile of v8, /device:TPU:24, one launch (start us, length us, event | category | flops | bytes accessed | tf_op | source)
XLA Modules:
  0.0 50.0 jit_solution(8233078450770830661)
XLA Ops:
  0.0 3.8 %collective-permute-start = (bf16[32,4,128]{2,1,0:T(4,128)(2,1)}, bf16[32,4,128]{2,1,0:T(4,128)(2,1)S(1)}, u32[]{:S(2)}, u32[]{:S(2)}) collective-permute-start(bf16[32,4,128]{2,1,0:T(4,128)(2,1)} %param.12), channel_id=1, source_target_pairs={{0,1},{1,0},{2,3},{3,2},{4,5},{5,4},{6,7},{7,6},{8,9},{9,8},{10,11... | collective-permute-start | bytes 98312 | tf_op jit(solution)/shard_map/ppermute | solution.py:498
  3.8 3.0 %own_heads.1 = (bf16[512,512]{1,0:T(8,128)(2,1)S(1)}, bf16[512,512]{1,0:T(8,128)(2,1)S(1)}, f32[32,256]{1,0:T(8,128)S(1)}, bf16[2,32,128]{2,1,0:T(8,128)(2,1)S(1...) custom-call(s32[32]{0:T(128)} %lengths_hbm.1, ...), custom_call_target="tpu_custom_call" | custom-call | flops 400000000 | bytes 14000000 | tf_op jit(solution)/shard_map/own_heads/pallas_call | solution.py:499
  6.8 0.0 collective-permute-done
  6.8 1.0 %other_heads.1 = bf16[32,1280]{1,0:T(8,128)(2,1)S(1)} custom-call(bf16[128,128]{1,0:T(8,128)(2,1)S(1)} %bitcast.8, f32[32,256]{1,0:T(8,128)S(1)} %get-tuple-element.18.table_ref, bf16[2,32,128]{2,1,0:T(8,128)(2,1)S(1)} %get-tuple-element.19.now_ref, s32[8,128]{1,0:T(8,128)S(1)} %get-tuple-element.20.length_ref, ...), custom_call_target="tpu_custom_call" | custom-call | tf_op jit(solution)/shard_map/other_heads/pallas_call | solution.py:549
  7.9 5.1 %all-gather = bf16[64,1280]{1,0:T(8,128)(2,1)S(1)} all-gather(bf16[32,1280]{1,0:T(8,128)(2,1)S(1)} %other_heads.1), channel_id=2, replica_groups={{0,1},{2,3},{4,5},{6,7},{8,9},{10,11},{12,13},{14,15},{16,17},{18,19},{..., dimensions={0}, use_global_device_ids=true | all-gather | bytes 245760 | tf_op jit(solution)/shard_map/all_gather | solution.py:558
  13.0 2.6 %unpack_weight.1.weight_ref = bf16[8192,512]{1,0:T(8,128)(2,1)S(1)} custom-call(s32[2048,512]{1,0:T(8,128)S(1)} %get-tuple-element.25.codes_ref, s32[64,512]{1,0:T(8,128)S(1)} %get-tuple-element.27.scales_ref), custom_call_target="tpu_custom_call" | custom-call | flops 20000000 | bytes 12000000 | tf_op jit(solution)/shard_map/unpack_weight/pallas_call | solution.py:562
  15.6 0.2 combine_halves.1
  15.8 23.4 %all_gather.14 = bf16[128,1024]{1,0:T(8,128)(2,1)S(1)} all-gather(bf16[32,1024]{1,0:T(8,128)(2,1)S(1)} %combine_halves.1), channel_id=1, replica_groups={{0,4,8,12},{1,5,9,13},{2,6,10,14},{3,7,11,15},{16,20,24,28},{17,21,25,2..., dimensions={0}, use_global_device_ids=true | all-gather | bytes 327680 | tf_op jit(solution)/shard_map/all_gather | solution.py:583
  39.2 8.2 %all_gather.15.gathered_ref = bf16[256,1024]{1,0:T(8,128)(2,1)S(1)} all-gather(bf16[128,1024]{1,0:T(8,128)(2,1)S(1)} %all_gather.14), channel_id=1, replica_groups={{1,2},{4,3},{5,6},{8,7},{9,10},{12,11},{13,14},{0,15},{17,18},{20,19},{..., dimensions={0}, use_global_device_ids=true | all-gather | bytes 786432 | tf_op jit(solution)/shard_map/all_gather | solution.py:586
  47.5 2.5 %project.1 = bf16[32,512]{1,0:T(8,128)(2,1)} custom-call(bf16[256,1024]{1,0:T(8,128)(2,1)S(1)} %all_gather.15.gathered_ref, bf16[256,256]{1,0:T(8,128)(2,1)S(1)} %get-tuple-element.29.hadamard_ref, bf16[8192,512]{1,0:T(8,128)(2,1)S(1)} %unpack_weight.1.weight_ref, s32[2048,512]{1,0:T(8,128)S(1)} %get-tuple-element.25.codes_ref, ...), custom_call_target="tpu_custom_call" | custom-call | tf_op jit(solution)/shard_map/project/pallas_call | solution.py:587
Async XLA Ops:
  0.0 6.8 %collective-permute-start = (bf16[32,4,128]{2,1,0:T(4,128)(2,1)}, bf16[32,4,128]{2,1,0:T(4,128)(2,1)S(1)}, u32[]{:S(2)}, u32[]{:S(2)}) collective-permute-start(bf16[32,4,128]{2,1,0:T(4,128)(2,1)} %param.12), channel_id=1, source_target_pairs={{0,1},{1,0},{2,3},{3,2},{4,5},{5,4},{6,7},{7,6},{8,9},{9,8},{10,11... | collective-permute-start | bytes 98312 | tf_op jit(solution)/shard_map/ppermute | solution.py:498

commit v9 on v8

--- a/solution.py
+++ b/solution.py
@@ -190,13 +190,9 @@
         new_weight.astype(jnp.float32), axis=1, keepdims=True
     )
     mixed = jnp.concatenate(mixed, axis=0)
-    high = mixed.astype(jnp.bfloat16)
-    rest = (mixed - high.astype(jnp.float32)).astype(jnp.bfloat16)
-    weighted = (
-        lax.dot_general(high, select, nt, preferred_element_type=jnp.float32)
-        + lax.dot_general(rest, select, nt, preferred_element_type=jnp.float32)
-        + jnp.dot(new_weight, value_now, preferred_element_type=jnp.float32)
-    )
+    weighted = lax.dot_general(
+        mixed.astype(jnp.bfloat16), select, nt, preferred_element_type=jnp.float32
+    ) + jnp.dot(new_weight, value_now, preferred_element_type=jnp.float32)
     some = total > 0.0
     floor_total = jnp.where(some, total, 1.0)
     logsum = jnp.where(some, top + jnp.log(floor_total), neg_floor)

time: 50.6 us -> 50.4 us (level)
  no operation moved by 1% of the time
where the time goes in v9:
time: 50.4 us; the launch traced here: 49.6 us
  blocking collectives  36.7 us (73%)
  Pallas kernels  9.12 us (18%)
  starting transfers between devices  3.81 us (8%)
    all_gather x1, blocking collectives, per_device(): lax.all_gather(attended, 'tensor', axis=0, tiled=True, axis_index_groups=...  23.3 us
    all_gather x1, blocking collectives, per_device(): lax.all_gather(gathered, 'tensor', axis=0, tiled=True, axis_index_groups=...  8.25 us
    all_gather x1, blocking collectives, per_device(): lax.all_gather(sending, 'tensor', axis=0, axis_index_groups=[[2 * a, 2 *...  5.11 us
    ppermute x1, starting transfers between devices, per_device(): other_queries = lax.ppermute(queries, 'tensor', pairs)  3.81 us
    pallas_call x1, Pallas kernels, per_device(): pl.pallas_call(own_kernel, out_shape=(shape((512, 512), bf16), shape((512...  2.89 us
    pallas_call x1, Pallas kernels, per_device(): pl.pallas_call(weight_kernel, out_shape=shape((8192, 512), bf16), in_spec...  2.58 us
    pallas_call x1, Pallas kernels, per_device(): pl.pallas_call(project_kernel, out_shape=shape((rows, 512), bf16), in_spe...  2.55 us
  transfers between devices with their start and end apart: 1, of which 0 were waited for; matrix products, arithmetic and copies ran while one was open for 0% of the time, Pallas kernels for 6%

profile of v9, /device:TPU:24, one launch (start us, length us, event | category | flops | bytes accessed | tf_op | source)
XLA Modules:
  0.0 49.6 jit_solution(7717745706809182796)
XLA Ops:
  0.0 3.8 %collective-permute-start = (bf16[32,4,128]{2,1,0:T(4,128)(2,1)}, bf16[32,4,128]{2,1,0:T(4,128)(2,1)S(1)}, u32[]{:S(2)}, u32[]{:S(2)}) collective-permute-start(bf16[32,4,128]{2,1,0:T(4,128)(2,1)} %param.12), channel_id=1, source_target_pairs={{0,1},{1,0},{2,3},{3,2},{4,5},{5,4},{6,7},{7,6},{8,9},{9,8},{10,11... | collective-permute-start | bytes 98312 | tf_op jit(solution)/shard_map/ppermute | solution.py:494
  3.8 2.9 %own_heads.1 = (bf16[512,512]{1,0:T(8,128)(2,1)S(1)}, bf16[512,512]{1,0:T(8,128)(2,1)S(1)}, f32[32,256]{1,0:T(8,128)S(1)}, bf16[2,32,128]{2,1,0:T(8,128)(2,1)S(1...) custom-call(s32[32]{0:T(128)} %lengths_hbm.1, ...), custom_call_target="tpu_custom_call" | custom-call | flops 400000000 | bytes 14000000 | tf_op jit(solution)/shard_map/own_heads/pallas_call | solution.py:495
  6.7 0.0 collective-permute-done
  6.7 0.9 %other_heads.1 = bf16[32,1280]{1,0:T(8,128)(2,1)S(1)} custom-call(bf16[128,128]{1,0:T(8,128)(2,1)S(1)} %bitcast.8, f32[32,256]{1,0:T(8,128)S(1)} %get-tuple-element.18.table_ref, bf16[2,32,128]{2,1,0:T(8,128)(2,1)S(1)} %get-tuple-element.19.now_ref, s32[8,128]{1,0:T(8,128)S(1)} %get-tuple-element.20.length_ref, ...), custom_call_target="tpu_custom_call" | custom-call | tf_op jit(solution)/shard_map/other_heads/pallas_call | solution.py:545
  7.7 5.1 %all-gather = bf16[64,1280]{1,0:T(8,128)(2,1)S(1)} all-gather(bf16[32,1280]{1,0:T(8,128)(2,1)S(1)} %other_heads.1), channel_id=2, replica_groups={{0,1},{2,3},{4,5},{6,7},{8,9},{10,11},{12,13},{14,15},{16,17},{18,19},{..., dimensions={0}, use_global_device_ids=true | all-gather | bytes 245760 | tf_op jit(solution)/shard_map/all_gather | solution.py:554
  12.8 2.6 %unpack_weight.1.weight_ref = bf16[8192,512]{1,0:T(8,128)(2,1)S(1)} custom-call(s32[2048,512]{1,0:T(8,128)S(1)} %get-tuple-element.25.codes_ref, s32[64,512]{1,0:T(8,128)S(1)} %get-tuple-element.27.scales_ref), custom_call_target="tpu_custom_call" | custom-call | flops 20000000 | bytes 12000000 | tf_op jit(solution)/shard_map/unpack_weight/pallas_call | solution.py:558
  15.3 0.2 combine_halves.1
  15.5 23.3 %all_gather.14 = bf16[128,1024]{1,0:T(8,128)(2,1)S(1)} all-gather(bf16[32,1024]{1,0:T(8,128)(2,1)S(1)} %combine_halves.1), channel_id=1, replica_groups={{0,4,8,12},{1,5,9,13},{2,6,10,14},{3,7,11,15},{16,20,24,28},{17,21,25,2..., dimensions={0}, use_global_device_ids=true | all-gather | bytes 327680 | tf_op jit(solution)/shard_map/all_gather | solution.py:579
  38.9 8.2 %all_gather.15.gathered_ref = bf16[256,1024]{1,0:T(8,128)(2,1)S(1)} all-gather(bf16[128,1024]{1,0:T(8,128)(2,1)S(1)} %all_gather.14), channel_id=1, replica_groups={{1,2},{4,3},{5,6},{8,7},{9,10},{12,11},{13,14},{0,15},{17,18},{20,19},{..., dimensions={0}, use_global_device_ids=true | all-gather | bytes 786432 | tf_op jit(solution)/shard_map/all_gather | solution.py:582
  47.1 2.5 %project.1 = bf16[32,512]{1,0:T(8,128)(2,1)} custom-call(bf16[256,1024]{1,0:T(8,128)(2,1)S(1)} %all_gather.15.gathered_ref, bf16[256,256]{1,0:T(8,128)(2,1)S(1)} %get-tuple-element.29.hadamard_ref, bf16[8192,512]{1,0:T(8,128)(2,1)S(1)} %unpack_weight.1.weight_ref, s32[2048,512]{1,0:T(8,128)S(1)} %get-tuple-element.25.codes_ref, ...), custom_call_target="tpu_custom_call" | custom-call | tf_op jit(solution)/shard_map/project/pallas_call | solution.py:583
Async XLA Ops:
  0.0 6.7 %collective-permute-start = (bf16[32,4,128]{2,1,0:T(4,128)(2,1)}, bf16[32,4,128]{2,1,0:T(4,128)(2,1)S(1)}, u32[]{:S(2)}, u32[]{:S(2)}) collective-permute-start(bf16[32,4,128]{2,1,0:T(4,128)(2,1)} %param.12), channel_id=1, source_target_pairs={{0,1},{1,0},{2,3},{3,2},{4,5},{5,4},{6,7},{7,6},{8,9},{9,8},{10,11... | collective-permute-start | bytes 98312 | tf_op jit(solution)/shard_map/ppermute | solution.py:494
